TPU v7x, 32 devices: a whole 2x2x4 slice. The times are simulated.
32 devices in a mesh: clip: 2 (over x), seq: 16 (over z, y, core).
Axes of the slice: x: 2, y: 2, z: 4, core: 2. Of those that a mesh axis runs over, the one named last changes fastest.
Arguments:
- spatial_saved: bfloat16 [3, 32, 256, 576], P(None, ('clip', 'seq')), parts along dimension 1, may hold values from -48 to 48
- hidden: bfloat16 [32, 256, 1152], P(('clip', 'seq')), parts along dimension 0, may hold values from -6 to 6
- temporal_out_grad: bfloat16 [32, 256, 576], P(('clip', 'seq')), parts along dimension 0, may hold values from -6 to 6
- stream_grad: bfloat16 [32, 256, 1152], P(('clip', 'seq')), parts along dimension 0, may hold values from -6 to 6
- modulation: float32 [1152], replicated, may hold values from -0.5 to 1
- temporal_weights: bfloat16 [1152, 1728], P('seq'), may hold values from -0.1875 to 0.1875
- spatial_weights: bfloat16 [576, 1152], P('seq'), may hold values from -0.25 to 0.25
Outputs:
- hidden_grad: bfloat16 [32, 256, 1152], P(('clip', 'seq')), parts along dimension 0
- spatial_grad: bfloat16 [3, 32, 256, 576], P(None, ('clip', 'seq')), parts along dimension 1
There are 2 independent parts, one for each index of `clip`. A program takes and returns all parts, laid end to end along the dimension named above; an argument that names none is the same for every part. Nothing has to cross between parts.
All inputs are finite; a program needn't handle non-finite values.
Results may differ from a plain program's by a relative error of at most 0.024.
Values may be sent and summed in bfloat16 or wider, within the bound.
No kernel may reach another device: no remote copies, remote signals or barrier semaphores. Data moves between devices by JAX's collectives and lax.ppermute only.
A program may use at most 64 MiB of HBM per device.

v0:
```python
import math

import jax
import jax.numpy as jnp
from jax import lax
from jax.sharding import PartitionSpec as P

HEADS = 8
HD = 72


epsilon = 1e-06


def attend_grad(query, keys, values, grad_o, form):
    key_form = form.replace("l", "m")
    scale = 1.0 / math.sqrt(query.shape[-1])
    scores = (
        jnp.einsum(
            form + "," + key_form + "->bhlm", query, keys, preferred_element_type=jnp.float32
        )
        * scale
    )
    attention = jax.nn.softmax(scores, axis=-1)
    rounded = attention.astype(jnp.bfloat16)
    output = jnp.einsum(
        "bhlm," + key_form + "->" + form, rounded, values, preferred_element_type=jnp.float32
    )
    delta = jnp.einsum(form + "," + form + "->bhl", grad_o.astype(jnp.float32), output)
    spread = jnp.einsum(
        form + "," + key_form + "->bhlm", grad_o, values, preferred_element_type=jnp.float32
    )
    dscore = (attention * (spread - delta[..., None])).astype(jnp.bfloat16)
    grad_query = jnp.einsum(
        "bhlm," + key_form + "->" + form, dscore, keys, preferred_element_type=jnp.float32
    )
    grad_keys = jnp.einsum(
        "bhlm," + form + "->" + key_form, dscore, query, preferred_element_type=jnp.float32
    )
    grad_values = jnp.einsum(
        "bhlm," + form + "->" + key_form, rounded, grad_o, preferred_element_type=jnp.float32
    )
    return (
        (grad_query * scale).astype(jnp.bfloat16),
        (grad_keys * scale).astype(jnp.bfloat16),
        grad_values.astype(jnp.bfloat16),
    )


def split_heads(block):
    return block.reshape(block.shape[:-1] + (HEADS, HD))


def merge_heads(block):
    return block.reshape(block.shape[:-2] + (HEADS * HD,))


def layer_norm(hidden, modulation):
    widened = hidden.astype(jnp.float32)
    mean_value = jnp.mean(widened, axis=-1, keepdims=True)
    centered = widened - mean_value
    inverse = lax.rsqrt(jnp.mean(centered * centered, axis=-1, keepdims=True) + epsilon)
    normal_form = centered * inverse
    normed = (normal_form * (1.0 + modulation)).astype(jnp.bfloat16)
    return (normed, normal_form, inverse)


def norm_back(grad_normed, normal_form, inverse, modulation):
    scaled = grad_normed * (1.0 + modulation)
    return inverse * (
        scaled
        - jnp.mean(scaled, axis=-1, keepdims=True)
        - normal_form * jnp.mean(scaled * normal_form, axis=-1, keepdims=True)
    )


def temporal_backward(projected, grad_patch):
    width = HEADS * HD
    grads = attend_grad(
        split_heads(projected[..., :width]),
        split_heads(projected[..., width : 2 * width]),
        split_heads(projected[..., 2 * width :]),
        split_heads(grad_patch),
        "lbhd",
    )
    return jnp.concatenate([merge_heads(gradient) for gradient in grads], axis=-1)


def shards(
    spatial_saved,
    hidden,
    temporal_out_grad,
    stream_grad,
    modulation,
    temporal_weights,
    spatial_weights,
):
    grad_patch = lax.all_to_all(temporal_out_grad, "seq", split_axis=1, concat_axis=0, tiled=True)
    hidden_patch = lax.all_to_all(hidden, "seq", split_axis=1, concat_axis=0, tiled=True)
    normed, normal_form, inverse = layer_norm(hidden_patch, modulation)
    projected = jnp.einsum(
        "fpd,dc->fpc",
        normed,
        lax.all_gather(temporal_weights, "seq", axis=0, tiled=True),
        preferred_element_type=jnp.float32,
    ).astype(jnp.bfloat16)
    projection_grads = temporal_backward(projected, grad_patch)
    branch = norm_back(
        jnp.einsum(
            "fpc,dc->fpd",
            projection_grads,
            lax.all_gather(temporal_weights, "seq", axis=0, tiled=True),
            preferred_element_type=jnp.float32,
        ),
        normal_form,
        inverse,
        modulation,
    ).astype(jnp.bfloat16)
    branch = lax.all_to_all(branch, "seq", split_axis=0, concat_axis=1, tiled=True)
    branch = lax.optimization_barrier(branch)
    hidden_grad = (stream_grad.astype(jnp.float32) + branch.astype(jnp.float32)).astype(
        jnp.bfloat16
    )
    attention_grad = jnp.einsum(
        "fpd,cd->fpc",
        hidden_grad,
        lax.all_gather(spatial_weights, "seq", axis=0, tiled=True),
        preferred_element_type=jnp.float32,
    ).astype(jnp.bfloat16)
    spatial = attend_grad(
        split_heads(spatial_saved[0]),
        split_heads(spatial_saved[1]),
        split_heads(spatial_saved[2]),
        split_heads(attention_grad),
        "blhd",
    )
    spatial_grad = jnp.stack([merge_heads(gradient) for gradient in spatial])
    return (hidden_grad, spatial_grad)


def solution(mesh):
    return jax.shard_map(
        shards,
        mesh=mesh,
        in_specs=(
            P(None, ("clip", "seq"), None, None),
            P(("clip", "seq"), None, None),
            P(("clip", "seq"), None, None),
            P(("clip", "seq"), None, None),
            P(),
            P("seq", None),
            P("seq", None),
        ),
        out_specs=(P(("clip", "seq"), None, None), P(None, ("clip", "seq"), None, None)),
        check_vma=False,
    )
```

profile of v0, /device:TPU:0, one launch (start us, length us, event | category | flops | bytes accessed | tf_op | source)
XLA Modules:
  0.0 136.8 jit_solution(4414544214536378165)
XLA Ops:
  7.9 1.4 %copy.61 = bf16[1,256,576]{2,0,1:T(2,128)(2,1)S(1)} copy(bf16[1,256,576]{1,2,0:T(8,128)(2,1)} %param.9) | data formatting | bytes 589824 | tf_op args[2]
  9.9 2.7 %reduce.13 = bf16[256,576]{1,0:T(8,128)(2,1)S(1)} reduce(bf16[256,1,576]{2,1,0:T(2,128)(2,1)S(1)} %bitcast.105, bf16[]{:T(256)} %broadcast.94), dimensions={1}, to_apply=%bitcast.75.reduce_sub_computation | reduce | bytes 589826
  12.6 1.1 reshape.177
  13.7 7.4 %all-to-all-start.1 = ((bf16[16,2,4608]{2,1,0:T(2,128)(2,1)}), bf16[16,2,4608]{2,1,0:T(2,128)(2,1)S(1)}, u32[]{:S(2)}, u32[]{:S(2)}) async-start(bf16[16,2,4608]{2,1,0:T(2,128)(2,1)} %reshape.177), calls=%async_computation.1 | async-start | bytes 589824 | tf_op jit(solution)/shard_map/all_to_all | solution.py:98
  22.0 4.2 %reduce.12 = bf16[256,1152]{1,0:T(8,128)(2,1)S(1)} reduce(bf16[256,1,1152]{2,1,0:T(2,128)(2,1)S(1)} %bitcast.101, bf16[]{:T(256)} %broadcast.94), dimensions={1}, to_apply=%bitcast.97.reduce_sub_computation | reduce | bytes 1179650
  27.2 9.1 %all-to-all-done.1 = bf16[16,2,4608]{2,1,0:T(2,128)(2,1)S(1)} async-done(((bf16[16,2,4608]{2,1,0:T(2,128)(2,1)}), bf16[16,2,4608]{2,1,0:T(2,128)(2,1)S(1)}, u32[]{:S(2)}, u32[]{:S(2)}) %all-to-all-start.1) | async-done | bytes 294944 | tf_op jit(solution)/shard_map/all_to_all | solution.py:98
  36.3 4.8 %all-to-all-start = ((bf16[16,2,9216]{2,1,0:T(2,128)(2,1)}), bf16[16,2,9216]{2,1,0:T(2,128)(2,1)S(1)}, u32[]{:S(2)}, u32[]{:S(2)}) async-start(bf16[16,2,9216]{2,1,0:T(2,128)(2,1)} %reshape.175), calls=%async_computation | async-start | bytes 1179648 | tf_op jit(solution)/shard_map/all_to_all | solution.py:99
  42.4 1.8 %bitcast_reduce_fusion = bf16[256,576]{1,0:T(8,128)(2,1)S(1)} fusion(bf16[256,1,576]{2,1,0:T(2,128)(2,1)S(1)} %reshape.178), kind=kLoop, calls=%fused_computation.78 | loop fusion | bytes 589824 | tf_op jit(solution)/shard_map/all_to_all | solution.py:98
  44.8 19.4 %all-to-all-done = bf16[16,2,9216]{2,1,0:T(2,128)(2,1)S(1)} async-done(((bf16[16,2,9216]{2,1,0:T(2,128)(2,1)}), bf16[16,2,9216]{2,1,0:T(2,128)(2,1)S(1)}, u32[]{:S(2)}, u32[]{:S(2)}) %all-to-all-start) | async-done | bytes 589856 | tf_op jit(solution)/shard_map/all_to_all | solution.py:99
  65.4 10.7 %all-gather.4.cloned.1.call-done = bf16[1152,1728]{1,0:T(8,128)(2,1)} async-done(((bf16[72,1728]{1,0:T(8,128)(2,1)}), bf16[1152,1728]{1,0:T(8,128)(2,1)}) %all-gather.4.cloned.1.call-update) | async-done | bytes 3981328 | tf_op jit(solution)/shard_map/all_gather | solution.py:104
  76.1 3.6 %fusion.9 = bf16[16,16,1728]{2,1,0:T(8,128)(2,1)S(1)} fusion(bf16[1152,1728]{1,0:T(8,128)(2,1)} %all-gather.4.cloned.1.call-done, f32[16,16,1152]{2,1,0:T(8,128)S(1)} %bitcast.102, f32[1152]{0:T(1024)S(1)} %broadcast_add_fusion, f32[16,16]{1,0:T(8,128)S(1)} %div.33, f32[16,16]{1,0:T(8,128)S(1)} %rsqrt.12), kind=kOutput, calls=%fused_computation.7 | convolution fusion | flops 1020837888 | bytes 6052352 | tf_op jit(solution)/shard_map/fpd,dc->fpc/dot_general | solution.py:101
  81.0 1.4 reshape.153
  82.4 2.0 %fusion.60 = (f32[16,8,16]{2,1,0:T(8,128)S(1)}, f32[16,8,16,16]{2,3,1,0:T(8,128)}) fusion(bf16[16,16,8,72]{3,2,1,0:T(8,128)(2,1)S(1)} %reshape.151, bf16[16,16,8,72]{3,2,1,0:T(8,128)(2,1)S(1)} %reshape.152), kind=kOutput, calls=%fused_computation.75 | convolution fusion | flops 4816911 | bytes 729088 | tf_op jit(solution)/shard_map/sub | solution.py:24
  84.4 2.7 %fusion.22 = bf16[16,16,8,72]{3,0,2,1:T(8,128)(2,1)} fusion(bf16[16,16,8,72]{3,2,1,0:T(8,128)(2,1)S(1)} %reshape.154, f32[16,8,16,16]{2,3,1,0:T(8,128)} %get-tuple-element.11, f32[16,8,16]{2,1,0:T(8,128)S(1)} %get-tuple-element.10), kind=kOutput, calls=%fused_computation.30 | convolution fusion | flops 4931584 | bytes 729088 | tf_op jit(solution)/shard_map/bhlm,lbhd->mbhd/dot_general | solution.py:40
  88.2 2.0 %fusion.17 = bf16[16,8,16,16]{2,3,1,0:T(8,128)(2,1)S(1)} fusion(f32[16,8,16]{2,1,0:T(8,128)S(1)} %copy.85, bf16[16,16,8,72]{3,2,1,0:T(8,128)(2,1)S(1)} %reshape.154, bf16[16,16,8,72]{3,2,1,0:T(8,128)(2,1)S(1)} %copy-done.6, f32[16,8,16,16]{2,3,1,0:T(8,128)} %get-tuple-element.11, f32[16,8,16]{2,1,0:T(8,128)} %copy-done.11), kind=kOutput, calls=%fused_computation.21 | convolution fusion | flops 4849664 | bytes 802816 | tf_op jit(solution)/shard_map/lbhd,mbhd->bhlm/dot_general | solution.py:30
  93.2 1.2 concatenate.3
  94.4 3.9 %fusion.57 = (f32[16,16]{1,0:T(8,128)S(1)}, f32[16,16]{1,0:T(8,128)S(1)}, f32[16,16,1152]{2,1,0:T(8,128)S(1)}) fusion(f32[16,16]{1,0:T(8,128)S(1)} %rsqrt.12, f32[16,16,1152]{2,1,0:T(8,128)S(1)} %bitcast.103, f32[16,16]{1,0:T(8,128)S(1)} %div.33, f32[1152]{0:T(1024)S(1)} %broadcast_add_fusion, bf16[16,16,1728]{2,1,0:T(8,128)(2,1)} %concatenate.3, ...), kind=kOutput, calls=%fused_computation.72 | convolution fusion | flops 1020984832 | bytes 7234048 | tf_op jit(solution)/shard_map/fpc,dc->fpd/dot_general | solution.py:109
  98.4 1.2 multiply_convert_fusion.1
  99.6 3.8 %all-to-all-start.2 = ((bf16[16,16,1152]{2,1,0:T(8,128)(2,1)}), bf16[16,16,1152]{2,1,0:T(8,128)(2,1)S(1)}, u32[]{:S(2)}, u32[]{:S(2)}) async-start(bf16[16,16,1152]{2,1,0:T(8,128)(2,1)} %multiply_convert_fusion.1), calls=%async_computation.2 | async-start | bytes 1179648 | tf_op jit(solution)/shard_map/all_to_all | solution.py:119
  104.2 2.2 %fusion.65 = (f32[8,256]{1,0:T(8,128)S(1)}, f32[8,256,256]{1,2,0:T(8,128)}) fusion(bf16[256,8,72]{0,2,1:T(8,128)(2,1)S(1)} %bitcast.107, bf16[256,8,72]{0,2,1:T(8,128)(2,1)S(1)} %bitcast.109), kind=kOutput, calls=%fused_computation.76 | convolution fusion | flops 77070592 | bytes 2695168 | tf_op jit(solution)/shard_map/sub | solution.py:24
  106.4 1.8 %fusion.27 = bf16[8,256,256]{1,2,0:T(8,128)(2,1)S(1)} fusion(f32[8,256,256]{1,2,0:T(8,128)} %get-tuple-element.14, f32[8,256]{1,0:T(8,128)S(1)} %get-tuple-element.13), kind=kLoop, calls=%fused_computation.46 | loop fusion | flops 1048576 | bytes 3153920 | tf_op jit(solution)/shard_map/convert_element_type | solution.py:25
  108.2 13.7 %all-gather.6.cloned.1.call-done = bf16[16,36,1152]{2,1,0:T(8,128)(2,1)} async-done(((bf16[1,36,1152]{2,1,0:T(8,128)(2,1)}), bf16[16,36,1152]{2,1,0:T(8,128)(2,1)}) %all-gather.6.cloned.1.call-update) | async-done | bytes 1327120 | tf_op jit(solution)/shard_map/all_gather | solution.py:127
  121.9 2.2 %reshape.166 = bf16[576,1152]{1,0:T(8,128)(2,1)S(1)} reshape(bf16[16,36,1152]{2,1,0:T(8,128)(2,1)} %all-gather.6.cloned.1.call-done) | data formatting | bytes 2654208
  124.2 1.2 add_convert_fusion
  (66 shorter events, 16.8 us)
Async XLA Ops:
  7.2 69.0 %all-gather.4.cloned.1.call-start = ((), (), s32[]{:S(2)}) async-start(), calls=%async_computation.3 | async-start | bytes 4386816 | tf_op jit(solution)/shard_map/all_gather | solution.py:104
  9.3 11.7 %copy-start.3 = (bf16[1,256,1152]{2,1,0:T(8,128)(2,1)S(1)}, bf16[1,256,1152]{2,1,0:T(8,128)(2,1)}, u32[]{:S(2)}) copy-start(bf16[1,256,1152]{2,1,0:T(8,128)(2,1)} %param.8) | copy-start | bytes 1769476
  13.7 22.6 %all-to-all-start.1 = ((bf16[16,2,4608]{2,1,0:T(2,128)(2,1)}), bf16[16,2,4608]{2,1,0:T(2,128)(2,1)S(1)}, u32[]{:S(2)}, u32[]{:S(2)}) async-start(bf16[16,2,4608]{2,1,0:T(2,128)(2,1)} %reshape.177), calls=%async_computation.1 | async-start | bytes 589824 | tf_op jit(solution)/shard_map/all_to_all | solution.py:98
  26.2 15.6 %copy-start.9 = (f32[1152]{0:T(1024)S(1)}, f32[1152]{0:T(1024)}, u32[]{:S(2)}) copy-start(f32[1152]{0:T(1024)} %param.11) | copy-start | bytes 13828
  36.3 28.0 %all-to-all-start = ((bf16[16,2,9216]{2,1,0:T(2,128)(2,1)}), bf16[16,2,9216]{2,1,0:T(2,128)(2,1)S(1)}, u32[]{:S(2)}, u32[]{:S(2)}) async-start(bf16[16,2,9216]{2,1,0:T(2,128)(2,1)} %reshape.175), calls=%async_computation | async-start | bytes 1179648 | tf_op jit(solution)/shard_map/all_to_all | solution.py:99
  41.1 80.8 %all-gather.6.cloned.1.call-start = ((), (), s32[]{:S(2)}) async-start(), calls=%async_computation.4 | async-start | bytes 1566720 | tf_op jit(solution)/shard_map/all_gather | solution.py:127
  84.4 2.7 %copy-start.11 = (f32[16,8,16]{2,1,0:T(8,128)}, f32[16,8,16]{2,1,0:T(8,128)S(1)}, u32[]{:S(2)}) copy-start(f32[16,8,16]{2,1,0:T(8,128)S(1)} %get-tuple-element.10) | copy-start | bytes 24580
  84.4 2.7 %copy-start.6 = (bf16[16,16,8,72]{3,2,1,0:T(8,128)(2,1)S(1)}, bf16[16,16,8,72]{3,2,1,0:T(8,128)(2,1)}, u32[]{:S(2)}) copy-start(bf16[16,16,8,72]{3,2,1,0:T(8,128)(2,1)} %reshape.153) | copy-start | bytes 884740
  84.4 2.7 %copy-start.10 = (f32[16,8,16,16]{2,3,1,0:T(8,128)S(1)}, f32[16,8,16,16]{2,3,1,0:T(8,128)}, u32[]{:S(2)}) copy-start(f32[16,8,16,16]{2,3,1,0:T(8,128)} %get-tuple-element.11) | copy-start | bytes 393220
  90.6 1.0 copy-start.5
  99.6 3.8 %copy-start.2 = (bf16[3,1,256,576]{2,3,1,0:T(8,128)(2,1)S(1)}, bf16[3,1,256,576]{2,3,1,0:T(8,128)(2,1)}, u32[]{:S(2)}) copy-start(bf16[3,1,256,576]{2,3,1,0:T(8,128)(2,1)} %param.7) | copy-start | bytes 2654212
  99.6 24.6 %all-to-all-start.2 = ((bf16[16,16,1152]{2,1,0:T(8,128)(2,1)}), bf16[16,16,1152]{2,1,0:T(8,128)(2,1)S(1)}, u32[]{:S(2)}, u32[]{:S(2)}) async-start(bf16[16,16,1152]{2,1,0:T(8,128)(2,1)} %multiply_convert_fusion.1), calls=%async_computation.2 | async-start | bytes 1179648 | tf_op jit(solution)/shard_map/all_to_all | solution.py:119
  106.4 1.8 %copy-start.7 = (f32[8,256]{1,0:T(8,128)}, f32[8,256]{1,0:T(8,128)S(1)}, u32[]{:S(2)}) copy-start(f32[8,256]{1,0:T(8,128)S(1)} %get-tuple-element.13) | copy-start | bytes 24580
  124.2 1.9 %copy-start.1 = (bf16[1,1,256,576]{2,3,1,0:T(8,128)(2,1)S(1)}, bf16[1,1,256,576]{2,3,1,0:T(8,128)(2,1)}, u32[]{:S(2)}) copy-start(bf16[1,1,256,576]{2,3,1,0:T(8,128)(2,1)} %get-tuple-element.7) | copy-start | bytes 884740
  125.4 1.0 copy-start.4
  125.4 1.8 %copy-start = (f32[8,256,256]{1,2,0:T(8,128)S(1)}, f32[8,256,256]{1,2,0:T(8,128)}, u32[]{:S(2)}) copy-start(f32[8,256,256]{1,2,0:T(8,128)} %get-tuple-element.14) | copy-start | bytes 6291460
  126.0 1.2 copy-start.8
Sparse Core Ops, SparseCore 0:
  10.3 65.7 all-gather.3
  78.3 43.5 all-gather.5
where the time goes:
time: 138 us; the launch traced here: 137 us
  waiting for transfers between devices  54.1 us (39%)
  matrix products  20.4 us (15%)
  local copies, waits for them, and re-layouts  18.4 us (13%)
  starting transfers between devices  16.2 us (12%)
  between operations  14.4 us (10%)
  other arithmetic  13.2 us (10%)
    all_to_all x1, waiting for transfers between devices, shards(): lax.all_to_all(hidden, 'seq', split_axis=1, concat_axis=0, tiled=True)  19.4 us
    all_gather x1, waiting for transfers between devices, shards(): lax.all_gather(spatial_weights, 'seq', axis=0, tiled=True)  13.7 us
    all_gather x1, waiting for transfers between devices, shards(): lax.all_gather(temporal_weights, 'seq', axis=0, tiled=True)  10.7 us
    unnamed x32, local copies, waits for them, and re-layouts  9.62 us
    all_to_all x1, waiting for transfers between devices, shards(): lax.all_to_all(temporal_out_grad, 'seq', split_axis=1, concat_axis=0, til...  9.12 us
    unnamed x3, other arithmetic  7.44 us
    all_to_all x1, starting transfers between devices, shards(): lax.all_to_all(temporal_out_grad, 'seq', split_axis=1, concat_axis=0, til...  7.39 us
    all_to_all x1, starting transfers between devices, shards(): lax.all_to_all(hidden, 'seq', split_axis=1, concat_axis=0, tiled=True)  4.79 us
  transfers between devices with their start and end apart: 5, of which 4 were waited for; matrix products, arithmetic and copies ran while one was open for 33% of the time, Pallas kernels for 0%

commit v1 on v0

v1 whole, which is shorter than its diff:
```python
import functools
import math

import jax
import jax.numpy as jnp
from jax import lax
from jax.experimental import pallas as pl
from jax.experimental.pallas import tpu as pltpu
from jax.sharding import PartitionSpec as P

HEADS = 8
HD = 72
LANES = 128

epsilon = 1e-06
VMEM_LIMIT = 48 * 1024 * 1024


def window(head, width):
    low, high = head * HD, (head + 1) * HD
    start = low // LANES * LANES
    stop = min(-(-high // LANES) * LANES, width)
    return start, stop, low, high


def keep(block, start, low, high):
    lane = lax.broadcasted_iota(jnp.int32, block.shape, 1) + start
    return jnp.where((lane >= low) & (lane < high), block, jnp.zeros_like(block))


def dot_nt(a, b):
    return lax.dot_general(a, b, (((1,), (1,)), ((), ())), preferred_element_type=jnp.float32)


def dot_tn(a, b):
    return lax.dot_general(a, b, (((0,), (0,)), ((), ())), preferred_element_type=jnp.float32)


def dot_nn(a, b):
    return jnp.dot(a, b, preferred_element_type=jnp.float32)


def soft(scores_t, scale):
    top = jnp.max(scores_t, axis=0, keepdims=True)
    raised = jnp.exp2((scores_t - top) * (scale * math.log2(math.e)))
    return raised * (1.0 / jnp.sum(raised, axis=0, keepdims=True))


class Tiles:
    def __init__(self):
        self.sums = {}

    def add(self, start, part):
        for offset in range(0, part.shape[1], LANES):
            piece = part[:, offset : offset + LANES]
            key = start + offset
            self.sums[key] = self.sums[key] + piece if key in self.sums else piece

    def store(self, ref, base, width, scale, upto):
        for key in sorted(self.sums):
            stop = min(key + LANES, width)
            if stop <= upto:
                done = self.sums.pop(key)[:, : stop - key] * scale
                ref[:, base + key : base + stop] = done.astype(ref.dtype)


def head_grads(attention_t, query, keys, values, grad_o, start, low, high):
    rounded_t = attention_t.astype(jnp.bfloat16)
    spread_t = dot_nt(keep(values, start, low, high), grad_o)
    wide = rounded_t.astype(jnp.float32)
    delta = jnp.sum(wide * spread_t, axis=0, keepdims=True)
    dscore_t = (attention_t.astype(jnp.float32) * (spread_t - delta)).astype(jnp.bfloat16)
    return (
        dot_tn(dscore_t, keep(keys, start, low, high)),
        dot_nn(dscore_t, keep(query, start, low, high)),
        dot_nn(rounded_t, keep(grad_o, start, low, high)),
    )


def temporal_kernel(patches, x_ref, mod_ref, w_ref, out_ref, bias_ref, proj_ref, keys_ref, grad_ref, gk_ref):
    tokens, width = out_ref.shape[0], w_ref.shape[1] // 3
    depth = w_ref.shape[0]
    scale = 1.0 / math.sqrt(HD)
    row = lax.broadcasted_iota(jnp.int32, (tokens, tokens), 0)
    column = lax.broadcasted_iota(jnp.int32, (tokens, tokens), 1)
    bias_ref[...] = jnp.where(lax.rem(row, patches) == lax.rem(column, patches), 0.0, -1e30)
    gain = 1.0 + mod_ref[...]
    widened = x_ref[:, :depth].astype(jnp.float32)
    centered = widened - jnp.mean(widened, axis=-1, keepdims=True)
    inverse = lax.rsqrt(jnp.mean(centered * centered, axis=-1, keepdims=True) + epsilon)
    normed = (centered * inverse * gain).astype(jnp.bfloat16)
    proj_ref[...] = dot_nn(normed, w_ref[...]).astype(jnp.bfloat16)
    keys_ref[...] = proj_ref[:, width : 2 * width]
    sums = [Tiles(), Tiles(), Tiles()]
    for head in range(HEADS):
        start, stop, low, high = window(head, width)
        query = proj_ref[:, start:stop]
        keys = keys_ref[:, start:stop]
        values = proj_ref[:, 2 * width + start : 2 * width + stop]
        grad_o = x_ref[:, depth + start : depth + stop]
        scores_t = dot_nt(keep(keys, start, low, high), query) + bias_ref[...]
        parts = head_grads(soft(scores_t, scale), query, keys, values, grad_o, start, low, high)
        for tiles, part in zip(sums, parts):
            tiles.add(start, part)
        upto = width if head == HEADS - 1 else high // LANES * LANES
        sums[0].store(grad_ref, 0, width, scale, upto)
        sums[1].store(gk_ref, 0, width, scale, upto)
        sums[2].store(grad_ref, 2 * width, width, 1.0, upto)
    grad_ref[:, width : 2 * width] = gk_ref[...]
    scaled = dot_nt(grad_ref[...], w_ref[...]) * gain
    widened = x_ref[:, :depth].astype(jnp.float32)
    centered = widened - jnp.mean(widened, axis=-1, keepdims=True)
    normal_form = centered * inverse
    branch = inverse * (
        scaled
        - jnp.mean(scaled, axis=-1, keepdims=True)
        - normal_form * jnp.mean(scaled * normal_form, axis=-1, keepdims=True)
    )
    out_ref[...] = branch.astype(out_ref.dtype)


def temporal(mixed, modulation, weights, patches):
    tokens, depth, width = mixed.shape[0], weights.shape[0], weights.shape[1] // 3
    return pl.pallas_call(
        functools.partial(temporal_kernel, patches),
        out_shape=jax.ShapeDtypeStruct((tokens, depth), jnp.bfloat16),
        scratch_shapes=[
            pltpu.VMEM((tokens, tokens), jnp.float32),
            pltpu.VMEM((tokens, 3 * width), jnp.bfloat16),
            pltpu.VMEM((tokens, width), jnp.bfloat16),
            pltpu.VMEM((tokens, 3 * width), jnp.bfloat16),
            pltpu.VMEM((tokens, width), jnp.bfloat16),
        ],
        compiler_params=pltpu.CompilerParams(vmem_limit_bytes=VMEM_LIMIT),
        cost_estimate=pl.CostEstimate(
            flops=12 * tokens * depth * width + 12 * HEADS * tokens * tokens * 2 * LANES,
            bytes_accessed=2 * (2 * tokens * 3 * width + 3 * depth * width),
            transcendentals=HEADS * tokens * tokens,
        ),
        name="temporal_backward",
    )(mixed, modulation.reshape(1, depth), weights)


def score_kernel(saved_ref, out_ref):
    width = saved_ref.shape[2]
    for head in range(HEADS):
        start, stop, low, high = window(head, width)
        keys = keep(saved_ref[1, :, start:stop], start, low, high)
        scores_t = dot_nt(keys, saved_ref[0, :, start:stop])
        out_ref[head] = soft(scores_t, 1.0 / math.sqrt(HD)).astype(out_ref.dtype)


def score(saved):
    tokens, width = saved.shape[1:]
    return pl.pallas_call(
        score_kernel,
        out_shape=jax.ShapeDtypeStruct((HEADS, tokens, tokens), jnp.bfloat16),
        compiler_params=pltpu.CompilerParams(vmem_limit_bytes=VMEM_LIMIT),
        cost_estimate=pl.CostEstimate(
            flops=2 * HEADS * tokens * tokens * 2 * LANES,
            bytes_accessed=2 * (3 * tokens * width + HEADS * tokens * tokens),
            transcendentals=HEADS * tokens * tokens,
        ),
        name="spatial_scores",
    )(saved)


def spatial_kernel(attention_ref, saved_ref, stream_ref, branch_ref, w_ref, hidden_ref, out_ref, grad_ref):
    width = saved_ref.shape[2]
    scale = 1.0 / math.sqrt(HD)
    hidden_grad = (
        stream_ref[...].astype(jnp.float32) + branch_ref[...].astype(jnp.float32)
    ).astype(jnp.bfloat16)
    hidden_ref[...] = hidden_grad
    grad_ref[...] = dot_nt(hidden_grad, w_ref[...]).astype(jnp.bfloat16)
    sums = [Tiles(), Tiles(), Tiles()]
    for head in range(HEADS):
        start, stop, low, high = window(head, width)
        parts = head_grads(
            attention_ref[head],
            saved_ref[0, :, start:stop],
            saved_ref[1, :, start:stop],
            saved_ref[2, :, start:stop],
            grad_ref[:, start:stop],
            start,
            low,
            high,
        )
        upto = width if head == HEADS - 1 else high // LANES * LANES
        for index, (tiles, part) in enumerate(zip(sums, parts)):
            tiles.add(start, part)
            tiles.store(out_ref.at[index], 0, width, 1.0 if index == 2 else scale, upto)


def spatial(attention_t, saved, stream, branch, weights):
    tokens, depth = stream.shape
    width = weights.shape[0]
    return pl.pallas_call(
        spatial_kernel,
        out_shape=(
            jax.ShapeDtypeStruct((tokens, depth), jnp.bfloat16),
            jax.ShapeDtypeStruct((3, tokens, width), jnp.bfloat16),
        ),
        scratch_shapes=[pltpu.VMEM((tokens, width), jnp.bfloat16)],
        compiler_params=pltpu.CompilerParams(vmem_limit_bytes=VMEM_LIMIT),
        cost_estimate=pl.CostEstimate(
            flops=2 * tokens * depth * width + 10 * HEADS * tokens * tokens * 2 * LANES,
            bytes_accessed=2 * (3 * tokens * depth + depth * width + 6 * tokens * width),
            transcendentals=0,
        ),
        name="spatial_backward",
    )(attention_t, saved, stream, branch, weights)


def shards(
    spatial_saved,
    hidden,
    temporal_out_grad,
    stream_grad,
    modulation,
    temporal_weights,
    spatial_weights,
):
    frames = lax.axis_size("seq")
    tokens, depth = hidden.shape[1:]
    width = temporal_out_grad.shape[2]
    patches = tokens // frames
    saved = spatial_saved.reshape(3, tokens, width)
    mixed = jnp.concatenate([hidden, temporal_out_grad], axis=2).reshape(frames, patches, depth + width)
    mixed = lax.all_to_all(mixed, "seq", split_axis=0, concat_axis=0, tiled=True)
    weights = lax.all_gather(temporal_weights, "seq", axis=0, tiled=True)
    attention_t = score(saved)
    branch = temporal(mixed.reshape(tokens, depth + width), modulation, weights, patches)
    branch = lax.all_to_all(
        branch.reshape(frames, patches, depth), "seq", split_axis=0, concat_axis=0, tiled=True
    )
    hidden_grad, spatial_grad = spatial(
        attention_t,
        saved,
        stream_grad.reshape(tokens, depth),
        branch.reshape(tokens, depth),
        lax.all_gather(spatial_weights, "seq", axis=0, tiled=True),
    )
    return (hidden_grad.reshape(1, tokens, depth), spatial_grad.reshape(3, 1, tokens, width))


def solution(mesh):
    return jax.shard_map(
        shards,
        mesh=mesh,
        in_specs=(
            P(None, ("clip", "seq"), None, None),
            P(("clip", "seq"), None, None),
            P(("clip", "seq"), None, None),
            P(("clip", "seq"), None, None),
            P(),
            P("seq", None),
            P("seq", None),
        ),
        out_specs=(P(("clip", "seq"), None, None), P(None, ("clip", "seq"), None, None)),
        check_vma=False,
    )
```

time: 138 us -> 136 us (0.986)
  waiting for transfers between devices: 54.1 us -> 84.5 us
  matrix products: 20.4 us -> 0 us
  Pallas kernels: 0 us -> 12.3 us
  other arithmetic: 13.2 us -> 2.09 us
  local copies, waits for them, and re-layouts: 18.4 us -> 10.5 us
  starting transfers between devices: 16.2 us -> 11.7 us
    all_gather x1, waiting for transfers between devices: 10.7 us -> 27.2 us  [shards(): weights = lax.all_gather(temporal_weights, 'seq', axis=0, tiled=True)]
    dot_general x13 -> x0, matrix products: 16.2 us -> none  [the longest x1 3.94 us: shards(): jnp.einsum('fpc,dc->fpd', projection_grads, lax.all_gather(temporal_weigh...]
    all_gather x1, waiting for transfers between devices: 13.7 us -> 27.7 us  [shards(): lax.all_gather(spatial_weights, 'seq', axis=0, tiled=True)]
    pallas_call x0 -> x3, Pallas kernels: none -> 12.3 us  [the longest x1 7.51 us: temporal(): pl.pallas_call(functools.partial(temporal_kernel, patches), out_shape=jax...]
    unnamed x3 -> x0, other arithmetic: 7.44 us -> none
    all_to_all x3 -> x2, starting transfers between devices: 16 us -> 11.6 us  [the longest x1 7.39 us: shards(): lax.all_to_all(mixed, 'seq', split_axis=0, concat_axis=0, tiled=True)]
    convert_element_type x4 -> x0, other arithmetic: 4.28 us -> none  [the longest x1 1.78 us: attend_grad(): rounded = attention.astype(jnp.bfloat16)]
    sub x2 -> x0, matrix products: 4.18 us -> none  [attend_grad(): attention = jax.nn.softmax(scores, axis=-1)]
  transfers between devices with their start and end apart: 5 -> 4, of which waited for: 4 -> 3; matrix products, arithmetic and copies ran while one was open for 33% -> 5% of each run, Pallas kernels for 0% -> 6%
where the time goes in v1:
time: 136 us; the launch traced here: 135 us
  waiting for transfers between devices  84.5 us (62%)
  between operations  14.1 us (10%)
  Pallas kernels  12.3 us (9%)
  starting transfers between devices  11.7 us (9%)
  local copies, waits for them, and re-layouts  10.5 us (8%)
  other arithmetic  2.09 us (2%)
    all_to_all x1, waiting for transfers between devices, shards(): lax.all_to_all(mixed, 'seq', split_axis=0, concat_axis=0, tiled=True)  28.3 us
    all_gather x1, waiting for transfers between devices, shards(): lax.all_gather(spatial_weights, 'seq', axis=0, tiled=True)  27.7 us
    all_gather x1, waiting for transfers between devices, shards(): weights = lax.all_gather(temporal_weights, 'seq', axis=0, tiled=True)  27.2 us
    unnamed x14, local copies, waits for them, and re-layouts  10.5 us
    pallas_call x1, Pallas kernels, temporal(): pl.pallas_call(functools.partial(temporal_kernel, patches), out_shape=jax...  7.51 us
    all_to_all x1, starting transfers between devices, shards(): lax.all_to_all(mixed, 'seq', split_axis=0, concat_axis=0, tiled=True)  7.39 us
    all_to_all x1, starting transfers between devices, shards(): lax.all_to_all(branch.reshape(frames, patches, depth), 'seq', split_axis=...  4.25 us
    pallas_call x1, Pallas kernels, spatial(): pl.pallas_call(spatial_kernel, out_shape=(jax.ShapeDtypeStruct((tokens, d...  3.91 us
  transfers between devices with their start and end apart: 4, of which 3 were waited for; matrix products, arithmetic and copies ran while one was open for 5% of the time, Pallas kernels for 6%

profile of v1, /device:TPU:0, one launch (start us, length us, event | category | flops | bytes accessed | tf_op | source)
XLA Modules:
  0.0 135.2 jit_solution(17326324995603218618)
XLA Ops:
  7.2 0.0 all-gather.4.cloned.1.call-start
  7.2 0.7 all-gather.4.cloned.1.call-update
  7.9 1.2 copy.16
  9.1 0.0 copy-start.4
  9.1 2.1 %pad_maximum_fusion = bf16[1,256,1728]{2,1,0:T(8,128)(2,1)} fusion(bf16[1,256,576]{2,1,0:T(8,128)(2,1)S(1)} %copy.16, bf16[1,256,1152]{2,1,0:T(8,128)(2,1)} %param.8), kind=kLoop, calls=%fused_computation | loop fusion | flops 1769472 | bytes 1769472 | tf_op jit(solution)/shard_map/concatenate | solution.py:229
  11.2 7.4 %all-to-all-start = ((bf16[16,16,1728]{2,1,0:T(8,128)(2,1)}), bf16[16,16,1728]{2,1,0:T(8,128)(2,1)S(1)}, u32[]{:S(2)}, u32[]{:S(2)}) async-start(bf16[16,16,1728]{2,1,0:T(8,128)(2,1)} %bitcast.2), calls=%async_computation | async-start | bytes 1835008 | tf_op jit(solution)/shard_map/all_to_all | solution.py:230
  18.6 0.0 all-gather.6.cloned.1.call-start
  18.6 0.7 all-gather.6.cloned.1.call-update
  19.3 28.3 %all-to-all-done = bf16[16,16,1728]{2,1,0:T(8,128)(2,1)S(1)} async-done(((bf16[16,16,1728]{2,1,0:T(8,128)(2,1)}), bf16[16,16,1728]{2,1,0:T(8,128)(2,1)S(1)}, u32[]{:S(2)}, u32[]{:S(2)}) %all-to-all-start) | async-done | bytes 884768 | tf_op jit(solution)/shard_map/all_to_all | solution.py:230
  47.6 27.2 %all-gather.4.cloned.1.call-done.w_ref = bf16[1152,1728]{1,0:T(8,128)(2,1)} async-done(((bf16[72,1728]{1,0:T(8,128)(2,1)}), bf16[1152,1728]{1,0:T(8,128)(2,1)}) %all-gather.4.cloned.1.call-update) | async-done | bytes 3981328 | tf_op jit(solution)/shard_map/all_gather | solution.py:231
  74.8 2.2 %copy-done.1 = bf16[1152,1728]{1,0:T(8,128)(2,1)S(1)} copy-done((bf16[1152,1728]{1,0:T(8,128)(2,1)S(1)}, bf16[1152,1728]{1,0:T(8,128)(2,1)}, u32[]{:S(2)}) %copy-start.1) | copy-done | bytes 3981336
  77.0 7.5 %temporal_backward.1 = bf16[256,1152]{1,0:T(8,128)(2,1)} custom-call(bf16[256,1728]{1,0:T(8,128)(2,1)S(1)} %bitcast.12, f32[1,1152]{1,0:T(1,128)S(1)} %reshape.35.mod_ref, bf16[1152,1728]{1,0:T(8,128)(2,1)S(1)} %copy-done.1), custom_call_target="tpu_custom_call" | custom-call | flops 3649044480 | bytes 5750784 | tf_op jit(solution)/shard_map/temporal_backward/pallas_call | solution.py:124
  84.5 4.2 %all-to-all-start.1 = ((bf16[16,16,1152]{2,1,0:T(8,128)(2,1)}), bf16[16,16,1152]{2,1,0:T(8,128)(2,1)}, u32[]{:S(2)}, u32[]{:S(2)}) async-start(bf16[16,16,1152]{2,1,0:T(8,128)(2,1)} %bitcast.4), calls=%async_computation.1 | async-start | bytes 1179648 | tf_op jit(solution)/shard_map/all_to_all | solution.py:234
  88.7 0.0 copy-done.3
  88.7 0.7 copy.15
  89.4 0.9 spatial_scores.1.attention_ref
  90.3 27.7 %all-gather.6.cloned.1.call-done = bf16[16,36,1152]{2,1,0:T(8,128)(2,1)} async-done(((bf16[1,36,1152]{2,1,0:T(8,128)(2,1)}), bf16[16,36,1152]{2,1,0:T(8,128)(2,1)}) %all-gather.6.cloned.1.call-update) | async-done | bytes 1327120 | tf_op jit(solution)/shard_map/all_gather | solution.py:242
  118.0 2.2 %reshape.41.w_ref = bf16[576,1152]{1,0:T(8,128)(2,1)S(1)} reshape(bf16[16,36,1152]{2,1,0:T(8,128)(2,1)} %all-gather.6.cloned.1.call-done) | data formatting | bytes 2654208
  120.2 0.0 all-to-all-done.1
  120.3 0.0 copy-start.2
  120.3 1.1 copy-done.2
  121.3 3.9 %spatial_backward.1 = (bf16[256,1152]{1,0:T(8,128)(2,1)}, bf16[3,256,576]{2,1,0:T(8,128)(2,1)S(1)}) custom-call(bf16[8,256,256]{2,1,0:T(8,128)(2,1)S(1)} %spatial_scores.1.attention_ref, bf16[3,256,576]{2,1,0:T(8,128)(2,1)S(1)} %bitcast.10, bf16[256,1152]{1,0:T(8,128)(2,1)S(1)} %bitcast.13, bf16[256,1152]{1,0:T(8,128)(2,1)} %bitcast.5.branch_ref, ...), custom_call_target="tpu_custom_call" | custom-call | flops 1681915904 | bytes 4866048 | tf_op jit(solution)/shard_map/spatial_backward/pallas_call | solution.py:198
  125.2 0.9 copy-done
  126.2 2.2 %copy.17 = bf16[3,1,256,576]{2,3,1,0:T(8,128)(2,1)} copy(bf16[3,1,256,576]{3,2,0,1:T(8,128)(2,1)} %bitcast.11) | data formatting | bytes 1769472
  (5 shorter events, 0.0 us)
Async XLA Ops:
  7.2 67.6 %all-gather.4.cloned.1.call-start = ((), (), s32[]{:S(2)}) async-start(), calls=%async_computation.2 | async-start | bytes 4386816 | tf_op jit(solution)/shard_map/all_gather | solution.py:231
  9.1 10.2 %copy-start.4 = (f32[1152]{0:T(1024)S(1)}, f32[1152]{0:T(1024)}, u32[]{:S(2)}) copy-start(f32[1152]{0:T(1024)} %param.11) | copy-start | bytes 13828
  11.2 36.5 %all-to-all-start = ((bf16[16,16,1728]{2,1,0:T(8,128)(2,1)}), bf16[16,16,1728]{2,1,0:T(8,128)(2,1)S(1)}, u32[]{:S(2)}, u32[]{:S(2)}) async-start(bf16[16,16,1728]{2,1,0:T(8,128)(2,1)} %bitcast.2), calls=%async_computation | async-start | bytes 1835008 | tf_op jit(solution)/shard_map/all_to_all | solution.py:230
  18.6 99.4 %all-gather.6.cloned.1.call-start = ((), (), s32[]{:S(2)}) async-start(), calls=%async_computation.3 | async-start | bytes 1566720 | tf_op jit(solution)/shard_map/all_gather | solution.py:242
  74.8 2.2 %copy-start.1 = (bf16[1152,1728]{1,0:T(8,128)(2,1)S(1)}, bf16[1152,1728]{1,0:T(8,128)(2,1)}, u32[]{:S(2)}) copy-start(bf16[1152,1728]{1,0:T(8,128)(2,1)} %all-gather.4.cloned.1.call-done.w_ref) | copy-start | bytes 11943940
  77.0 11.8 %copy-start.3 = (bf16[3,1,256,576]{2,3,1,0:T(8,128)(2,1)S(1)}, bf16[3,1,256,576]{2,3,1,0:T(8,128)(2,1)}, u32[]{:S(2)}) copy-start(bf16[3,1,256,576]{2,3,1,0:T(8,128)(2,1)} %param.7) | copy-start | bytes 2654212
  84.5 35.8 %all-to-all-start.1 = ((bf16[16,16,1152]{2,1,0:T(8,128)(2,1)}), bf16[16,16,1152]{2,1,0:T(8,128)(2,1)}, u32[]{:S(2)}, u32[]{:S(2)}) async-start(bf16[16,16,1152]{2,1,0:T(8,128)(2,1)} %bitcast.4), calls=%async_computation.1 | async-start | bytes 1179648 | tf_op jit(solution)/shard_map/all_to_all | solution.py:234
  120.3 1.1 copy-start.2
  125.2 0.9 copy-start
Sparse Core Ops, SparseCore 0:
  10.3 64.4 all-gather.3
  76.9 41.0 all-gather.5

commit v2 on v1

--- a/solution.py
+++ b/solution.py
@@ -13,7 +13,7 @@
 LANES = 128
 
 epsilon = 1e-06
-VMEM_LIMIT = 48 * 1024 * 1024
+VMEM_LIMIT = 32 * 1024 * 1024
 
 
 def window(head, width):
@@ -77,19 +77,42 @@
     )
 
 
-def temporal_kernel(patches, x_ref, mod_ref, w_ref, out_ref, bias_ref, proj_ref, keys_ref, grad_ref, gk_ref):
-    tokens, width = out_ref.shape[0], w_ref.shape[1] // 3
-    depth = w_ref.shape[0]
+def temporal_kernel(patches, count, place_ref, x_ref, gain_ref, *refs):
+    pieces, refs = refs[:count], refs[count:]
+    out_ref, bias_ref, proj_ref, keys_ref, grad_ref, gk_ref, held_ref, sems = refs
+    tokens, depth = out_ref.shape
+    width = keys_ref.shape[1]
     scale = 1.0 / math.sqrt(HD)
+    copies = []
+    for index, piece in enumerate(pieces):
+        for slot in range(piece.shape[0]):
+            rows, columns = piece.shape[1:]
+            number = len(copies)
+            if rows == depth:
+                copies.append(pltpu.make_async_copy(piece.at[slot], held_ref, sems.at[number]))
+                copies[-1].start()
+                continue
+            row = pl.multiple_of(place_ref[2 * number], rows)
+            column = pl.multiple_of(place_ref[2 * number + 1], columns)
+            copies.append(
+                pltpu.make_async_copy(
+                    piece.at[slot],
+                    held_ref.at[pl.ds(row, rows), pl.ds(column, columns)],
+                    sems.at[number],
+                )
+            )
+            copies[-1].start()
     row = lax.broadcasted_iota(jnp.int32, (tokens, tokens), 0)
     column = lax.broadcasted_iota(jnp.int32, (tokens, tokens), 1)
     bias_ref[...] = jnp.where(lax.rem(row, patches) == lax.rem(column, patches), 0.0, -1e30)
-    gain = 1.0 + mod_ref[...]
+    gain = gain_ref[...]
     widened = x_ref[:, :depth].astype(jnp.float32)
     centered = widened - jnp.mean(widened, axis=-1, keepdims=True)
     inverse = lax.rsqrt(jnp.mean(centered * centered, axis=-1, keepdims=True) + epsilon)
     normed = (centered * inverse * gain).astype(jnp.bfloat16)
-    proj_ref[...] = dot_nn(normed, w_ref[...]).astype(jnp.bfloat16)
+    for copy in copies:
+        copy.wait()
+    proj_ref[...] = dot_nn(normed, held_ref[:, : 3 * width]).astype(jnp.bfloat16)
     keys_ref[...] = proj_ref[:, width : 2 * width]
     sums = [Tiles(), Tiles(), Tiles()]
     for head in range(HEADS):
@@ -107,7 +130,7 @@
         sums[1].store(gk_ref, 0, width, scale, upto)
         sums[2].store(grad_ref, 2 * width, width, 1.0, upto)
     grad_ref[:, width : 2 * width] = gk_ref[...]
-    scaled = dot_nt(grad_ref[...], w_ref[...]) * gain
+    scaled = dot_nt(grad_ref[...], held_ref[:, : 3 * width]) * gain
     widened = x_ref[:, :depth].astype(jnp.float32)
     centered = widened - jnp.mean(widened, axis=-1, keepdims=True)
     normal_form = centered * inverse
@@ -119,17 +142,25 @@
     out_ref[...] = branch.astype(out_ref.dtype)
 
 
-def temporal(mixed, modulation, weights, patches):
-    tokens, depth, width = mixed.shape[0], weights.shape[0], weights.shape[1] // 3
+def temporal(mixed, gain, pieces, places, width, patches):
+    tokens, depth = mixed.shape[0], gain.shape[1]
+    held = max(2 * pieces[0].shape[2], 3 * width) if len(pieces) > 1 else pieces[0].shape[2]
+    count = sum(piece.shape[0] for piece in pieces)
     return pl.pallas_call(
-        functools.partial(temporal_kernel, patches),
+        functools.partial(temporal_kernel, patches, len(pieces)),
         out_shape=jax.ShapeDtypeStruct((tokens, depth), jnp.bfloat16),
+        in_specs=[pl.BlockSpec(memory_space=pltpu.SMEM)]
+        + [pl.BlockSpec(memory_space=pltpu.VMEM)] * 2
+        + [pl.BlockSpec(memory_space=pl.ANY)] * len(pieces),
+        out_specs=pl.BlockSpec(memory_space=pltpu.VMEM),
         scratch_shapes=[
             pltpu.VMEM((tokens, tokens), jnp.float32),
             pltpu.VMEM((tokens, 3 * width), jnp.bfloat16),
             pltpu.VMEM((tokens, width), jnp.bfloat16),
             pltpu.VMEM((tokens, 3 * width), jnp.bfloat16),
             pltpu.VMEM((tokens, width), jnp.bfloat16),
+            pltpu.VMEM((depth, held), jnp.bfloat16),
+            pltpu.SemaphoreType.DMA((count,)),
         ],
         compiler_params=pltpu.CompilerParams(vmem_limit_bytes=VMEM_LIMIT),
         cost_estimate=pl.CostEstimate(
@@ -138,70 +169,94 @@
             transcendentals=HEADS * tokens * tokens,
         ),
         name="temporal_backward",
-    )(mixed, modulation.reshape(1, depth), weights)
-
-
-def score_kernel(saved_ref, out_ref):
-    width = saved_ref.shape[2]
+    )(places, mixed, gain, *pieces)
+
+
+def prepare_kernel(count, place_ref, saved_ref, stream_ref, *refs):
+    pieces, refs = refs[:count], refs[count:]
+    attention_ref, values_ref, held_stream_ref, weights_ref, held_ref, sems = refs
+    copies = []
+    for piece in pieces:
+        for slot in range(piece.shape[0]):
+            number = len(copies)
+            if piece.shape[2] == held_ref.shape[2]:
+                target = held_ref.at[slot]
+            else:
+                column = pl.multiple_of(place_ref[2 * number + 1], piece.shape[2])
+                target = held_ref.at[place_ref[2 * number], :, pl.ds(column, piece.shape[2])]
+            copies.append(pltpu.make_async_copy(piece.at[slot], target, sems.at[number]))
+            copies[-1].start()
+    held_stream_ref[...] = stream_ref[...]
     for head in range(HEADS):
-        start, stop, low, high = window(head, width)
-        keys = keep(saved_ref[1, :, start:stop], start, low, high)
-        scores_t = dot_nt(keys, saved_ref[0, :, start:stop])
-        out_ref[head] = soft(scores_t, 1.0 / math.sqrt(HD)).astype(out_ref.dtype)
-
-
-def score(saved):
-    tokens, width = saved.shape[1:]
+        scores_t = dot_tn(saved_ref[1, head], saved_ref[0, head])
+        attention_ref[head] = soft(scores_t, 1.0 / math.sqrt(HD)).astype(attention_ref.dtype)
+        values_ref[head] = saved_ref[2, head].astype(jnp.float32).T.astype(values_ref.dtype)
+    for copy in copies:
+        copy.wait()
+    blocks = [held_ref[chip].astype(jnp.float32) for chip in range(held_ref.shape[0])]
+    joined = jnp.concatenate(blocks, axis=0)[:, : weights_ref.shape[1]]
+    weights_ref[...] = joined.astype(weights_ref.dtype)
+
+
+def prepare(saved, stream, pieces, places, width):
+    tokens, depth = stream.shape
+    rows = pieces[0].shape[1]
+    held = max(depth, pieces[0].shape[2] * (1 if len(pieces) == 1 else 2))
+    count = sum(piece.shape[0] for piece in pieces)
     return pl.pallas_call(
-        score_kernel,
-        out_shape=jax.ShapeDtypeStruct((HEADS, tokens, tokens), jnp.bfloat16),
+        functools.partial(prepare_kernel, len(pieces)),
+        out_shape=(
+            jax.ShapeDtypeStruct((HEADS, tokens, tokens), jnp.bfloat16),
+            jax.ShapeDtypeStruct((HEADS, tokens, HD), jnp.bfloat16),
+            jax.ShapeDtypeStruct((tokens, depth), jnp.bfloat16),
+            jax.ShapeDtypeStruct((width, depth), jnp.bfloat16),
+        ),
+        in_specs=[pl.BlockSpec(memory_space=pltpu.SMEM)]
+        + [pl.BlockSpec(memory_space=pltpu.VMEM)] * 2
+        + [pl.BlockSpec(memory_space=pl.ANY)] * len(pieces),
+        out_specs=(pl.BlockSpec(memory_space=pltpu.VMEM),) * 4,
+        scratch_shapes=[
+            pltpu.VMEM((width // rows, rows, held), jnp.bfloat16),
+            pltpu.SemaphoreType.DMA((count,)),
+        ],
         compiler_params=pltpu.CompilerParams(vmem_limit_bytes=VMEM_LIMIT),
         cost_estimate=pl.CostEstimate(
             flops=2 * HEADS * tokens * tokens * 2 * LANES,
-            bytes_accessed=2 * (3 * tokens * width + HEADS * tokens * tokens),
+            bytes_accessed=2 * (4 * HEADS * tokens * HD + HEADS * tokens * tokens),
             transcendentals=HEADS * tokens * tokens,
         ),
-        name="spatial_scores",
-    )(saved)
-
-
-def spatial_kernel(attention_ref, saved_ref, stream_ref, branch_ref, w_ref, hidden_ref, out_ref, grad_ref):
-    width = saved_ref.shape[2]
+        name="spatial_prepare",
+    )(places, saved, stream, *pieces)
+
+
+def spatial_kernel(attention_ref, values_ref, saved_ref, stream_ref, branch_ref, w_ref, hidden_ref, out_ref):
     scale = 1.0 / math.sqrt(HD)
     hidden_grad = (
         stream_ref[...].astype(jnp.float32) + branch_ref[...].astype(jnp.float32)
     ).astype(jnp.bfloat16)
     hidden_ref[...] = hidden_grad
-    grad_ref[...] = dot_nt(hidden_grad, w_ref[...]).astype(jnp.bfloat16)
-    sums = [Tiles(), Tiles(), Tiles()]
+    grad_all = dot_nt(w_ref[...], hidden_grad)
     for head in range(HEADS):
-        start, stop, low, high = window(head, width)
-        parts = head_grads(
-            attention_ref[head],
-            saved_ref[0, :, start:stop],
-            saved_ref[1, :, start:stop],
-            saved_ref[2, :, start:stop],
-            grad_ref[:, start:stop],
-            start,
-            low,
-            high,
-        )
-        upto = width if head == HEADS - 1 else high // LANES * LANES
-        for index, (tiles, part) in enumerate(zip(sums, parts)):
-            tiles.add(start, part)
-            tiles.store(out_ref.at[index], 0, width, 1.0 if index == 2 else scale, upto)
-
-
-def spatial(attention_t, saved, stream, branch, weights):
+        grad_o = grad_all[head * HD : (head + 1) * HD].astype(jnp.bfloat16)
+        rounded_t = attention_ref[head]
+        wide = rounded_t.astype(jnp.float32)
+        spread_t = dot_nn(values_ref[head], grad_o)
+        delta = jnp.sum(wide * spread_t, axis=0, keepdims=True)
+        dscore_t = (wide * (spread_t - delta)).astype(jnp.bfloat16)
+        out_ref[0, head] = (dot_nn(saved_ref[1, head], dscore_t) * scale).astype(out_ref.dtype)
+        out_ref[1, head] = (dot_nt(saved_ref[0, head], dscore_t) * scale).astype(out_ref.dtype)
+        out_ref[2, head] = dot_nt(grad_o, rounded_t).astype(out_ref.dtype)
+
+
+def spatial(attention_t, values, saved, stream, branch, weights):
     tokens, depth = stream.shape
     width = weights.shape[0]
     return pl.pallas_call(
         spatial_kernel,
         out_shape=(
             jax.ShapeDtypeStruct((tokens, depth), jnp.bfloat16),
-            jax.ShapeDtypeStruct((3, tokens, width), jnp.bfloat16),
-        ),
-        scratch_shapes=[pltpu.VMEM((tokens, width), jnp.bfloat16)],
+            jax.ShapeDtypeStruct((3, HEADS, HD, tokens), jnp.bfloat16),
+        ),
         compiler_params=pltpu.CompilerParams(vmem_limit_bytes=VMEM_LIMIT),
         cost_estimate=pl.CostEstimate(
             flops=2 * tokens * depth * width + 10 * HEADS * tokens * tokens * 2 * LANES,
@@ -209,10 +264,75 @@
             transcendentals=0,
         ),
         name="spatial_backward",
-    )(attention_t, saved, stream, branch, weights)
+    )(attention_t, values, saved, stream, branch, weights)
+
+
+def moved(block, clips, devices, target):
+    pairs = []
+    for clip in range(clips):
+        for own in range(devices):
+            x, y, z, core = target(clip, own // 2 % 2, own // 4, own % 2)
+            pairs.append((clip * devices + own, x * devices + (2 * z + y) * 2 + core))
+    return lax.ppermute(block, ("clip", "seq"), pairs)
+
+
+class Gather:
+    def __init__(self, clips, devices):
+        self.send = functools.partial(moved, clips=clips, devices=devices)
+        clip, own = lax.axis_index("clip"), lax.axis_index("seq")
+        self.x, self.core, self.y, self.z = clip % 2, own % 2, own // 2 % 2, own // 4
+        self.pairs = devices // 8
+
+    def block(self, weights):
+        half = -(-weights.shape[1] // (2 * LANES)) * LANES
+        padded = jnp.pad(weights, ((0, 0), (0, 2 * half - weights.shape[1])))
+        mine = lax.dynamic_slice(padded, (0, half * self.x), (weights.shape[0], half))
+        other = self.send(mine, target=lambda x, y, z, core: (x, y, z, 1 - core))
+        return jnp.where(
+            self.core == 0, jnp.concatenate([mine, other]), jnp.concatenate([other, mine])
+        )
+
+    def along(self, block):
+        return [
+            self.send(block, target=lambda x, y, z, core: (x, y, z ^ (2 * pair + core), core))
+            for pair in range(self.pairs)
+        ]
+
+    def beside(self, first):
+        second = self.send(
+            first,
+            target=lambda x, y, z, core: (x, 1 - y, z, core) if core else (x ^ 1, y, z, core),
+        )
+        return jnp.concatenate([first, second])
+
+    def across(self, both):
+        rest = self.send(
+            both,
+            target=lambda x, y, z, core: (x ^ 1, y, z, core) if core else (x, 1 - y, z, core),
+        )
+        return jnp.concatenate([both, rest])
+
+    def swap(self, four):
+        return self.send(four, target=lambda x, y, z, core: (x, y, z, 1 - core))
+
+    def places(self, pairs, rows, half):
+        found = []
+        for parity in (self.core, 1 - self.core):
+            for slot in range(4):
+                for pair in pairs:
+                    far_x = jnp.where(parity == 0, slot % 2, slot // 2)
+                    far_y = jnp.where(parity == 0, slot // 2, slot % 2)
+                    chip = 2 * (self.z ^ (2 * pair + parity)) + (self.y ^ far_y)
+                    found += [rows * chip, half * (self.x ^ far_x)]
+        return found
+
+
+def tied(first, second):
+    return lax.optimization_barrier((first, second))
 
 
 def shards(
+    clips,
     spatial_saved,
     hidden,
     temporal_out_grad,
@@ -225,28 +345,57 @@
     tokens, depth = hidden.shape[1:]
     width = temporal_out_grad.shape[2]
     patches = tokens // frames
-    saved = spatial_saved.reshape(3, tokens, width)
+    chips = frames // 2
+    gain = 1.0 + modulation.reshape(1, depth)
+    saved = spatial_saved.transpose(0, 1, 3, 2).reshape(3, HEADS, HD, tokens)
     mixed = jnp.concatenate([hidden, temporal_out_grad], axis=2).reshape(frames, patches, depth + width)
-    mixed = lax.all_to_all(mixed, "seq", split_axis=0, concat_axis=0, tiled=True)
-    weights = lax.all_gather(temporal_weights, "seq", axis=0, tiled=True)
-    attention_t = score(saved)
-    branch = temporal(mixed.reshape(tokens, depth + width), modulation, weights, patches)
+    if clips % 2 == 0 and chips >= 4 and chips & (chips - 1) == 0 and 2 * depth // frames % 16 == 0:
+        gather = Gather(clips, frames)
+        firsts = gather.along(gather.block(temporal_weights))
+        small = gather.along(gather.block(spatial_weights))
+        rows, half = firsts[0].shape
+        places = [place for pair in range(len(firsts)) for place in gather.places([pair], rows, half)]
+        small_places = gather.places(range(len(firsts)), 1, small[0].shape[1])
+        places, small_places = (jnp.stack(p).astype(jnp.int32) for p in (places, small_places))
+        (firsts, small, places, small_places, gain), mixed = tied(
+            (firsts, small, places, small_places, gain), mixed
+        )
+        mixed = lax.all_to_all(mixed, "seq", split_axis=0, concat_axis=0, tiled=True)
+        both = [gather.beside(first[None]) for first in firsts]
+        small = gather.beside(jnp.stack(small))
+        both[0], small = tied(both[0], small)
+        four = [gather.across(block) for block in both]
+        four[-1], mixed = tied(four[-1], mixed)
+        pieces = [piece for block in four for piece in (block, gather.swap(block))]
+        small = gather.across(small)
+        small_pieces = [small, gather.swap(small)]
+    else:
+        mixed = lax.all_to_all(mixed, "seq", split_axis=0, concat_axis=0, tiled=True)
+        places = small_places = jnp.zeros((2,), jnp.int32)
+        pieces = [lax.all_gather(temporal_weights, "seq", axis=0, tiled=True)[None]]
+        small_pieces = [lax.all_gather(spatial_weights, "seq", axis=0, tiled=True)[None]]
+    branch = temporal(mixed.reshape(tokens, depth + width), gain, pieces, places, width, patches)
+    attention_t, values, stream, weights = prepare(
+        saved, stream_grad.reshape(tokens, depth), small_pieces, small_places, width
+    )
     branch = lax.all_to_all(
         branch.reshape(frames, patches, depth), "seq", split_axis=0, concat_axis=0, tiled=True
     )
     hidden_grad, spatial_grad = spatial(
         attention_t,
+        values,
         saved,
-        stream_grad.reshape(tokens, depth),
+        stream,
         branch.reshape(tokens, depth),
-        lax.all_gather(spatial_weights, "seq", axis=0, tiled=True),
-    )
-    return (hidden_grad.reshape(1, tokens, depth), spatial_grad.reshape(3, 1, tokens, width))
+        weights,
+    )
+    spatial_grad = spatial_grad.reshape(3, 1, width, tokens).transpose(0, 1, 3, 2)
+    return (hidden_grad.reshape(1, tokens, depth), spatial_grad)
 
 
 def solution(mesh):
     return jax.shard_map(
-        shards,
+        functools.partial(shards, mesh.shape["clip"]),
         mesh=mesh,
         in_specs=(
             P(None, ("clip", "seq"), None, None),

time: 136 us -> 106 us (0.78)
  waiting for transfers between devices: 84.5 us -> 48.8 us
  starting transfers between devices: 11.7 us -> 29.5 us
  between operations: 14.1 us -> 0.96 us
  Pallas kernels: 12.3 us -> 16.1 us
  local copies, waits for them, and re-layouts: 10.5 us -> 9.02 us
    all_gather x2 -> x0, waiting for transfers between devices: 54.8 us -> none  [the longest x1 27.7 us: shards(): lax.all_gather(spatial_weights, 'seq', axis=0, tiled=True)]
    ppermute x0 -> x15, waiting for transfers between devices: none -> 40.8 us  [moved(): return lax.ppermute(block, ('clip', 'seq'), pairs)]
    all_to_all x1, waiting for transfers between devices: 28.3 us -> 0.01 us  [shards(): lax.all_to_all(mixed, 'seq', split_axis=0, concat_axis=0, tiled=True)]
    ppermute x0 -> x15, starting transfers between devices: none -> 17 us  [moved(): return lax.ppermute(block, ('clip', 'seq'), pairs)]
    all_to_all x1, waiting for transfers between devices: 0.01 us -> 8 us  [shards(): lax.all_to_all(branch.reshape(frames, patches, depth), 'seq', split_axis=...]
    unnamed x14 -> x23, local copies, waits for them, and re-layouts: 10.5 us -> 5.89 us
    pallas_call x2, Pallas kernels: 8.38 us -> 11.4 us  [the longest x1 9.32 us: temporal(): pl.pallas_call(functools.partial(temporal_kernel, patches, len(pieces)),...]
    dynamic_slice x0 -> x2, local copies, waits for them, and re-layouts: none -> 1.81 us  [block(): lax.dynamic_slice(padded, (0, half * self.x), (weights.shape[0], half))]
  transfers between devices with their start and end apart: 4 -> 17, of which waited for: 3 -> 9; matrix products, arithmetic and copies ran while one was open for 5% -> 5% of each run, Pallas kernels for 6% -> 11%
where the time goes in v2:
time: 106 us
  waiting for transfers between devices  48.8 us (46%)
  starting transfers between devices  29.5 us (28%)
  Pallas kernels  16.1 us (15%)
  local copies, waits for them, and re-layouts  9.02 us (9%)
  other arithmetic  1.41 us (1%)
    ppermute x15, waiting for transfers between devices, moved(): return lax.ppermute(block, ('clip', 'seq'), pairs)  40.8 us
    ppermute x15, starting transfers between devices, moved(): return lax.ppermute(block, ('clip', 'seq'), pairs)  17 us
    pallas_call x1, Pallas kernels, temporal(): pl.pallas_call(functools.partial(temporal_kernel, patches, len(pieces)),...  9.32 us
    all_to_all x1, waiting for transfers between devices, shards(): lax.all_to_all(branch.reshape(frames, patches, depth), 'seq', split_axis=...  8 us
    all_to_all x1, starting transfers between devices, shards(): lax.all_to_all(mixed, 'seq', split_axis=0, concat_axis=0, tiled=True)  7.35 us
    unnamed x23, local copies, waits for them, and re-layouts  5.89 us
    all_to_all x1, starting transfers between devices, shards(): lax.all_to_all(branch.reshape(frames, patches, depth), 'seq', split_axis=...  5.12 us
    pallas_call x1, Pallas kernels, spatial(): pl.pallas_call(spatial_kernel, out_shape=(jax.ShapeDtypeStruct((tokens, d...  4.75 us
  transfers between devices with their start and end apart: 17, of which 9 were waited for; matrix products, arithmetic and copies ran while one was open for 5% of the time, Pallas kernels for 11%

profile of v2, /device:TPU:0, one launch (start us, length us, event | category | flops | bytes accessed | tf_op | source)
XLA Modules:
  0.0 105.9 jit_solution(12661681275324072457)
XLA Ops:
  3.0 1.2 %copy.9 = bf16[1,256,576]{2,1,0:T(8,128)(2,1)S(1)} copy(bf16[1,256,576]{1,2,0:T(8,128)(2,1)} %param.9) | data formatting | bytes 589824 | tf_op args[2]
  6.0 4.1 %collective-permute-start.2 = (bf16[144,896]{1,0:T(8,128)(2,1)S(1)}, bf16[144,896]{1,0:T(8,128)(2,1)S(1)}, u32[]{:S(2)}, u32[]{:S(2)}) collective-permute-start(bf16[144,896]{1,0:T(8,128)(2,1)S(1)} %maximum_select_fusion), channel_id=1, source_target_pairs={{0,8},{1,13},{2,10},{3,15},{4,12},{5,9},{6,14},{7,11},{8,0},{9,5},... | collective-permute-start | bytes 774152 | tf_op jit(solution)/shard_map/ppermute | solution.py:276
  11.3 14.0 %collective-permute-done.5 = bf16[72,640]{1,0:T(8,128)(2,1)S(1)} collective-permute-done((bf16[72,640]{1,0:T(8,128)(2,1)S(1)}, bf16[72,640]{1,0:T(8,128)(2,1)S(1)}, u32[]{:S(2)}, u32[]{:S(2)}) %collective-permute-start.5) | collective-permute-done | bytes 92192 | tf_op jit(solution)/shard_map/ppermute | solution.py:276
  25.2 7.3 %all-to-all-start = ((bf16[16,16,1728]{2,1,0:T(8,128)(2,1)}), bf16[16,16,1728]{2,1,0:T(8,128)(2,1)S(1)}, u32[]{:S(2)}, u32[]{:S(2)}) async-start(bf16[16,16,1728]{2,1,0:T(8,128)(2,1)} %bitcast.44), calls=%async_computation | async-start | bytes 1835008 | tf_op jit(solution)/shard_map/all_to_all | solution.py:363
  32.6 1.5 %collective-permute-start.7 = (bf16[2,72,640]{2,1,0:T(8,128)(2,1)S(1)}, bf16[2,72,640]{2,1,0:T(8,128)(2,1)S(1)}, u32[]{:S(2)}, u32[]{:S(2)}) collective-permute-start(bf16[2,72,640]{2,1,0:T(8,128)(2,1)S(1)} %pad_maximum_fusion.5), channel_id=1, source_target_pairs={{0,16},{1,3},{2,18},{3,1},{4,20},{5,7},{6,22},{7,5},{8,24},{9,11},... | collective-permute-start | bytes 552968 | tf_op jit(solution)/shard_map/ppermute | solution.py:276
  34.7 1.5 %collective-permute-start.10 = (bf16[1,144,896]{2,1,0:T(8,128)(2,1)S(1)}, bf16[1,144,896]{2,1,0:T(8,128)(2,1)S(1)}, u32[]{:S(2)}, u32[]{:S(2)}) collective-permute-start(bf16[1,144,896]{2,1,0:T(8,128)(2,1)S(1)} %bitcast.67), channel_id=1, source_target_pairs={{0,16},{1,3},{2,18},{3,1},{4,20},{5,7},{6,22},{7,5},{8,24},{9,11},... | collective-permute-start | bytes 774152 | tf_op jit(solution)/shard_map/ppermute | solution.py:276
  36.2 2.0 %collective-permute-done.7 = bf16[2,72,640]{2,1,0:T(8,128)(2,1)S(1)} collective-permute-done((bf16[2,72,640]{2,1,0:T(8,128)(2,1)S(1)}, bf16[2,72,640]{2,1,0:T(8,128)(2,1)S(1)}, u32[]{:S(2)}, u32[]{:S(2)}) %collective-permute-start.7) | collective-permute-done | bytes 184352 | tf_op jit(solution)/shard_map/ppermute | solution.py:276
  38.3 2.7 %collective-permute-done.6 = bf16[1,144,896]{2,1,0:T(8,128)(2,1)S(1)} collective-permute-done((bf16[1,144,896]{2,1,0:T(8,128)(2,1)S(1)}, bf16[1,144,896]{2,1,0:T(8,128)(2,1)S(1)}, u32[]{:S(2)}, u32[]{:S(2)}) %collective-permute-start.6) | collective-permute-done | bytes 258080 | tf_op jit(solution)/shard_map/ppermute | solution.py:276
  41.0 2.0 %collective-permute-start.12 = (bf16[2,144,896]{2,1,0:T(8,128)(2,1)S(1)}, bf16[2,144,896]{2,1,0:T(8,128)(2,1)S(1)}, u32[]{:S(2)}, u32[]{:S(2)}) collective-permute-start(bf16[2,144,896]{2,1,0:T(8,128)(2,1)S(1)} %pad_maximum_fusion.2), channel_id=1, source_target_pairs={{0,2},{1,17},{2,0},{3,19},{4,6},{5,21},{6,4},{7,23},{8,10},{9,25},... | collective-permute-start | bytes 1548296 | tf_op jit(solution)/shard_map/ppermute | solution.py:276
  43.8 2.0 %collective-permute-start.11 = (bf16[2,144,896]{2,1,0:T(8,128)(2,1)S(1)}, bf16[2,144,896]{2,1,0:T(8,128)(2,1)S(1)}, u32[]{:S(2)}, u32[]{:S(2)}) collective-permute-start(bf16[2,144,896]{2,1,0:T(8,128)(2,1)S(1)} %pad_maximum_fusion.3), channel_id=1, source_target_pairs={{0,2},{1,17},{2,0},{3,19},{4,6},{5,21},{6,4},{7,23},{8,10},{9,25},... | collective-permute-start | bytes 1548296 | tf_op jit(solution)/shard_map/ppermute | solution.py:276
  45.8 12.7 %collective-permute-done.12 = bf16[2,144,896]{2,1,0:T(8,128)(2,1)S(1)} collective-permute-done((bf16[2,144,896]{2,1,0:T(8,128)(2,1)S(1)}, bf16[2,144,896]{2,1,0:T(8,128)(2,1)S(1)}, u32[]{:S(2)}, u32[]{:S(2)}) %collective-permute-start.12) | collective-permute-done | bytes 516128 | tf_op jit(solution)/shard_map/ppermute | solution.py:276
  59.5 4.6 %collective-permute-done.11 = bf16[2,144,896]{2,1,0:T(8,128)(2,1)S(1)} collective-permute-done((bf16[2,144,896]{2,1,0:T(8,128)(2,1)S(1)}, bf16[2,144,896]{2,1,0:T(8,128)(2,1)S(1)}, u32[]{:S(2)}, u32[]{:S(2)}) %collective-permute-start.11) | collective-permute-done | bytes 516128 | tf_op jit(solution)/shard_map/ppermute | solution.py:276
  64.2 2.1 %collective-permute-start.14 = (bf16[4,144,896]{2,1,0:T(8,128)(2,1)S(1)}, bf16[4,144,896]{2,1,0:T(8,128)(2,1)S(1)}, u32[]{:S(2)}, u32[]{:S(2)}) collective-permute-start(bf16[4,144,896]{2,1,0:T(8,128)(2,1)S(1)} %pad_maximum_fusion.refs_2_), channel_id=1, source_target_pairs={{0,1},{1,0},{2,3},{3,2},{4,5},{5,4},{6,7},{7,6},{8,9},{9,8},{10,11... | collective-permute-start | bytes 3096584 | tf_op jit(solution)/shard_map/ppermute | solution.py:276
  66.3 2.3 %collective-permute-done.14.refs_3_ = bf16[4,144,896]{2,1,0:T(8,128)(2,1)S(1)} collective-permute-done((bf16[4,144,896]{2,1,0:T(8,128)(2,1)S(1)}, bf16[4,144,896]{2,1,0:T(8,128)(2,1)S(1)}, u32[]{:S(2)}, u32[]{:S(2)}) %collective-permute-start.14) | collective-permute-done | bytes 1032224 | tf_op jit(solution)/shard_map/ppermute | solution.py:276
  68.6 9.3 %temporal_backward.1 = bf16[256,1152]{1,0:T(8,128)(2,1)} custom-call(s32[32]{0:T(128)S(1)} %stack.189.place_ref, bf16[256,1728]{1,0:T(8,128)(2,1)S(1)} %bitcast.62, f32[1,1152]{1,0:T(1,128)S(1)} %add.141.gain_ref, bf16[4,144,896]{2,1,0:T(8,128)(2,1)S(1)} %constant_dynamic-update-slice_fusion.2.refs_0_, bf16[4,144,896]{2,1,0:T(8,128)(2,1)} %collective-permute-done.13.refs_1_, ...), custom_call_target="tpu_custom_call" | custom-call | flops 3649044480 | bytes 5750784 | tf_op jit(solution)/shard_map/temporal_backward/pallas_call | solution.py:149
  77.9 5.1 %all-to-all-start.1 = ((bf16[16,16,1152]{2,1,0:T(8,128)(2,1)}), bf16[16,16,1152]{2,1,0:T(8,128)(2,1)S(1)}, u32[]{:S(2)}, u32[]{:S(2)}) async-start(bf16[16,16,1152]{2,1,0:T(8,128)(2,1)} %bitcast.53), calls=%async_computation.1 | async-start | bytes 1179648 | tf_op jit(solution)/shard_map/all_to_all | solution.py:381
  83.1 1.0 constant_dynamic-update-slice_fusion.refs_0_
  84.6 1.8 %collective-permute-done.9.refs_1_ = bf16[8,72,640]{2,1,0:T(8,128)(2,1)S(1)} collective-permute-done((bf16[8,72,640]{2,1,0:T(8,128)(2,1)S(1)}, bf16[8,72,640]{2,1,0:T(8,128)(2,1)S(1)}, u32[]{:S(2)}, u32[]{:S(2)}) %collective-permute-start.9) | collective-permute-done | bytes 737312 | tf_op jit(solution)/shard_map/ppermute | solution.py:276
  86.4 2.1 %spatial_prepare.1 = (bf16[8,256,256]{2,1,0:T(8,128)(2,1)S(1)}, bf16[8,256,72]{2,1,0:T(8,128)(2,1)S(1)}, bf16[256,1152]{1,0:T(8,128)(2,1)S(1)}, bf16[576,1152]{1,0:T(8,128)(2,1)S(1)}) custom-call(s32[32]{0:T(128)S(1)} %stack.212.place_ref, bf16[3,8,72,256]{3,2,1,0:T(8,128)(2,1)S(1)} %bitcast.63, bf16[256,1152]{1,0:T(8,128)(2,1)S(1)} %bitcast.66, ...), custom_call_target="tpu_custom_call" | custom-call | flops 268435456 | bytes 2228224 | tf_op jit(solution)/shard_map/spatial_prepare/pallas_call | solution.py:206
  88.5 1.1 %copy-done.2 = bf16[576,1152]{1,0:T(8,128)(2,1)} copy-done((bf16[576,1152]{1,0:T(8,128)(2,1)}, bf16[576,1152]{1,0:T(8,128)(2,1)S(1)}, u32[]{:S(2)}) %copy-start.2) | copy-done | bytes 1327128
  90.6 8.0 %all-to-all-done.1 = bf16[16,16,1152]{2,1,0:T(8,128)(2,1)S(1)} async-done(((bf16[16,16,1152]{2,1,0:T(8,128)(2,1)}), bf16[16,16,1152]{2,1,0:T(8,128)(2,1)S(1)}, u32[]{:S(2)}, u32[]{:S(2)}) %all-to-all-start.1) | async-done | bytes 589856 | tf_op jit(solution)/shard_map/all_to_all | solution.py:381
  98.6 1.3 %copy-done.3 = bf16[576,1152]{1,0:T(8,128)(2,1)S(1)} copy-done((bf16[576,1152]{1,0:T(8,128)(2,1)S(1)}, bf16[576,1152]{1,0:T(8,128)(2,1)}, u32[]{:S(2)}) %copy-start.3) | copy-done | bytes 1327128
  99.9 1.2 %copy-done.5 = bf16[8,256,256]{2,1,0:T(8,128)(2,1)S(1)} copy-done((bf16[8,256,256]{2,1,0:T(8,128)(2,1)S(1)}, bf16[8,256,256]{2,1,0:T(8,128)(2,1)}, u32[]{:S(2)}) %copy-start.5) | copy-done | bytes 1048600
  101.1 4.8 %spatial_backward.1 = (bf16[256,1152]{1,0:T(8,128)(2,1)}, bf16[3,8,72,256]{3,2,1,0:T(8,128)(2,1)}) custom-call(bf16[8,256,256]{2,1,0:T(8,128)(2,1)S(1)} %copy-done.5, bf16[8,256,72]{2,1,0:T(8,128)(2,1)S(1)} %get-tuple-element.26.values_ref, bf16[3,8,72,256]{3,2,1,0:T(8,128)(2,1)S(1)} %bitcast.64, bf16[256,1152]{1,0:T(8,128)(2,1)S(1)} %get-tuple-element.27.stream_ref, ...), custom_call_target="tpu_custom_call" | custom-call | flops 1681915904 | bytes 4866048 | tf_op jit(solution)/shard_map/spatial_backward/pallas_call | solution.py:254
  (52 shorter events, 9.3 us)
Async XLA Ops:
  0.6 3.6 %copy-start.8 = (bf16[1,256,1152]{2,1,0:T(8,128)(2,1)S(1)}, bf16[1,256,1152]{2,1,0:T(8,128)(2,1)}, u32[]{:S(2)}) copy-start(bf16[1,256,1152]{2,1,0:T(8,128)(2,1)} %param.8) | copy-start | bytes 1769476
  1.7 3.6 %collective-permute-start = (bf16[72,896]{1,0:T(8,128)(2,1)S(1)}, bf16[72,896]{1,0:T(8,128)(2,1)S(1)}, u32[]{:S(2)}, u32[]{:S(2)}) collective-permute-start(bf16[72,896]{1,0:T(8,128)(2,1)S(1)} %pad_dynamic-slice_fusion), channel_id=1, source_target_pairs={{0,1},{1,0},{2,3},{3,2},{4,5},{5,4},{6,7},{7,6},{8,9},{9,8},{10,11... | collective-permute-start | bytes 387080 | tf_op jit(solution)/shard_map/ppermute | solution.py:276
  3.0 7.1 %collective-permute-start.3 = (bf16[36,640]{1,0:T(8,128)(2,1)S(1)}, bf16[36,640]{1,0:T(8,128)(2,1)S(1)}, u32[]{:S(2)}, u32[]{:S(2)}) collective-permute-start(bf16[36,640]{1,0:T(8,128)(2,1)S(1)} %pad_dynamic-slice_fusion.1), channel_id=1, source_target_pairs={{0,1},{1,0},{2,3},{3,2},{4,5},{5,4},{6,7},{7,6},{8,9},{9,8},{10,11... | collective-permute-start | bytes 138248 | tf_op jit(solution)/shard_map/ppermute | solution.py:276
  4.2 6.7 %copy-start.9 = (f32[1152]{0:T(1024)S(1)}, f32[1152]{0:T(1024)}, u32[]{:S(2)}) copy-start(f32[1152]{0:T(1024)} %param.11) | copy-start | bytes 13828
  5.3 19.9 %collective-permute-start.1 = (bf16[144,896]{1,0:T(8,128)(2,1)S(1)}, bf16[144,896]{1,0:T(8,128)(2,1)S(1)}, u32[]{:S(2)}, u32[]{:S(2)}) collective-permute-start(bf16[144,896]{1,0:T(8,128)(2,1)S(1)} %maximum_select_fusion), channel_id=1, source_target_pairs={{0,0},{1,5},{2,2},{3,7},{4,4},{5,1},{6,6},{7,3},{8,8},{9,13},{10,1... | collective-permute-start | bytes 774152 | tf_op jit(solution)/shard_map/ppermute | solution.py:276
  6.0 19.2 %collective-permute-start.2 = (bf16[144,896]{1,0:T(8,128)(2,1)S(1)}, bf16[144,896]{1,0:T(8,128)(2,1)S(1)}, u32[]{:S(2)}, u32[]{:S(2)}) collective-permute-start(bf16[144,896]{1,0:T(8,128)(2,1)S(1)} %maximum_select_fusion), channel_id=1, source_target_pairs={{0,8},{1,13},{2,10},{3,15},{4,12},{5,9},{6,14},{7,11},{8,0},{9,5},... | collective-permute-start | bytes 774152 | tf_op jit(solution)/shard_map/ppermute | solution.py:276
  10.1 1.1 %collective-permute-start.4 = (bf16[72,640]{1,0:T(8,128)(2,1)S(1)}, bf16[72,640]{1,0:T(8,128)(2,1)S(1)}, u32[]{:S(2)}, u32[]{:S(2)}) collective-permute-start(bf16[72,640]{1,0:T(8,128)(2,1)S(1)} %maximum_select_fusion.1), channel_id=1, source_target_pairs={{0,0},{1,5},{2,2},{3,7},{4,4},{5,1},{6,6},{7,3},{8,8},{9,13},{10,1... | collective-permute-start | bytes 276488 | tf_op jit(solution)/shard_map/ppermute | solution.py:276
  10.8 14.4 %collective-permute-start.5 = (bf16[72,640]{1,0:T(8,128)(2,1)S(1)}, bf16[72,640]{1,0:T(8,128)(2,1)S(1)}, u32[]{:S(2)}, u32[]{:S(2)}) collective-permute-start(bf16[72,640]{1,0:T(8,128)(2,1)S(1)} %maximum_select_fusion.1), channel_id=1, source_target_pairs={{0,8},{1,13},{2,10},{3,15},{4,12},{5,9},{6,14},{7,11},{8,0},{9,5},... | collective-permute-start | bytes 276488 | tf_op jit(solution)/shard_map/ppermute | solution.py:276
  25.2 18.5 %copy-start.6 = (bf16[144,896]{1,0:T(8,128)(2,1)}, bf16[144,896]{1,0:T(8,128)(2,1)S(1)}, u32[]{:S(2)}) copy-start(bf16[144,896]{1,0:T(8,128)(2,1)S(1)} %collective-permute-done.2) | copy-start | bytes 774148
  25.2 39.0 %all-to-all-start = ((bf16[16,16,1728]{2,1,0:T(8,128)(2,1)}), bf16[16,16,1728]{2,1,0:T(8,128)(2,1)S(1)}, u32[]{:S(2)}, u32[]{:S(2)}) async-start(bf16[16,16,1728]{2,1,0:T(8,128)(2,1)} %bitcast.44), calls=%async_computation | async-start | bytes 1835008 | tf_op jit(solution)/shard_map/all_to_all | solution.py:363
  32.6 5.6 %collective-permute-start.7 = (bf16[2,72,640]{2,1,0:T(8,128)(2,1)S(1)}, bf16[2,72,640]{2,1,0:T(8,128)(2,1)S(1)}, u32[]{:S(2)}, u32[]{:S(2)}) collective-permute-start(bf16[2,72,640]{2,1,0:T(8,128)(2,1)S(1)} %pad_maximum_fusion.5), channel_id=1, source_target_pairs={{0,16},{1,3},{2,18},{3,1},{4,20},{5,7},{6,22},{7,5},{8,24},{9,11},... | collective-permute-start | bytes 552968 | tf_op jit(solution)/shard_map/ppermute | solution.py:276
  34.1 6.8 %collective-permute-start.6 = (bf16[1,144,896]{2,1,0:T(8,128)(2,1)S(1)}, bf16[1,144,896]{2,1,0:T(8,128)(2,1)S(1)}, u32[]{:S(2)}, u32[]{:S(2)}) collective-permute-start(bf16[1,144,896]{2,1,0:T(8,128)(2,1)S(1)} %bitcast.74), channel_id=1, source_target_pairs={{0,16},{1,3},{2,18},{3,1},{4,20},{5,7},{6,22},{7,5},{8,24},{9,11},... | collective-permute-start | bytes 774152 | tf_op jit(solution)/shard_map/ppermute | solution.py:276
  34.7 9.0 %collective-permute-start.10 = (bf16[1,144,896]{2,1,0:T(8,128)(2,1)S(1)}, bf16[1,144,896]{2,1,0:T(8,128)(2,1)S(1)}, u32[]{:S(2)}, u32[]{:S(2)}) collective-permute-start(bf16[1,144,896]{2,1,0:T(8,128)(2,1)S(1)} %bitcast.67), channel_id=1, source_target_pairs={{0,16},{1,3},{2,18},{3,1},{4,20},{5,7},{6,22},{7,5},{8,24},{9,11},... | collective-permute-start | bytes 774152 | tf_op jit(solution)/shard_map/ppermute | solution.py:276
  41.0 17.5 %collective-permute-start.12 = (bf16[2,144,896]{2,1,0:T(8,128)(2,1)S(1)}, bf16[2,144,896]{2,1,0:T(8,128)(2,1)S(1)}, u32[]{:S(2)}, u32[]{:S(2)}) collective-permute-start(bf16[2,144,896]{2,1,0:T(8,128)(2,1)S(1)} %pad_maximum_fusion.2), channel_id=1, source_target_pairs={{0,2},{1,17},{2,0},{3,19},{4,6},{5,21},{6,4},{7,23},{8,10},{9,25},... | collective-permute-start | bytes 1548296 | tf_op jit(solution)/shard_map/ppermute | solution.py:276
  43.8 20.3 %copy-start.7 = (bf16[144,896]{1,0:T(8,128)(2,1)S(1)}, bf16[144,896]{1,0:T(8,128)(2,1)}, u32[]{:S(2)}) copy-start(bf16[144,896]{1,0:T(8,128)(2,1)} %copy-done.6) | copy-start | bytes 774148
  43.8 20.3 %collective-permute-start.11 = (bf16[2,144,896]{2,1,0:T(8,128)(2,1)S(1)}, bf16[2,144,896]{2,1,0:T(8,128)(2,1)S(1)}, u32[]{:S(2)}, u32[]{:S(2)}) collective-permute-start(bf16[2,144,896]{2,1,0:T(8,128)(2,1)S(1)} %pad_maximum_fusion.3), channel_id=1, source_target_pairs={{0,2},{1,17},{2,0},{3,19},{4,6},{5,21},{6,4},{7,23},{8,10},{9,25},... | collective-permute-start | bytes 1548296 | tf_op jit(solution)/shard_map/ppermute | solution.py:276
  58.6 7.7 %collective-permute-start.13 = (bf16[4,144,896]{2,1,0:T(8,128)(2,1)S(1)}, bf16[4,144,896]{2,1,0:T(8,128)(2,1)}, u32[]{:S(2)}, u32[]{:S(2)}) collective-permute-start(bf16[4,144,896]{2,1,0:T(8,128)(2,1)S(1)} %constant_dynamic-update-slice_fusion.2.refs_0_), channel_id=1, source_target_pairs={{0,1},{1,0},{2,3},{3,2},{4,5},{5,4},{6,7},{7,6},{8,9},{9,8},{10,11... | collective-permute-start | bytes 3096584 | tf_op jit(solution)/shard_map/ppermute | solution.py:276
  64.2 4.3 %collective-permute-start.14 = (bf16[4,144,896]{2,1,0:T(8,128)(2,1)S(1)}, bf16[4,144,896]{2,1,0:T(8,128)(2,1)S(1)}, u32[]{:S(2)}, u32[]{:S(2)}) collective-permute-start(bf16[4,144,896]{2,1,0:T(8,128)(2,1)S(1)} %pad_maximum_fusion.refs_2_), channel_id=1, source_target_pairs={{0,1},{1,0},{2,3},{3,2},{4,5},{5,4},{6,7},{7,6},{8,9},{9,8},{10,11... | collective-permute-start | bytes 3096584 | tf_op jit(solution)/shard_map/ppermute | solution.py:276
  66.3 16.8 %collective-permute-start.8 = (bf16[4,72,640]{2,1,0:T(8,128)(2,1)S(1)}, bf16[4,72,640]{2,1,0:T(8,128)(2,1)}, u32[]{:S(2)}, u32[]{:S(2)}) collective-permute-start(bf16[4,72,640]{2,1,0:T(8,128)(2,1)S(1)} %pad_maximum_fusion.4), channel_id=1, source_target_pairs={{0,2},{1,17},{2,0},{3,19},{4,6},{5,21},{6,4},{7,23},{8,10},{9,25},... | collective-permute-start | bytes 1105928 | tf_op jit(solution)/shard_map/ppermute | solution.py:276
  77.9 8.5 %copy-start = (bf16[3,1,256,576]{2,3,1,0:T(8,128)(2,1)S(1)}, bf16[3,1,256,576]{2,3,1,0:T(8,128)(2,1)}, u32[]{:S(2)}) copy-start(bf16[3,1,256,576]{2,3,1,0:T(8,128)(2,1)} %param.7) | copy-start | bytes 2654212
  77.9 8.5 %copy-start.1 = (bf16[1,256,1152]{2,1,0:T(8,128)(2,1)S(1)}, bf16[1,256,1152]{2,1,0:T(8,128)(2,1)}, u32[]{:S(2)}) copy-start(bf16[1,256,1152]{2,1,0:T(8,128)(2,1)} %param.10) | copy-start | bytes 1769476
  77.9 20.7 %all-to-all-start.1 = ((bf16[16,16,1152]{2,1,0:T(8,128)(2,1)}), bf16[16,16,1152]{2,1,0:T(8,128)(2,1)S(1)}, u32[]{:S(2)}, u32[]{:S(2)}) async-start(bf16[16,16,1152]{2,1,0:T(8,128)(2,1)} %bitcast.53), calls=%async_computation.1 | async-start | bytes 1179648 | tf_op jit(solution)/shard_map/all_to_all | solution.py:381
  84.1 2.3 %collective-permute-start.9 = (bf16[8,72,640]{2,1,0:T(8,128)(2,1)S(1)}, bf16[8,72,640]{2,1,0:T(8,128)(2,1)S(1)}, u32[]{:S(2)}, u32[]{:S(2)}) collective-permute-start(bf16[8,72,640]{2,1,0:T(8,128)(2,1)S(1)} %constant_dynamic-update-slice_fusion.refs_0_), channel_id=1, source_target_pairs={{0,1},{1,0},{2,3},{3,2},{4,5},{5,4},{6,7},{7,6},{8,9},{9,8},{10,11... | collective-permute-start | bytes 2211848 | tf_op jit(solution)/shard_map/ppermute | solution.py:276
  98.6 1.3 %copy-start.3 = (bf16[576,1152]{1,0:T(8,128)(2,1)S(1)}, bf16[576,1152]{1,0:T(8,128)(2,1)}, u32[]{:S(2)}) copy-start(bf16[576,1152]{1,0:T(8,128)(2,1)} %copy-done.2) | copy-start | bytes 3981316
  (3 other events, 3.3 us)

commit v3 on v2

--- a/solution.py
+++ b/solution.py
@@ -11,9 +11,10 @@
 HEADS = 8
 HD = 72
 LANES = 128
+PARTS = 2
 
 epsilon = 1e-06
-VMEM_LIMIT = 32 * 1024 * 1024
+VMEM_LIMIT = 24 * 1024 * 1024
 
 
 def window(head, width):
@@ -174,7 +175,8 @@
 
 def prepare_kernel(count, place_ref, saved_ref, stream_ref, *refs):
     pieces, refs = refs[:count], refs[count:]
-    attention_ref, values_ref, held_stream_ref, weights_ref, held_ref, sems = refs
+    attention_refs, weights_refs = refs[:PARTS], refs[PARTS : 2 * PARTS]
+    values_ref, held_stream_ref, held_ref, sems = refs[2 * PARTS :]
     copies = []
     for piece in pieces:
         for slot in range(piece.shape[0]):
@@ -189,13 +191,16 @@
     held_stream_ref[...] = stream_ref[...]
     for head in range(HEADS):
         scores_t = dot_tn(saved_ref[1, head], saved_ref[0, head])
-        attention_ref[head] = soft(scores_t, 1.0 / math.sqrt(HD)).astype(attention_ref.dtype)
+        part = attention_refs[head * PARTS // HEADS]
+        part[head % (HEADS // PARTS)] = soft(scores_t, 1.0 / math.sqrt(HD)).astype(part.dtype)
         values_ref[head] = saved_ref[2, head].astype(jnp.float32).T.astype(values_ref.dtype)
     for copy in copies:
         copy.wait()
     blocks = [held_ref[chip].astype(jnp.float32) for chip in range(held_ref.shape[0])]
-    joined = jnp.concatenate(blocks, axis=0)[:, : weights_ref.shape[1]]
-    weights_ref[...] = joined.astype(weights_ref.dtype)
+    joined = jnp.concatenate(blocks, axis=0)
+    for index, part in enumerate(weights_refs):
+        rows, depth = part.shape
+        part[...] = joined[index * rows : (index + 1) * rows, :depth].astype(part.dtype)
 
 
 def prepare(saved, stream, pieces, places, width):
@@ -205,16 +210,16 @@
     count = sum(piece.shape[0] for piece in pieces)
     return pl.pallas_call(
         functools.partial(prepare_kernel, len(pieces)),
-        out_shape=(
-            jax.ShapeDtypeStruct((HEADS, tokens, tokens), jnp.bfloat16),
+        out_shape=(jax.ShapeDtypeStruct((HEADS // PARTS, tokens, tokens), jnp.bfloat16),) * PARTS
+        + (jax.ShapeDtypeStruct((width // PARTS, depth), jnp.bfloat16),) * PARTS
+        + (
             jax.ShapeDtypeStruct((HEADS, tokens, HD), jnp.bfloat16),
             jax.ShapeDtypeStruct((tokens, depth), jnp.bfloat16),
-            jax.ShapeDtypeStruct((width, depth), jnp.bfloat16),
         ),
         in_specs=[pl.BlockSpec(memory_space=pltpu.SMEM)]
         + [pl.BlockSpec(memory_space=pltpu.VMEM)] * 2
         + [pl.BlockSpec(memory_space=pl.ANY)] * len(pieces),
-        out_specs=(pl.BlockSpec(memory_space=pltpu.VMEM),) * 4,
+        out_specs=(pl.BlockSpec(memory_space=pltpu.VMEM),) * (2 * PARTS + 2),
         scratch_shapes=[
             pltpu.VMEM((width // rows, rows, held), jnp.bfloat16),
             pltpu.SemaphoreType.DMA((count,)),
@@ -229,16 +234,17 @@
     )(places, saved, stream, *pieces)
 
 
-def spatial_kernel(attention_ref, values_ref, saved_ref, stream_ref, branch_ref, w_ref, hidden_ref, out_ref):
+def spatial_kernel(values_ref, saved_ref, stream_ref, branch_ref, *refs):
+    attention_refs, w_refs, (hidden_ref, out_ref) = refs[:PARTS], refs[PARTS:-2], refs[-2:]
     scale = 1.0 / math.sqrt(HD)
     hidden_grad = (
         stream_ref[...].astype(jnp.float32) + branch_ref[...].astype(jnp.float32)
     ).astype(jnp.bfloat16)
     hidden_ref[...] = hidden_grad
-    grad_all = dot_nt(w_ref[...], hidden_grad)
+    grad_all = jnp.concatenate([dot_nt(w_ref[...], hidden_grad) for w_ref in w_refs], axis=0)
     for head in range(HEADS):
         grad_o = grad_all[head * HD : (head + 1) * HD].astype(jnp.bfloat16)
-        rounded_t = attention_ref[head]
+        rounded_t = attention_refs[head * PARTS // HEADS][head % (HEADS // PARTS)]
         wide = rounded_t.astype(jnp.float32)
         spread_t = dot_nn(values_ref[head], grad_o)
         delta = jnp.sum(wide * spread_t, axis=0, keepdims=True)
@@ -250,7 +256,7 @@
 
 def spatial(attention_t, values, saved, stream, branch, weights):
     tokens, depth = stream.shape
-    width = weights.shape[0]
+    width = HEADS * HD
     return pl.pallas_call(
         spatial_kernel,
         out_shape=(
@@ -264,7 +270,7 @@
             transcendentals=0,
         ),
         name="spatial_backward",
-    )(attention_t, values, saved, stream, branch, weights)
+    )(values, saved, stream, branch, *attention_t, *weights)
 
 
 def moved(block, clips, devices, target):
@@ -303,7 +309,7 @@
             first,
             target=lambda x, y, z, core: (x, 1 - y, z, core) if core else (x ^ 1, y, z, core),
         )
-        return jnp.concatenate([first, second])
+        return first, second
 
     def across(self, both):
         rest = self.send(
@@ -351,43 +357,42 @@
     mixed = jnp.concatenate([hidden, temporal_out_grad], axis=2).reshape(frames, patches, depth + width)
     if clips % 2 == 0 and chips >= 4 and chips & (chips - 1) == 0 and 2 * depth // frames % 16 == 0:
         gather = Gather(clips, frames)
-        firsts = gather.along(gather.block(temporal_weights))
-        small = gather.along(gather.block(spatial_weights))
+        block = gather.block(temporal_weights)
+        firsts = gather.along(block)
         rows, half = firsts[0].shape
+        small_block = gather.block(spatial_weights)
         places = [place for pair in range(len(firsts)) for place in gather.places([pair], rows, half)]
-        small_places = gather.places(range(len(firsts)), 1, small[0].shape[1])
+        small_places = gather.places(range(len(firsts)), 1, small_block.shape[1])
         places, small_places = (jnp.stack(p).astype(jnp.int32) for p in (places, small_places))
-        (firsts, small, places, small_places, gain), mixed = tied(
-            (firsts, small, places, small_places, gain), mixed
+        both = [jnp.concatenate(gather.beside(firsts[0][None]))]
+        (both[0], firsts, small_block, places, small_places, gain), mixed = tied(
+            (both[0], firsts, small_block, places, small_places, gain), mixed
         )
         mixed = lax.all_to_all(mixed, "seq", split_axis=0, concat_axis=0, tiled=True)
-        both = [gather.beside(first[None]) for first in firsts]
-        small = gather.beside(jnp.stack(small))
-        both[0], small = tied(both[0], small)
+        both += [jnp.concatenate(gather.beside(first[None])) for first in firsts[1:]]
+        small = jnp.stack(gather.along(small_block))
         four = [gather.across(block) for block in both]
-        four[-1], mixed = tied(four[-1], mixed)
+        (four[-1], small), mixed = tied((four[-1], small), mixed)
         pieces = [piece for block in four for piece in (block, gather.swap(block))]
-        small = gather.across(small)
-        small_pieces = [small, gather.swap(small)]
+        small = gather.beside(small)
     else:
         mixed = lax.all_to_all(mixed, "seq", split_axis=0, concat_axis=0, tiled=True)
         places = small_places = jnp.zeros((2,), jnp.int32)
         pieces = [lax.all_gather(temporal_weights, "seq", axis=0, tiled=True)[None]]
-        small_pieces = [lax.all_gather(spatial_weights, "seq", axis=0, tiled=True)[None]]
+        gather, small_pieces = None, [lax.all_gather(spatial_weights, "seq", axis=0, tiled=True)[None]]
     branch = temporal(mixed.reshape(tokens, depth + width), gain, pieces, places, width, patches)
-    attention_t, values, stream, weights = prepare(
+    if gather:
+        small, branch = tied(small, branch)
+        small = gather.across(jnp.concatenate(small))
+        small_pieces = [small, gather.swap(small)]
+    *parts, values, stream = prepare(
         saved, stream_grad.reshape(tokens, depth), small_pieces, small_places, width
     )
     branch = lax.all_to_all(
         branch.reshape(frames, patches, depth), "seq", split_axis=0, concat_axis=0, tiled=True
     )
     hidden_grad, spatial_grad = spatial(
-        attention_t,
-        values,
-        saved,
-        stream,
-        branch.reshape(tokens, depth),
-        weights,
+        parts[:PARTS], values, saved, stream, branch.reshape(tokens, depth), parts[PARTS:]
     )
     spatial_grad = spatial_grad.reshape(3, 1, width, tokens).transpose(0, 1, 3, 2)
     return (hidden_grad.reshape(1, tokens, depth), spatial_grad)

time: 106 us -> 98.7 us (0.931)
  waiting for transfers between devices: 48.8 us -> 42.1 us
  local copies, waits for them, and re-layouts: 9.02 us -> 7.28 us
  starting transfers between devices: 29.5 us -> 30.9 us
    ppermute x15, starting transfers between devices: 17 us -> 22.2 us  [moved(): return lax.ppermute(block, ('clip', 'seq'), pairs)]
    ppermute x15, waiting for transfers between devices: 40.8 us -> 35.9 us  [moved(): return lax.ppermute(block, ('clip', 'seq'), pairs)]
    all_to_all x1, starting transfers between devices: 7.35 us -> 4.98 us  [shards(): lax.all_to_all(mixed, 'seq', split_axis=0, concat_axis=0, tiled=True)]
    all_to_all x1, waiting for transfers between devices: 8 us -> 6.2 us  [shards(): lax.all_to_all(branch.reshape(frames, patches, depth), 'seq', split_axis=...]
    all_to_all x1, starting transfers between devices: 5.12 us -> 3.76 us  [shards(): lax.all_to_all(branch.reshape(frames, patches, depth), 'seq', split_axis=...]
    unnamed x23 -> x28, local copies, waits for them, and re-layouts: 5.89 us -> 5.9 us
  transfers between devices with their start and end apart: 17 -> 17, of which waited for: 9 -> 10; matrix products, arithmetic and copies ran while one was open for 5% -> 2% of each run, Pallas kernels for 11% -> 12%
where the time goes in v3:
time: 98.7 us; the launch traced here: 98.2 us
  waiting for transfers between devices  42.1 us (43%)
  starting transfers between devices  30.9 us (31%)
  Pallas kernels  15.6 us (16%)
  local copies, waits for them, and re-layouts  7.28 us (7%)
  other arithmetic  1.4 us (1%)
    ppermute x15, waiting for transfers between devices, moved(): return lax.ppermute(block, ('clip', 'seq'), pairs)  35.9 us
    ppermute x15, starting transfers between devices, moved(): return lax.ppermute(block, ('clip', 'seq'), pairs)  22.2 us
    pallas_call x1, Pallas kernels, temporal(): pl.pallas_call(functools.partial(temporal_kernel, patches, len(pieces)),...  9.33 us
    all_to_all x1, waiting for transfers between devices, shards(): lax.all_to_all(branch.reshape(frames, patches, depth), 'seq', split_axis=...  6.2 us
    unnamed x28, local copies, waits for them, and re-layouts  5.9 us
    all_to_all x1, starting transfers between devices, shards(): lax.all_to_all(mixed, 'seq', split_axis=0, concat_axis=0, tiled=True)  4.98 us
    pallas_call x1, Pallas kernels, spatial(): pl.pallas_call(spatial_kernel, out_shape=(jax.ShapeDtypeStruct((tokens, d...  4.2 us
    all_to_all x1, starting transfers between devices, shards(): lax.all_to_all(branch.reshape(frames, patches, depth), 'seq', split_axis=...  3.76 us
  transfers between devices with their start and end apart: 17, of which 10 were waited for; matrix products, arithmetic and copies ran while one was open for 2% of the time, Pallas kernels for 12%

profile of v3, /device:TPU:0, one launch (start us, length us, event | category | flops | bytes accessed | tf_op | source)
XLA Modules:
  0.0 98.2 jit_solution(4619552673393415379)
XLA Ops:
  4.0 4.1 %collective-permute-start.4 = (bf16[36,640]{1,0:T(8,128)(2,1)S(1)}, bf16[36,640]{1,0:T(8,128)(2,1)S(1)}, u32[]{:S(2)}, u32[]{:S(2)}) collective-permute-start(bf16[36,640]{1,0:T(8,128)(2,1)S(1)} %pad_dynamic-slice_fusion.1), channel_id=1, source_target_pairs={{0,1},{1,0},{2,3},{3,2},{4,5},{5,4},{6,7},{7,6},{8,9},{9,8},{10,11... | collective-permute-start | bytes 138248 | tf_op jit(solution)/shard_map/ppermute | solution.py:282
  9.3 2.6 %collective-permute-start.3 = (bf16[144,896]{1,0:T(8,128)(2,1)S(1)}, bf16[144,896]{1,0:T(8,128)(2,1)S(1)}, u32[]{:S(2)}, u32[]{:S(2)}) collective-permute-start(bf16[144,896]{1,0:T(8,128)(2,1)S(1)} %maximum_select_fusion), channel_id=1, source_target_pairs={{0,8},{1,13},{2,10},{3,15},{4,12},{5,9},{6,14},{7,11},{8,0},{9,5},... | collective-permute-start | bytes 774152 | tf_op jit(solution)/shard_map/ppermute | solution.py:282
  11.9 1.5 %collective-permute-start.2 = (bf16[1,144,896]{2,1,0:T(8,128)(2,1)S(1)}, bf16[1,144,896]{2,1,0:T(8,128)(2,1)S(1)}, u32[]{:S(2)}, u32[]{:S(2)}) collective-permute-start(bf16[1,144,896]{2,1,0:T(8,128)(2,1)S(1)} %bitcast.70), channel_id=1, source_target_pairs={{0,16},{1,3},{2,18},{3,1},{4,20},{5,7},{6,22},{7,5},{8,24},{9,11},... | collective-permute-start | bytes 774152 | tf_op jit(solution)/shard_map/ppermute | solution.py:282
  13.7 4.5 %collective-permute-done.2 = bf16[1,144,896]{2,1,0:T(8,128)(2,1)S(1)} collective-permute-done((bf16[1,144,896]{2,1,0:T(8,128)(2,1)S(1)}, bf16[1,144,896]{2,1,0:T(8,128)(2,1)S(1)}, u32[]{:S(2)}, u32[]{:S(2)}) %collective-permute-start.2) | collective-permute-done | bytes 258080 | tf_op jit(solution)/shard_map/ppermute | solution.py:282
  18.3 5.5 %collective-permute-done.3 = bf16[144,896]{1,0:T(8,128)(2,1)S(1)} collective-permute-done((bf16[144,896]{1,0:T(8,128)(2,1)S(1)}, bf16[144,896]{1,0:T(8,128)(2,1)S(1)}, u32[]{:S(2)}, u32[]{:S(2)}) %collective-permute-start.3) | collective-permute-done | bytes 258080 | tf_op jit(solution)/shard_map/ppermute | solution.py:282
  23.8 5.0 %all-to-all-start = ((bf16[16,16,1728]{2,1,0:T(8,128)(2,1)}), bf16[16,16,1728]{2,1,0:T(8,128)(2,1)S(1)}, u32[]{:S(2)}, u32[]{:S(2)}) async-start(bf16[16,16,1728]{2,1,0:T(8,128)(2,1)} %bitcast.45), calls=%async_computation | async-start | bytes 1835008 | tf_op jit(solution)/shard_map/all_to_all | solution.py:371
  28.8 1.6 %collective-permute-start.5 = (bf16[1,144,896]{2,1,0:T(8,128)(2,1)S(1)}, bf16[1,144,896]{2,1,0:T(8,128)(2,1)S(1)}, u32[]{:S(2)}, u32[]{:S(2)}) collective-permute-start(bf16[1,144,896]{2,1,0:T(8,128)(2,1)S(1)} %bitcast.67), channel_id=1, source_target_pairs={{0,16},{1,3},{2,18},{3,1},{4,20},{5,7},{6,22},{7,5},{8,24},{9,11},... | collective-permute-start | bytes 774152 | tf_op jit(solution)/shard_map/ppermute | solution.py:282
  30.4 1.9 %collective-permute-start.10 = (bf16[2,144,896]{2,1,0:T(8,128)(2,1)S(1)}, bf16[2,144,896]{2,1,0:T(8,128)(2,1)S(1)}, u32[]{:S(2)}, u32[]{:S(2)}) collective-permute-start(bf16[2,144,896]{2,1,0:T(8,128)(2,1)S(1)} %pad_maximum_fusion.2), channel_id=1, source_target_pairs={{0,2},{1,17},{2,0},{3,19},{4,6},{5,21},{6,4},{7,23},{8,10},{9,25},... | collective-permute-start | bytes 1548296 | tf_op jit(solution)/shard_map/ppermute | solution.py:282
  32.2 5.0 %collective-permute-done.5 = bf16[1,144,896]{2,1,0:T(8,128)(2,1)S(1)} collective-permute-done((bf16[1,144,896]{2,1,0:T(8,128)(2,1)S(1)}, bf16[1,144,896]{2,1,0:T(8,128)(2,1)S(1)}, u32[]{:S(2)}, u32[]{:S(2)}) %collective-permute-start.5) | collective-permute-done | bytes 258080 | tf_op jit(solution)/shard_map/ppermute | solution.py:282
  37.3 2.6 %collective-permute-start.6 = (bf16[2,144,896]{2,1,0:T(8,128)(2,1)S(1)}, bf16[2,144,896]{2,1,0:T(8,128)(2,1)S(1)}, u32[]{:S(2)}, u32[]{:S(2)}) collective-permute-start(bf16[2,144,896]{2,1,0:T(8,128)(2,1)S(1)} %pad_maximum_fusion.3), channel_id=1, source_target_pairs={{0,2},{1,17},{2,0},{3,19},{4,6},{5,21},{6,4},{7,23},{8,10},{9,25},... | collective-permute-start | bytes 1548296 | tf_op jit(solution)/shard_map/ppermute | solution.py:282
  40.6 2.4 %collective-permute-start.8 = (bf16[72,640]{1,0:T(8,128)(2,1)S(1)}, bf16[72,640]{1,0:T(8,128)(2,1)S(1)}, u32[]{:S(2)}, u32[]{:S(2)}) collective-permute-start(bf16[72,640]{1,0:T(8,128)(2,1)S(1)} %maximum_select_fusion.1), channel_id=1, source_target_pairs={{0,8},{1,13},{2,10},{3,15},{4,12},{5,9},{6,14},{7,11},{8,0},{9,5},... | collective-permute-start | bytes 276488 | tf_op jit(solution)/shard_map/ppermute | solution.py:282
  43.0 13.5 %collective-permute-done.8 = bf16[72,640]{1,0:T(8,128)(2,1)S(1)} collective-permute-done((bf16[72,640]{1,0:T(8,128)(2,1)S(1)}, bf16[72,640]{1,0:T(8,128)(2,1)S(1)}, u32[]{:S(2)}, u32[]{:S(2)}) %collective-permute-start.8) | collective-permute-done | bytes 92192 | tf_op jit(solution)/shard_map/ppermute | solution.py:282
  57.4 1.5 %collective-permute-start.9 = (bf16[2,72,640]{2,1,0:T(8,128)(2,1)S(1)}, bf16[2,72,640]{2,1,0:T(8,128)(2,1)S(1)}, u32[]{:S(2)}, u32[]{:S(2)}) collective-permute-start(bf16[2,72,640]{2,1,0:T(8,128)(2,1)S(1)} %pad_maximum_fusion.5), channel_id=1, source_target_pairs={{0,16},{1,3},{2,18},{3,1},{4,20},{5,7},{6,22},{7,5},{8,24},{9,11},... | collective-permute-start | bytes 552968 | tf_op jit(solution)/shard_map/ppermute | solution.py:282
  59.4 1.3 %collective-permute-done.12.refs_3_ = bf16[4,144,896]{2,1,0:T(8,128)(2,1)S(1)} collective-permute-done((bf16[4,144,896]{2,1,0:T(8,128)(2,1)S(1)}, bf16[4,144,896]{2,1,0:T(8,128)(2,1)S(1)}, u32[]{:S(2)}, u32[]{:S(2)}) %collective-permute-start.12) | collective-permute-done | bytes 1032224 | tf_op jit(solution)/shard_map/ppermute | solution.py:282
  60.8 9.3 %temporal_backward.1 = bf16[256,1152]{1,0:T(8,128)(2,1)} custom-call(s32[32]{0:T(128)S(1)} %stack.189.place_ref, bf16[256,1728]{1,0:T(8,128)(2,1)S(1)} %bitcast.62, f32[1,1152]{1,0:T(1,128)S(1)} %add.141.gain_ref, bf16[4,144,896]{2,1,0:T(8,128)(2,1)S(1)} %constant_dynamic-update-slice_fusion.refs_0_, bf16[4,144,896]{2,1,0:T(8,128)(2,1)} %collective-permute-done.11.refs_1_, ...), custom_call_target="tpu_custom_call" | custom-call | flops 3649044480 | bytes 5750784 | tf_op jit(solution)/shard_map/temporal_backward/pallas_call | solution.py:150
  70.2 1.5 %collective-permute-start.13 = (bf16[4,72,640]{2,1,0:T(8,128)(2,1)S(1)}, bf16[4,72,640]{2,1,0:T(8,128)(2,1)S(1)}, u32[]{:S(2)}, u32[]{:S(2)}) collective-permute-start(bf16[4,72,640]{2,1,0:T(8,128)(2,1)S(1)} %pad_maximum_fusion.4), channel_id=1, source_target_pairs={{0,2},{1,17},{2,0},{3,19},{4,6},{5,21},{6,4},{7,23},{8,10},{9,25},... | collective-permute-start | bytes 1105928 | tf_op jit(solution)/shard_map/ppermute | solution.py:282
  71.7 3.8 %all-to-all-start.1 = ((bf16[16,16,1152]{2,1,0:T(8,128)(2,1)}), bf16[16,16,1152]{2,1,0:T(8,128)(2,1)S(1)}, u32[]{:S(2)}, u32[]{:S(2)}) async-start(bf16[16,16,1152]{2,1,0:T(8,128)(2,1)} %bitcast.53), calls=%async_computation.1 | async-start | bytes 1179648 | tf_op jit(solution)/shard_map/all_to_all | solution.py:391
  75.6 2.2 %collective-permute-done.13 = bf16[4,72,640]{2,1,0:T(8,128)(2,1)S(1)} collective-permute-done((bf16[4,72,640]{2,1,0:T(8,128)(2,1)S(1)}, bf16[4,72,640]{2,1,0:T(8,128)(2,1)S(1)}, u32[]{:S(2)}, u32[]{:S(2)}) %collective-permute-start.13) | collective-permute-done | bytes 368672 | tf_op jit(solution)/shard_map/ppermute | solution.py:282
  77.9 2.2 %collective-permute-done.14.refs_1_ = bf16[8,72,640]{2,1,0:T(8,128)(2,1)S(1)} collective-permute-done((bf16[8,72,640]{2,1,0:T(8,128)(2,1)S(1)}, bf16[8,72,640]{2,1,0:T(8,128)(2,1)S(1)}, u32[]{:S(2)}, u32[]{:S(2)}) %collective-permute-start.14) | collective-permute-done | bytes 737312 | tf_op jit(solution)/shard_map/ppermute | solution.py:282
  80.1 2.1 %spatial_prepare.1 = (bf16[4,256,256]{2,1,0:T(8,128)(2,1)S(1)}, bf16[4,256,256]{2,1,0:T(8,128)(2,1)S(1)}, bf16[288,1152]{1,0:T(8,128)(2,1)S(1)}, bf16[288,1152]{...) custom-call(s32[32]{0:T(128)S(1)} %stack.212.place_ref, ...), custom_call_target="tpu_custom_call" | custom-call | flops 268435456 | bytes 2228224 | tf_op jit(solution)/shard_map/spatial_prepare/pallas_call | solution.py:211
  84.6 6.2 %all-to-all-done.1 = bf16[16,16,1152]{2,1,0:T(8,128)(2,1)S(1)} async-done(((bf16[16,16,1152]{2,1,0:T(8,128)(2,1)}), bf16[16,16,1152]{2,1,0:T(8,128)(2,1)S(1)}, u32[]{:S(2)}, u32[]{:S(2)}) %all-to-all-start.1) | async-done | bytes 589856 | tf_op jit(solution)/shard_map/all_to_all | solution.py:391
  90.8 1.1 %copy-done.3 = bf16[256,1152]{1,0:T(8,128)(2,1)S(1)} copy-done((bf16[256,1152]{1,0:T(8,128)(2,1)S(1)}, bf16[256,1152]{1,0:T(8,128)(2,1)}, u32[]{:S(2)}) %copy-start.3) | copy-done | bytes 589848
  92.9 1.0 %copy-done.7 = bf16[8,256,72]{2,1,0:T(8,128)(2,1)S(1)} copy-done((bf16[8,256,72]{2,1,0:T(8,128)(2,1)S(1)}, bf16[8,256,72]{2,1,0:T(8,128)(2,1)}, u32[]{:S(2)}) %copy-start.7) | copy-done | bytes 294936
  94.0 4.2 %spatial_backward.1 = (bf16[256,1152]{1,0:T(8,128)(2,1)}, bf16[3,8,72,256]{3,2,1,0:T(8,128)(2,1)}) custom-call(bf16[8,256,72]{2,1,0:T(8,128)(2,1)S(1)} %copy-done.7, bf16[3,8,72,256]{3,2,1,0:T(8,128)(2,1)S(1)} %bitcast.64, bf16[256,1152]{1,0:T(8,128)(2,1)S(1)} %copy-done.3, bf16[256,1152]{1,0:T(8,128)(2,1)S(1)} %bitcast.65, ...), custom_call_target="tpu_custom_call" | custom-call | flops 1681915904 | bytes 4866048 | tf_op jit(solution)/shard_map/spatial_backward/pallas_call | solution.py:260
  (57 shorter events, 10.7 us)
Async XLA Ops:
  0.6 3.3 %copy-start.10 = (bf16[36,1152]{1,0:T(8,128)(2,1)S(1)}, bf16[36,1152]{1,0:T(8,128)(2,1)}, u32[]{:S(2)}) copy-start(bf16[36,1152]{1,0:T(8,128)(2,1)} %param.13) | copy-start | bytes 248836
  0.6 7.4 %copy-start.9 = (bf16[1,256,576]{1,2,0:T(8,128)(2,1)S(1)}, bf16[1,256,576]{1,2,0:T(8,128)(2,1)}, u32[]{:S(2)}) copy-start(bf16[1,256,576]{1,2,0:T(8,128)(2,1)} %param.9) | copy-start | bytes 884740
  0.7 7.6 %copy-start.8 = (bf16[1,256,1152]{2,1,0:T(8,128)(2,1)S(1)}, bf16[1,256,1152]{2,1,0:T(8,128)(2,1)}, u32[]{:S(2)}) copy-start(bf16[1,256,1152]{2,1,0:T(8,128)(2,1)} %param.8) | copy-start | bytes 1769476
  1.7 1.5 %collective-permute-start = (bf16[72,896]{1,0:T(8,128)(2,1)S(1)}, bf16[72,896]{1,0:T(8,128)(2,1)S(1)}, u32[]{:S(2)}, u32[]{:S(2)}) collective-permute-start(bf16[72,896]{1,0:T(8,128)(2,1)S(1)} %pad_dynamic-slice_fusion), channel_id=1, source_target_pairs={{0,1},{1,0},{2,3},{3,2},{4,5},{5,4},{6,7},{7,6},{8,9},{9,8},{10,11... | collective-permute-start | bytes 387080 | tf_op jit(solution)/shard_map/ppermute | solution.py:282
  3.3 8.6 %collective-permute-start.1 = (bf16[144,896]{1,0:T(8,128)(2,1)S(1)}, bf16[144,896]{1,0:T(8,128)(2,1)S(1)}, u32[]{:S(2)}, u32[]{:S(2)}) collective-permute-start(bf16[144,896]{1,0:T(8,128)(2,1)S(1)} %maximum_select_fusion), channel_id=1, source_target_pairs={{0,0},{1,5},{2,2},{3,7},{4,4},{5,1},{6,6},{7,3},{8,8},{9,13},{10,1... | collective-permute-start | bytes 774152 | tf_op jit(solution)/shard_map/ppermute | solution.py:282
  4.0 9.7 %collective-permute-start.4 = (bf16[36,640]{1,0:T(8,128)(2,1)S(1)}, bf16[36,640]{1,0:T(8,128)(2,1)S(1)}, u32[]{:S(2)}, u32[]{:S(2)}) collective-permute-start(bf16[36,640]{1,0:T(8,128)(2,1)S(1)} %pad_dynamic-slice_fusion.1), channel_id=1, source_target_pairs={{0,1},{1,0},{2,3},{3,2},{4,5},{5,4},{6,7},{7,6},{8,9},{9,8},{10,11... | collective-permute-start | bytes 138248 | tf_op jit(solution)/shard_map/ppermute | solution.py:282
  8.3 5.1 %copy-start.11 = (f32[1152]{0:T(1024)S(1)}, f32[1152]{0:T(1024)}, u32[]{:S(2)}) copy-start(f32[1152]{0:T(1024)} %param.11) | copy-start | bytes 13828
  9.3 14.5 %collective-permute-start.3 = (bf16[144,896]{1,0:T(8,128)(2,1)S(1)}, bf16[144,896]{1,0:T(8,128)(2,1)S(1)}, u32[]{:S(2)}, u32[]{:S(2)}) collective-permute-start(bf16[144,896]{1,0:T(8,128)(2,1)S(1)} %maximum_select_fusion), channel_id=1, source_target_pairs={{0,8},{1,13},{2,10},{3,15},{4,12},{5,9},{6,14},{7,11},{8,0},{9,5},... | collective-permute-start | bytes 774152 | tf_op jit(solution)/shard_map/ppermute | solution.py:282
  11.9 6.3 %collective-permute-start.2 = (bf16[1,144,896]{2,1,0:T(8,128)(2,1)S(1)}, bf16[1,144,896]{2,1,0:T(8,128)(2,1)S(1)}, u32[]{:S(2)}, u32[]{:S(2)}) collective-permute-start(bf16[1,144,896]{2,1,0:T(8,128)(2,1)S(1)} %bitcast.70), channel_id=1, source_target_pairs={{0,16},{1,3},{2,18},{3,1},{4,20},{5,7},{6,22},{7,5},{8,24},{9,11},... | collective-permute-start | bytes 774152 | tf_op jit(solution)/shard_map/ppermute | solution.py:282
  23.8 33.0 %all-to-all-start = ((bf16[16,16,1728]{2,1,0:T(8,128)(2,1)}), bf16[16,16,1728]{2,1,0:T(8,128)(2,1)S(1)}, u32[]{:S(2)}, u32[]{:S(2)}) async-start(bf16[16,16,1728]{2,1,0:T(8,128)(2,1)} %bitcast.45), calls=%async_computation | async-start | bytes 1835008 | tf_op jit(solution)/shard_map/all_to_all | solution.py:371
  28.8 8.4 %collective-permute-start.5 = (bf16[1,144,896]{2,1,0:T(8,128)(2,1)S(1)}, bf16[1,144,896]{2,1,0:T(8,128)(2,1)S(1)}, u32[]{:S(2)}, u32[]{:S(2)}) collective-permute-start(bf16[1,144,896]{2,1,0:T(8,128)(2,1)S(1)} %bitcast.67), channel_id=1, source_target_pairs={{0,16},{1,3},{2,18},{3,1},{4,20},{5,7},{6,22},{7,5},{8,24},{9,11},... | collective-permute-start | bytes 774152 | tf_op jit(solution)/shard_map/ppermute | solution.py:282
  30.4 26.2 %collective-permute-start.10 = (bf16[2,144,896]{2,1,0:T(8,128)(2,1)S(1)}, bf16[2,144,896]{2,1,0:T(8,128)(2,1)S(1)}, u32[]{:S(2)}, u32[]{:S(2)}) collective-permute-start(bf16[2,144,896]{2,1,0:T(8,128)(2,1)S(1)} %pad_maximum_fusion.2), channel_id=1, source_target_pairs={{0,2},{1,17},{2,0},{3,19},{4,6},{5,21},{6,4},{7,23},{8,10},{9,25},... | collective-permute-start | bytes 1548296 | tf_op jit(solution)/shard_map/ppermute | solution.py:282
  37.3 19.4 %collective-permute-start.6 = (bf16[2,144,896]{2,1,0:T(8,128)(2,1)S(1)}, bf16[2,144,896]{2,1,0:T(8,128)(2,1)S(1)}, u32[]{:S(2)}, u32[]{:S(2)}) collective-permute-start(bf16[2,144,896]{2,1,0:T(8,128)(2,1)S(1)} %pad_maximum_fusion.3), channel_id=1, source_target_pairs={{0,2},{1,17},{2,0},{3,19},{4,6},{5,21},{6,4},{7,23},{8,10},{9,25},... | collective-permute-start | bytes 1548296 | tf_op jit(solution)/shard_map/ppermute | solution.py:282
  39.9 3.1 %collective-permute-start.7 = (bf16[72,640]{1,0:T(8,128)(2,1)S(1)}, bf16[72,640]{1,0:T(8,128)(2,1)S(1)}, u32[]{:S(2)}, u32[]{:S(2)}) collective-permute-start(bf16[72,640]{1,0:T(8,128)(2,1)S(1)} %maximum_select_fusion.1), channel_id=1, source_target_pairs={{0,0},{1,5},{2,2},{3,7},{4,4},{5,1},{6,6},{7,3},{8,8},{9,13},{10,1... | collective-permute-start | bytes 276488 | tf_op jit(solution)/shard_map/ppermute | solution.py:282
  40.6 15.9 %collective-permute-start.8 = (bf16[72,640]{1,0:T(8,128)(2,1)S(1)}, bf16[72,640]{1,0:T(8,128)(2,1)S(1)}, u32[]{:S(2)}, u32[]{:S(2)}) collective-permute-start(bf16[72,640]{1,0:T(8,128)(2,1)S(1)} %maximum_select_fusion.1), channel_id=1, source_target_pairs={{0,8},{1,13},{2,10},{3,15},{4,12},{5,9},{6,14},{7,11},{8,0},{9,5},... | collective-permute-start | bytes 276488 | tf_op jit(solution)/shard_map/ppermute | solution.py:282
  56.6 2.8 %collective-permute-start.11 = (bf16[4,144,896]{2,1,0:T(8,128)(2,1)S(1)}, bf16[4,144,896]{2,1,0:T(8,128)(2,1)}, u32[]{:S(2)}, u32[]{:S(2)}) collective-permute-start(bf16[4,144,896]{2,1,0:T(8,128)(2,1)S(1)} %constant_dynamic-update-slice_fusion.refs_0_), channel_id=1, source_target_pairs={{0,1},{1,0},{2,3},{3,2},{4,5},{5,4},{6,7},{7,6},{8,9},{9,8},{10,11... | collective-permute-start | bytes 3096584 | tf_op jit(solution)/shard_map/ppermute | solution.py:282
  56.8 3.9 %collective-permute-start.12 = (bf16[4,144,896]{2,1,0:T(8,128)(2,1)S(1)}, bf16[4,144,896]{2,1,0:T(8,128)(2,1)S(1)}, u32[]{:S(2)}, u32[]{:S(2)}) collective-permute-start(bf16[4,144,896]{2,1,0:T(8,128)(2,1)S(1)} %pad_maximum_fusion.refs_2_), channel_id=1, source_target_pairs={{0,1},{1,0},{2,3},{3,2},{4,5},{5,4},{6,7},{7,6},{8,9},{9,8},{10,11... | collective-permute-start | bytes 3096584 | tf_op jit(solution)/shard_map/ppermute | solution.py:282
  57.4 12.7 %collective-permute-start.9 = (bf16[2,72,640]{2,1,0:T(8,128)(2,1)S(1)}, bf16[2,72,640]{2,1,0:T(8,128)(2,1)S(1)}, u32[]{:S(2)}, u32[]{:S(2)}) collective-permute-start(bf16[2,72,640]{2,1,0:T(8,128)(2,1)S(1)} %pad_maximum_fusion.5), channel_id=1, source_target_pairs={{0,16},{1,3},{2,18},{3,1},{4,20},{5,7},{6,22},{7,5},{8,24},{9,11},... | collective-permute-start | bytes 552968 | tf_op jit(solution)/shard_map/ppermute | solution.py:282
  70.2 7.6 %collective-permute-start.13 = (bf16[4,72,640]{2,1,0:T(8,128)(2,1)S(1)}, bf16[4,72,640]{2,1,0:T(8,128)(2,1)S(1)}, u32[]{:S(2)}, u32[]{:S(2)}) collective-permute-start(bf16[4,72,640]{2,1,0:T(8,128)(2,1)S(1)} %pad_maximum_fusion.4), channel_id=1, source_target_pairs={{0,2},{1,17},{2,0},{3,19},{4,6},{5,21},{6,4},{7,23},{8,10},{9,25},... | collective-permute-start | bytes 1105928 | tf_op jit(solution)/shard_map/ppermute | solution.py:282
  71.7 19.1 %all-to-all-start.1 = ((bf16[16,16,1152]{2,1,0:T(8,128)(2,1)}), bf16[16,16,1152]{2,1,0:T(8,128)(2,1)S(1)}, u32[]{:S(2)}, u32[]{:S(2)}) async-start(bf16[16,16,1152]{2,1,0:T(8,128)(2,1)} %bitcast.53), calls=%async_computation.1 | async-start | bytes 1179648 | tf_op jit(solution)/shard_map/all_to_all | solution.py:391
  75.5 4.6 %copy-start = (bf16[3,1,256,576]{2,3,1,0:T(8,128)(2,1)S(1)}, bf16[3,1,256,576]{2,3,1,0:T(8,128)(2,1)}, u32[]{:S(2)}) copy-start(bf16[3,1,256,576]{2,3,1,0:T(8,128)(2,1)} %param.7) | copy-start | bytes 2654212
  75.5 4.6 %copy-start.1 = (bf16[1,256,1152]{2,1,0:T(8,128)(2,1)S(1)}, bf16[1,256,1152]{2,1,0:T(8,128)(2,1)}, u32[]{:S(2)}) copy-start(bf16[1,256,1152]{2,1,0:T(8,128)(2,1)} %param.10) | copy-start | bytes 1769476
  77.8 2.3 %collective-permute-start.14 = (bf16[8,72,640]{2,1,0:T(8,128)(2,1)S(1)}, bf16[8,72,640]{2,1,0:T(8,128)(2,1)S(1)}, u32[]{:S(2)}, u32[]{:S(2)}) collective-permute-start(bf16[8,72,640]{2,1,0:T(8,128)(2,1)S(1)} %constant_dynamic-update-slice_fusion.2.refs_0_), channel_id=1, source_target_pairs={{0,1},{1,0},{2,3},{3,2},{4,5},{5,4},{6,7},{7,6},{8,9},{9,8},{10,11... | collective-permute-start | bytes 2211848 | tf_op jit(solution)/shard_map/ppermute | solution.py:282
  90.8 1.1 %copy-start.3 = (bf16[256,1152]{1,0:T(8,128)(2,1)S(1)}, bf16[256,1152]{1,0:T(8,128)(2,1)}, u32[]{:S(2)}) copy-start(bf16[256,1152]{1,0:T(8,128)(2,1)} %copy-done.2) | copy-start | bytes 1769476
  (5 other events, 4.5 us)

commit v4 on v3

--- a/solution.py
+++ b/solution.py
@@ -282,6 +282,10 @@
     return lax.ppermute(block, ("clip", "seq"), pairs)
 
 
+def half_of(columns):
+    return -(-columns // (2 * LANES)) * LANES
+
+
 class Gather:
     def __init__(self, clips, devices):
         self.send = functools.partial(moved, clips=clips, devices=devices)
@@ -290,17 +294,22 @@
         self.pairs = devices // 8
 
     def block(self, weights):
-        half = -(-weights.shape[1] // (2 * LANES)) * LANES
-        padded = jnp.pad(weights, ((0, 0), (0, 2 * half - weights.shape[1])))
-        mine = lax.dynamic_slice(padded, (0, half * self.x), (weights.shape[0], half))
-        other = self.send(mine, target=lambda x, y, z, core: (x, y, z, 1 - core))
-        return jnp.where(
-            self.core == 0, jnp.concatenate([mine, other]), jnp.concatenate([other, mine])
+        other = self.send(weights, target=lambda x, y, z, core: (x, y, z, 1 - core))
+        rows = jnp.where(
+            self.core == 0,
+            jnp.concatenate([weights, other]),
+            jnp.concatenate([other, weights]),
         )
-
-    def along(self, block):
+        half = half_of(weights.shape[1])
+        padded = jnp.pad(rows, ((0, 0), (0, 2 * half - weights.shape[1])))
+        return jnp.where(self.x == 0, padded[:, :half], padded[:, half:])
+
+    def along(self, block, late=None):
         return [
-            self.send(block, target=lambda x, y, z, core: (x, y, z ^ (2 * pair + core), core))
+            self.send(
+                block if pair or late is None else late,
+                target=lambda x, y, z, core: (x, y, z ^ (2 * pair + core), core),
+            )
             for pair in range(self.pairs)
         ]
 
@@ -358,19 +367,19 @@
     if clips % 2 == 0 and chips >= 4 and chips & (chips - 1) == 0 and 2 * depth // frames % 16 == 0:
         gather = Gather(clips, frames)
         block = gather.block(temporal_weights)
-        firsts = gather.along(block)
+        late, mixed = tied(block, mixed)
+        firsts = gather.along(block, late)
         rows, half = firsts[0].shape
-        small_block = gather.block(spatial_weights)
         places = [place for pair in range(len(firsts)) for place in gather.places([pair], rows, half)]
-        small_places = gather.places(range(len(firsts)), 1, small_block.shape[1])
+        small_places = gather.places(range(len(firsts)), 1, half_of(depth))
         places, small_places = (jnp.stack(p).astype(jnp.int32) for p in (places, small_places))
         both = [jnp.concatenate(gather.beside(firsts[0][None]))]
-        (both[0], firsts, small_block, places, small_places, gain), mixed = tied(
-            (both[0], firsts, small_block, places, small_places, gain), mixed
+        (both[0], firsts, spatial_weights, places, small_places, gain), mixed = tied(
+            (both[0], firsts, spatial_weights, places, small_places, gain), mixed
         )
         mixed = lax.all_to_all(mixed, "seq", split_axis=0, concat_axis=0, tiled=True)
         both += [jnp.concatenate(gather.beside(first[None])) for first in firsts[1:]]
-        small = jnp.stack(gather.along(small_block))
+        small = jnp.stack(gather.along(gather.block(spatial_weights)))
         four = [gather.across(block) for block in both]
         (four[-1], small), mixed = tied((four[-1], small), mixed)
         pieces = [piece for block in four for piece in (block, gather.swap(block))]

time: 98.7 us -> 97.4 us (0.987)
  waiting for transfers between devices: 42.1 us -> 34.2 us
  starting transfers between devices: 30.9 us -> 37.4 us
    ppermute x15, waiting for transfers between devices: 35.9 us -> 27.1 us  [moved(): return lax.ppermute(block, ('clip', 'seq'), pairs)]
    all_to_all x1, starting transfers between devices: 4.98 us -> 11.2 us  [shards(): lax.all_to_all(mixed, 'seq', split_axis=0, concat_axis=0, tiled=True)]
    dynamic_slice x2 -> x0, local copies, waits for them, and re-layouts: 1.04 us -> none  [block(): lax.dynamic_slice(padded, (0, half * self.x), (weights.shape[0], half))]
  transfers between devices with their start and end apart: 17 -> 17, of which waited for: 10 -> 8; matrix products, arithmetic and copies ran while one was open for 2% -> 3% of each run, Pallas kernels for 12% -> 12%
where the time goes in v4:
time: 97.4 us; the launch traced here: 96.9 us
  starting transfers between devices  37.4 us (38%)
  waiting for transfers between devices  34.2 us (35%)
  Pallas kernels  15.6 us (16%)
  local copies, waits for them, and re-layouts  7.19 us (7%)
  other arithmetic  1.56 us (2%)
    ppermute x15, waiting for transfers between devices, moved(): return lax.ppermute(block, ('clip', 'seq'), pairs)  27.1 us
    ppermute x15, starting transfers between devices, moved(): return lax.ppermute(block, ('clip', 'seq'), pairs)  22.3 us
    all_to_all x1, starting transfers between devices, shards(): lax.all_to_all(mixed, 'seq', split_axis=0, concat_axis=0, tiled=True)  11.2 us
    pallas_call x1, Pallas kernels, temporal(): pl.pallas_call(functools.partial(temporal_kernel, patches, len(pieces)),...  9.32 us
    all_to_all x1, waiting for transfers between devices, shards(): lax.all_to_all(branch.reshape(frames, patches, depth), 'seq', split_axis=...  7.13 us
    unnamed x28, local copies, waits for them, and re-layouts  6.85 us
    pallas_call x1, Pallas kernels, spatial(): pl.pallas_call(spatial_kernel, out_shape=(jax.ShapeDtypeStruct((tokens, d...  4.2 us
    all_to_all x1, starting transfers between devices, shards(): lax.all_to_all(branch.reshape(frames, patches, depth), 'seq', split_axis=...  3.91 us
  transfers between devices with their start and end apart: 17, of which 8 were waited for; matrix products, arithmetic and copies ran while one was open for 3% of the time, Pallas kernels for 12%

profile of v4, /device:TPU:0, one launch (start us, length us, event | category | flops | bytes accessed | tf_op | source)
XLA Modules:
  0.0 96.9 jit_solution(10093642557194281026)
XLA Ops:
  1.2 1.2 %copy.9 = bf16[1,256,576]{2,1,0:T(8,128)(2,1)S(1)} copy(bf16[1,256,576]{1,2,0:T(8,128)(2,1)} %param.9) | data formatting | bytes 589824 | tf_op args[2]
  4.2 2.7 %collective-permute-start.2 = (bf16[1,144,896]{2,1,0:T(8,128)(2,1)S(1)}, bf16[1,144,896]{2,1,0:T(8,128)(2,1)S(1)}, u32[]{:S(2)}, u32[]{:S(2)}) collective-permute-start(bf16[1,144,896]{2,1,0:T(8,128)(2,1)S(1)} %bitcast.70), channel_id=1, source_target_pairs={{0,16},{1,3},{2,18},{3,1},{4,20},{5,7},{6,22},{7,5},{8,24},{9,11},... | collective-permute-start | bytes 774152 | tf_op jit(solution)/shard_map/ppermute | solution.py:282
  6.9 2.6 %collective-permute-start.3 = (bf16[144,896]{1,0:T(8,128)(2,1)S(1)}, bf16[144,896]{1,0:T(8,128)(2,1)S(1)}, u32[]{:S(2)}, u32[]{:S(2)}) collective-permute-start(bf16[144,896]{1,0:T(8,128)(2,1)S(1)} %fusion), channel_id=1, source_target_pairs={{0,8},{1,13},{2,10},{3,15},{4,12},{5,9},{6,14},{7,11},{8,0},{9,5},... | collective-permute-start | bytes 774152 | tf_op jit(solution)/shard_map/ppermute | solution.py:282
  9.7 1.5 %collective-permute-done.2 = bf16[1,144,896]{2,1,0:T(8,128)(2,1)S(1)} collective-permute-done((bf16[1,144,896]{2,1,0:T(8,128)(2,1)S(1)}, bf16[1,144,896]{2,1,0:T(8,128)(2,1)S(1)}, u32[]{:S(2)}, u32[]{:S(2)}) %collective-permute-start.2) | collective-permute-done | bytes 258080 | tf_op jit(solution)/shard_map/ppermute | solution.py:282
  11.3 4.7 %collective-permute-done.3 = bf16[144,896]{1,0:T(8,128)(2,1)S(1)} collective-permute-done((bf16[144,896]{1,0:T(8,128)(2,1)S(1)}, bf16[144,896]{1,0:T(8,128)(2,1)S(1)}, u32[]{:S(2)}, u32[]{:S(2)}) %collective-permute-start.3) | collective-permute-done | bytes 258080 | tf_op jit(solution)/shard_map/ppermute | solution.py:282
  16.0 11.2 %all-to-all-start = ((bf16[16,16,1728]{2,1,0:T(8,128)(2,1)}), bf16[16,16,1728]{2,1,0:T(8,128)(2,1)S(1)}, u32[]{:S(2)}, u32[]{:S(2)}) async-start(bf16[16,16,1728]{2,1,0:T(8,128)(2,1)} %bitcast), calls=%async_computation | async-start | bytes 1835008 | tf_op jit(solution)/shard_map/all_to_all | solution.py:380
  27.6 2.1 %collective-permute-start.4 = (bf16[1,144,896]{2,1,0:T(8,128)(2,1)S(1)}, bf16[1,144,896]{2,1,0:T(8,128)(2,1)S(1)}, u32[]{:S(2)}, u32[]{:S(2)}) collective-permute-start(bf16[1,144,896]{2,1,0:T(8,128)(2,1)S(1)} %bitcast.67), channel_id=1, source_target_pairs={{0,16},{1,3},{2,18},{3,1},{4,20},{5,7},{6,22},{7,5},{8,24},{9,11},... | collective-permute-start | bytes 774152 | tf_op jit(solution)/shard_map/ppermute | solution.py:282
  29.8 1.7 %collective-permute-start.10 = (bf16[2,144,896]{2,1,0:T(8,128)(2,1)S(1)}, bf16[2,144,896]{2,1,0:T(8,128)(2,1)S(1)}, u32[]{:S(2)}, u32[]{:S(2)}) collective-permute-start(bf16[2,144,896]{2,1,0:T(8,128)(2,1)S(1)} %pad_maximum_fusion.2), channel_id=1, source_target_pairs={{0,2},{1,17},{2,0},{3,19},{4,6},{5,21},{6,4},{7,23},{8,10},{9,25},... | collective-permute-start | bytes 1548296 | tf_op jit(solution)/shard_map/ppermute | solution.py:282
  31.5 4.3 %collective-permute-done.4 = bf16[1,144,896]{2,1,0:T(8,128)(2,1)S(1)} collective-permute-done((bf16[1,144,896]{2,1,0:T(8,128)(2,1)S(1)}, bf16[1,144,896]{2,1,0:T(8,128)(2,1)S(1)}, u32[]{:S(2)}, u32[]{:S(2)}) %collective-permute-start.4) | collective-permute-done | bytes 258080 | tf_op jit(solution)/shard_map/ppermute | solution.py:282
  35.8 2.8 %collective-permute-start.5 = (bf16[2,144,896]{2,1,0:T(8,128)(2,1)S(1)}, bf16[2,144,896]{2,1,0:T(8,128)(2,1)S(1)}, u32[]{:S(2)}, u32[]{:S(2)}) collective-permute-start(bf16[2,144,896]{2,1,0:T(8,128)(2,1)S(1)} %pad_maximum_fusion.3), channel_id=1, source_target_pairs={{0,2},{1,17},{2,0},{3,19},{4,6},{5,21},{6,4},{7,23},{8,10},{9,25},... | collective-permute-start | bytes 1548296 | tf_op jit(solution)/shard_map/ppermute | solution.py:282
  39.3 2.4 %collective-permute-start.8 = (bf16[72,640]{1,0:T(8,128)(2,1)S(1)}, bf16[72,640]{1,0:T(8,128)(2,1)S(1)}, u32[]{:S(2)}, u32[]{:S(2)}) collective-permute-start(bf16[72,640]{1,0:T(8,128)(2,1)S(1)} %fusion.1), channel_id=1, source_target_pairs={{0,8},{1,13},{2,10},{3,15},{4,12},{5,9},{6,14},{7,11},{8,0},{9,5},... | collective-permute-start | bytes 276488 | tf_op jit(solution)/shard_map/ppermute | solution.py:282
  41.8 12.4 %collective-permute-done.8 = bf16[72,640]{1,0:T(8,128)(2,1)S(1)} collective-permute-done((bf16[72,640]{1,0:T(8,128)(2,1)S(1)}, bf16[72,640]{1,0:T(8,128)(2,1)S(1)}, u32[]{:S(2)}, u32[]{:S(2)}) %collective-permute-start.8) | collective-permute-done | bytes 92192 | tf_op jit(solution)/shard_map/ppermute | solution.py:282
  55.1 2.8 %collective-permute-start.9 = (bf16[2,72,640]{2,1,0:T(8,128)(2,1)S(1)}, bf16[2,72,640]{2,1,0:T(8,128)(2,1)S(1)}, u32[]{:S(2)}, u32[]{:S(2)}) collective-permute-start(bf16[2,72,640]{2,1,0:T(8,128)(2,1)S(1)} %pad_maximum_fusion.5), channel_id=1, source_target_pairs={{0,16},{1,3},{2,18},{3,1},{4,20},{5,7},{6,22},{7,5},{8,24},{9,11},... | collective-permute-start | bytes 552968 | tf_op jit(solution)/shard_map/ppermute | solution.py:282
  58.5 9.3 %temporal_backward.1 = bf16[256,1152]{1,0:T(8,128)(2,1)} custom-call(s32[32]{0:T(128)S(1)} %stack.189.place_ref, bf16[256,1728]{1,0:T(8,128)(2,1)S(1)} %bitcast.62, f32[1,1152]{1,0:T(1,128)S(1)} %add.133.gain_ref, bf16[4,144,896]{2,1,0:T(8,128)(2,1)S(1)} %constant_dynamic-update-slice_fusion.refs_0_, bf16[4,144,896]{2,1,0:T(8,128)(2,1)} %collective-permute-done.11.refs_1_, ...), custom_call_target="tpu_custom_call" | custom-call | flops 3649044480 | bytes 5750784 | tf_op jit(solution)/shard_map/temporal_backward/pallas_call | solution.py:150
  67.9 2.2 %collective-permute-start.13 = (bf16[4,72,640]{2,1,0:T(8,128)(2,1)S(1)}, bf16[4,72,640]{2,1,0:T(8,128)(2,1)S(1)}, u32[]{:S(2)}, u32[]{:S(2)}) collective-permute-start(bf16[4,72,640]{2,1,0:T(8,128)(2,1)S(1)} %pad_maximum_fusion.4), channel_id=1, source_target_pairs={{0,2},{1,17},{2,0},{3,19},{4,6},{5,21},{6,4},{7,23},{8,10},{9,25},... | collective-permute-start | bytes 1105928 | tf_op jit(solution)/shard_map/ppermute | solution.py:282
  70.0 3.9 %all-to-all-start.1 = ((bf16[16,16,1152]{2,1,0:T(8,128)(2,1)}), bf16[16,16,1152]{2,1,0:T(8,128)(2,1)S(1)}, u32[]{:S(2)}, u32[]{:S(2)}) async-start(bf16[16,16,1152]{2,1,0:T(8,128)(2,1)} %bitcast.53), calls=%async_computation.1 | async-start | bytes 1179648 | tf_op jit(solution)/shard_map/all_to_all | solution.py:400
  74.0 1.5 %collective-permute-done.13 = bf16[4,72,640]{2,1,0:T(8,128)(2,1)S(1)} collective-permute-done((bf16[4,72,640]{2,1,0:T(8,128)(2,1)S(1)}, bf16[4,72,640]{2,1,0:T(8,128)(2,1)S(1)}, u32[]{:S(2)}, u32[]{:S(2)}) %collective-permute-start.13) | collective-permute-done | bytes 368672 | tf_op jit(solution)/shard_map/ppermute | solution.py:282
  75.8 2.1 %collective-permute-done.14.refs_1_ = bf16[8,72,640]{2,1,0:T(8,128)(2,1)S(1)} collective-permute-done((bf16[8,72,640]{2,1,0:T(8,128)(2,1)S(1)}, bf16[8,72,640]{2,1,0:T(8,128)(2,1)S(1)}, u32[]{:S(2)}, u32[]{:S(2)}) %collective-permute-start.14) | collective-permute-done | bytes 737312 | tf_op jit(solution)/shard_map/ppermute | solution.py:282
  77.9 2.1 %spatial_prepare.1 = (bf16[4,256,256]{2,1,0:T(8,128)(2,1)S(1)}, bf16[4,256,256]{2,1,0:T(8,128)(2,1)S(1)}, bf16[288,1152]{1,0:T(8,128)(2,1)S(1)}, bf16[288,1152]{...) custom-call(s32[32]{0:T(128)S(1)} %stack.212.place_ref, ...), custom_call_target="tpu_custom_call" | custom-call | flops 268435456 | bytes 2228224 | tf_op jit(solution)/shard_map/spatial_prepare/pallas_call | solution.py:211
  82.4 7.1 %all-to-all-done.1 = bf16[16,16,1152]{2,1,0:T(8,128)(2,1)S(1)} async-done(((bf16[16,16,1152]{2,1,0:T(8,128)(2,1)}), bf16[16,16,1152]{2,1,0:T(8,128)(2,1)S(1)}, u32[]{:S(2)}, u32[]{:S(2)}) %all-to-all-start.1) | async-done | bytes 589856 | tf_op jit(solution)/shard_map/all_to_all | solution.py:400
  89.5 1.1 %copy-done.3 = bf16[256,1152]{1,0:T(8,128)(2,1)S(1)} copy-done((bf16[256,1152]{1,0:T(8,128)(2,1)S(1)}, bf16[256,1152]{1,0:T(8,128)(2,1)}, u32[]{:S(2)}) %copy-start.3) | copy-done | bytes 589848
  90.6 1.0 %copy-done.5 = bf16[4,256,256]{2,1,0:T(8,128)(2,1)S(1)} copy-done((bf16[4,256,256]{2,1,0:T(8,128)(2,1)S(1)}, bf16[4,256,256]{2,1,0:T(8,128)(2,1)}, u32[]{:S(2)}) %copy-start.5) | copy-done | bytes 524312
  91.6 1.0 %copy-done.7 = bf16[8,256,72]{2,1,0:T(8,128)(2,1)S(1)} copy-done((bf16[8,256,72]{2,1,0:T(8,128)(2,1)S(1)}, bf16[8,256,72]{2,1,0:T(8,128)(2,1)}, u32[]{:S(2)}) %copy-start.7) | copy-done | bytes 294936
  92.7 4.2 %spatial_backward.1 = (bf16[256,1152]{1,0:T(8,128)(2,1)}, bf16[3,8,72,256]{3,2,1,0:T(8,128)(2,1)}) custom-call(bf16[8,256,72]{2,1,0:T(8,128)(2,1)S(1)} %copy-done.7, bf16[3,8,72,256]{3,2,1,0:T(8,128)(2,1)S(1)} %bitcast.64, bf16[256,1152]{1,0:T(8,128)(2,1)S(1)} %copy-done.3, bf16[256,1152]{1,0:T(8,128)(2,1)S(1)} %bitcast.65, ...), custom_call_target="tpu_custom_call" | custom-call | flops 1681915904 | bytes 4866048 | tf_op jit(solution)/shard_map/spatial_backward/pallas_call | solution.py:260
  (57 shorter events, 8.3 us)
Async XLA Ops:
  0.6 1.7 %copy-start.8 = (bf16[1,256,1152]{2,1,0:T(8,128)(2,1)S(1)}, bf16[1,256,1152]{2,1,0:T(8,128)(2,1)}, u32[]{:S(2)}) copy-start(bf16[1,256,1152]{2,1,0:T(8,128)(2,1)} %param.8) | copy-start | bytes 1769476
  0.6 2.7 %collective-permute-start = (bf16[72,1728]{1,0:T(8,128)(2,1)}, bf16[72,1728]{1,0:T(8,128)(2,1)S(1)}, u32[]{:S(2)}, u32[]{:S(2)}) collective-permute-start(bf16[72,1728]{1,0:T(8,128)(2,1)} %param.12), channel_id=1, source_target_pairs={{0,1},{1,0},{2,3},{3,2},{4,5},{5,4},{6,7},{7,6},{8,9},{9,8},{10,11... | collective-permute-start | bytes 746504 | tf_op jit(solution)/shard_map/ppermute | solution.py:282
  3.3 6.1 %copy-start.11 = (f32[1152]{0:T(1024)S(1)}, f32[1152]{0:T(1024)}, u32[]{:S(2)}) copy-start(f32[1152]{0:T(1024)} %param.11) | copy-start | bytes 13828
  3.5 0.7 collective-permute-start.1
  4.2 7.0 %collective-permute-start.2 = (bf16[1,144,896]{2,1,0:T(8,128)(2,1)S(1)}, bf16[1,144,896]{2,1,0:T(8,128)(2,1)S(1)}, u32[]{:S(2)}, u32[]{:S(2)}) collective-permute-start(bf16[1,144,896]{2,1,0:T(8,128)(2,1)S(1)} %bitcast.70), channel_id=1, source_target_pairs={{0,16},{1,3},{2,18},{3,1},{4,20},{5,7},{6,22},{7,5},{8,24},{9,11},... | collective-permute-start | bytes 774152 | tf_op jit(solution)/shard_map/ppermute | solution.py:282
  6.9 9.1 %collective-permute-start.3 = (bf16[144,896]{1,0:T(8,128)(2,1)S(1)}, bf16[144,896]{1,0:T(8,128)(2,1)S(1)}, u32[]{:S(2)}, u32[]{:S(2)}) collective-permute-start(bf16[144,896]{1,0:T(8,128)(2,1)S(1)} %fusion), channel_id=1, source_target_pairs={{0,8},{1,13},{2,10},{3,15},{4,12},{5,9},{6,14},{7,11},{8,0},{9,5},... | collective-permute-start | bytes 774152 | tf_op jit(solution)/shard_map/ppermute | solution.py:282
  11.2 15.9 %copy-start.10 = (bf16[36,1152]{1,0:T(8,128)(2,1)S(1)}, bf16[36,1152]{1,0:T(8,128)(2,1)}, u32[]{:S(2)}) copy-start(bf16[36,1152]{1,0:T(8,128)(2,1)} %param.13) | copy-start | bytes 248836
  16.0 38.6 %all-to-all-start = ((bf16[16,16,1728]{2,1,0:T(8,128)(2,1)}), bf16[16,16,1728]{2,1,0:T(8,128)(2,1)S(1)}, u32[]{:S(2)}, u32[]{:S(2)}) async-start(bf16[16,16,1728]{2,1,0:T(8,128)(2,1)} %bitcast), calls=%async_computation | async-start | bytes 1835008 | tf_op jit(solution)/shard_map/all_to_all | solution.py:380
  27.2 4.3 %collective-permute-start.6 = (bf16[36,1152]{1,0:T(8,128)(2,1)S(1)}, bf16[36,1152]{1,0:T(8,128)(2,1)S(1)}, u32[]{:S(2)}, u32[]{:S(2)}) collective-permute-start(bf16[36,1152]{1,0:T(8,128)(2,1)S(1)} %copy-done.10), channel_id=1, source_target_pairs={{0,1},{1,0},{2,3},{3,2},{4,5},{5,4},{6,7},{7,6},{8,9},{9,8},{10,11... | collective-permute-start | bytes 248840 | tf_op jit(solution)/shard_map/ppermute | solution.py:282
  27.6 8.1 %collective-permute-start.4 = (bf16[1,144,896]{2,1,0:T(8,128)(2,1)S(1)}, bf16[1,144,896]{2,1,0:T(8,128)(2,1)S(1)}, u32[]{:S(2)}, u32[]{:S(2)}) collective-permute-start(bf16[1,144,896]{2,1,0:T(8,128)(2,1)S(1)} %bitcast.67), channel_id=1, source_target_pairs={{0,16},{1,3},{2,18},{3,1},{4,20},{5,7},{6,22},{7,5},{8,24},{9,11},... | collective-permute-start | bytes 774152 | tf_op jit(solution)/shard_map/ppermute | solution.py:282
  29.8 24.5 %collective-permute-start.10 = (bf16[2,144,896]{2,1,0:T(8,128)(2,1)S(1)}, bf16[2,144,896]{2,1,0:T(8,128)(2,1)S(1)}, u32[]{:S(2)}, u32[]{:S(2)}) collective-permute-start(bf16[2,144,896]{2,1,0:T(8,128)(2,1)S(1)} %pad_maximum_fusion.2), channel_id=1, source_target_pairs={{0,2},{1,17},{2,0},{3,19},{4,6},{5,21},{6,4},{7,23},{8,10},{9,25},... | collective-permute-start | bytes 1548296 | tf_op jit(solution)/shard_map/ppermute | solution.py:282
  35.8 18.6 %collective-permute-start.5 = (bf16[2,144,896]{2,1,0:T(8,128)(2,1)S(1)}, bf16[2,144,896]{2,1,0:T(8,128)(2,1)S(1)}, u32[]{:S(2)}, u32[]{:S(2)}) collective-permute-start(bf16[2,144,896]{2,1,0:T(8,128)(2,1)S(1)} %pad_maximum_fusion.3), channel_id=1, source_target_pairs={{0,2},{1,17},{2,0},{3,19},{4,6},{5,21},{6,4},{7,23},{8,10},{9,25},... | collective-permute-start | bytes 1548296 | tf_op jit(solution)/shard_map/ppermute | solution.py:282
  38.6 3.2 %collective-permute-start.7 = (bf16[72,640]{1,0:T(8,128)(2,1)S(1)}, bf16[72,640]{1,0:T(8,128)(2,1)S(1)}, u32[]{:S(2)}, u32[]{:S(2)}) collective-permute-start(bf16[72,640]{1,0:T(8,128)(2,1)S(1)} %fusion.1), channel_id=1, source_target_pairs={{0,0},{1,5},{2,2},{3,7},{4,4},{5,1},{6,6},{7,3},{8,8},{9,13},{10,1... | collective-permute-start | bytes 276488 | tf_op jit(solution)/shard_map/ppermute | solution.py:282
  39.3 14.9 %collective-permute-start.8 = (bf16[72,640]{1,0:T(8,128)(2,1)S(1)}, bf16[72,640]{1,0:T(8,128)(2,1)S(1)}, u32[]{:S(2)}, u32[]{:S(2)}) collective-permute-start(bf16[72,640]{1,0:T(8,128)(2,1)S(1)} %fusion.1), channel_id=1, source_target_pairs={{0,8},{1,13},{2,10},{3,15},{4,12},{5,9},{6,14},{7,11},{8,0},{9,5},... | collective-permute-start | bytes 276488 | tf_op jit(solution)/shard_map/ppermute | solution.py:282
  54.3 3.5 %collective-permute-start.11 = (bf16[4,144,896]{2,1,0:T(8,128)(2,1)S(1)}, bf16[4,144,896]{2,1,0:T(8,128)(2,1)}, u32[]{:S(2)}, u32[]{:S(2)}) collective-permute-start(bf16[4,144,896]{2,1,0:T(8,128)(2,1)S(1)} %constant_dynamic-update-slice_fusion.refs_0_), channel_id=1, source_target_pairs={{0,1},{1,0},{2,3},{3,2},{4,5},{5,4},{6,7},{7,6},{8,9},{9,8},{10,11... | collective-permute-start | bytes 3096584 | tf_op jit(solution)/shard_map/ppermute | solution.py:282
  54.5 3.9 %collective-permute-start.12 = (bf16[4,144,896]{2,1,0:T(8,128)(2,1)S(1)}, bf16[4,144,896]{2,1,0:T(8,128)(2,1)S(1)}, u32[]{:S(2)}, u32[]{:S(2)}) collective-permute-start(bf16[4,144,896]{2,1,0:T(8,128)(2,1)S(1)} %pad_maximum_fusion.refs_2_), channel_id=1, source_target_pairs={{0,1},{1,0},{2,3},{3,2},{4,5},{5,4},{6,7},{7,6},{8,9},{9,8},{10,11... | collective-permute-start | bytes 3096584 | tf_op jit(solution)/shard_map/ppermute | solution.py:282
  55.1 12.7 %collective-permute-start.9 = (bf16[2,72,640]{2,1,0:T(8,128)(2,1)S(1)}, bf16[2,72,640]{2,1,0:T(8,128)(2,1)S(1)}, u32[]{:S(2)}, u32[]{:S(2)}) collective-permute-start(bf16[2,72,640]{2,1,0:T(8,128)(2,1)S(1)} %pad_maximum_fusion.5), channel_id=1, source_target_pairs={{0,16},{1,3},{2,18},{3,1},{4,20},{5,7},{6,22},{7,5},{8,24},{9,11},... | collective-permute-start | bytes 552968 | tf_op jit(solution)/shard_map/ppermute | solution.py:282
  67.9 7.6 %collective-permute-start.13 = (bf16[4,72,640]{2,1,0:T(8,128)(2,1)S(1)}, bf16[4,72,640]{2,1,0:T(8,128)(2,1)S(1)}, u32[]{:S(2)}, u32[]{:S(2)}) collective-permute-start(bf16[4,72,640]{2,1,0:T(8,128)(2,1)S(1)} %pad_maximum_fusion.4), channel_id=1, source_target_pairs={{0,2},{1,17},{2,0},{3,19},{4,6},{5,21},{6,4},{7,23},{8,10},{9,25},... | collective-permute-start | bytes 1105928 | tf_op jit(solution)/shard_map/ppermute | solution.py:282
  70.0 19.5 %all-to-all-start.1 = ((bf16[16,16,1152]{2,1,0:T(8,128)(2,1)}), bf16[16,16,1152]{2,1,0:T(8,128)(2,1)S(1)}, u32[]{:S(2)}, u32[]{:S(2)}) async-start(bf16[16,16,1152]{2,1,0:T(8,128)(2,1)} %bitcast.53), calls=%async_computation.1 | async-start | bytes 1179648 | tf_op jit(solution)/shard_map/all_to_all | solution.py:400
  74.0 3.9 %copy-start = (bf16[3,1,256,576]{2,3,1,0:T(8,128)(2,1)S(1)}, bf16[3,1,256,576]{2,3,1,0:T(8,128)(2,1)}, u32[]{:S(2)}) copy-start(bf16[3,1,256,576]{2,3,1,0:T(8,128)(2,1)} %param.7) | copy-start | bytes 2654212
  74.0 3.9 %copy-start.1 = (bf16[1,256,1152]{2,1,0:T(8,128)(2,1)S(1)}, bf16[1,256,1152]{2,1,0:T(8,128)(2,1)}, u32[]{:S(2)}) copy-start(bf16[1,256,1152]{2,1,0:T(8,128)(2,1)} %param.10) | copy-start | bytes 1769476
  75.6 2.3 %collective-permute-start.14 = (bf16[8,72,640]{2,1,0:T(8,128)(2,1)S(1)}, bf16[8,72,640]{2,1,0:T(8,128)(2,1)S(1)}, u32[]{:S(2)}, u32[]{:S(2)}) collective-permute-start(bf16[8,72,640]{2,1,0:T(8,128)(2,1)S(1)} %constant_dynamic-update-slice_fusion.2.refs_0_), channel_id=1, source_target_pairs={{0,1},{1,0},{2,3},{3,2},{4,5},{5,4},{6,7},{7,6},{8,9},{9,8},{10,11... | collective-permute-start | bytes 2211848 | tf_op jit(solution)/shard_map/ppermute | solution.py:282
  89.5 1.1 %copy-start.3 = (bf16[256,1152]{1,0:T(8,128)(2,1)S(1)}, bf16[256,1152]{1,0:T(8,128)(2,1)}, u32[]{:S(2)}) copy-start(bf16[256,1152]{1,0:T(8,128)(2,1)} %copy-done.2) | copy-start | bytes 1769476
  90.6 1.0 %copy-start.5 = (bf16[4,256,256]{2,1,0:T(8,128)(2,1)S(1)}, bf16[4,256,256]{2,1,0:T(8,128)(2,1)}, u32[]{:S(2)}) copy-start(bf16[4,256,256]{2,1,0:T(8,128)(2,1)} %copy-done.4) | copy-start | bytes 1572868
  (5 other events, 4.5 us)

commit v5 on v4

--- a/solution.py
+++ b/solution.py
@@ -173,10 +173,10 @@
     )(places, mixed, gain, *pieces)
 
 
-def prepare_kernel(count, place_ref, saved_ref, stream_ref, *refs):
+def prepare_kernel(count, place_ref, stream_ref, *refs):
     pieces, refs = refs[:count], refs[count:]
-    attention_refs, weights_refs = refs[:PARTS], refs[PARTS : 2 * PARTS]
-    values_ref, held_stream_ref, held_ref, sems = refs[2 * PARTS :]
+    weights_refs = refs[:PARTS]
+    held_stream_ref, held_ref, sems = refs[PARTS:]
     copies = []
     for piece in pieces:
         for slot in range(piece.shape[0]):
@@ -189,11 +189,6 @@
             copies.append(pltpu.make_async_copy(piece.at[slot], target, sems.at[number]))
             copies[-1].start()
     held_stream_ref[...] = stream_ref[...]
-    for head in range(HEADS):
-        scores_t = dot_tn(saved_ref[1, head], saved_ref[0, head])
-        part = attention_refs[head * PARTS // HEADS]
-        part[head % (HEADS // PARTS)] = soft(scores_t, 1.0 / math.sqrt(HD)).astype(part.dtype)
-        values_ref[head] = saved_ref[2, head].astype(jnp.float32).T.astype(values_ref.dtype)
     for copy in copies:
         copy.wait()
     blocks = [held_ref[chip].astype(jnp.float32) for chip in range(held_ref.shape[0])]
@@ -203,39 +198,38 @@
         part[...] = joined[index * rows : (index + 1) * rows, :depth].astype(part.dtype)
 
 
-def prepare(saved, stream, pieces, places, width):
+def prepare(stream, pieces, places, width):
     tokens, depth = stream.shape
     rows = pieces[0].shape[1]
     held = max(depth, pieces[0].shape[2] * (1 if len(pieces) == 1 else 2))
     count = sum(piece.shape[0] for piece in pieces)
     return pl.pallas_call(
         functools.partial(prepare_kernel, len(pieces)),
-        out_shape=(jax.ShapeDtypeStruct((HEADS // PARTS, tokens, tokens), jnp.bfloat16),) * PARTS
-        + (jax.ShapeDtypeStruct((width // PARTS, depth), jnp.bfloat16),) * PARTS
-        + (
-            jax.ShapeDtypeStruct((HEADS, tokens, HD), jnp.bfloat16),
-            jax.ShapeDtypeStruct((tokens, depth), jnp.bfloat16),
-        ),
+        out_shape=(jax.ShapeDtypeStruct((width // PARTS, depth), jnp.bfloat16),) * PARTS
+        + (jax.ShapeDtypeStruct((tokens, depth), jnp.bfloat16),),
         in_specs=[pl.BlockSpec(memory_space=pltpu.SMEM)]
-        + [pl.BlockSpec(memory_space=pltpu.VMEM)] * 2
+        + [pl.BlockSpec(memory_space=pltpu.VMEM)]
         + [pl.BlockSpec(memory_space=pl.ANY)] * len(pieces),
-        out_specs=(pl.BlockSpec(memory_space=pltpu.VMEM),) * (2 * PARTS + 2),
+        out_specs=(pl.BlockSpec(memory_space=pltpu.VMEM),) * (PARTS + 1),
         scratch_shapes=[
             pltpu.VMEM((width // rows, rows, held), jnp.bfloat16),
             pltpu.SemaphoreType.DMA((count,)),
         ],
         compiler_params=pltpu.CompilerParams(vmem_limit_bytes=VMEM_LIMIT),
         cost_estimate=pl.CostEstimate(
-            flops=2 * HEADS * tokens * tokens * 2 * LANES,
-            bytes_accessed=2 * (4 * HEADS * tokens * HD + HEADS * tokens * tokens),
-            transcendentals=HEADS * tokens * tokens,
+            flops=0, bytes_accessed=4 * depth * (tokens + width), transcendentals=0
         ),
         name="spatial_prepare",
-    )(places, saved, stream, *pieces)
-
-
-def spatial_kernel(values_ref, saved_ref, stream_ref, branch_ref, *refs):
-    attention_refs, w_refs, (hidden_ref, out_ref) = refs[:PARTS], refs[PARTS:-2], refs[-2:]
+    )(places, stream, *pieces)
+
+
+def attention_of(saved_ref, head):
+    scores_t = dot_tn(saved_ref[1, head], saved_ref[0, head])
+    return soft(scores_t, 1.0 / math.sqrt(HD)).astype(jnp.bfloat16)
+
+
+def spatial_kernel(saved_ref, stream_ref, branch_ref, *refs):
+    w_refs, (hidden_ref, out_ref) = refs[:-2], refs[-2:]
     scale = 1.0 / math.sqrt(HD)
     hidden_grad = (
         stream_ref[...].astype(jnp.float32) + branch_ref[...].astype(jnp.float32)
@@ -244,9 +238,9 @@
     grad_all = jnp.concatenate([dot_nt(w_ref[...], hidden_grad) for w_ref in w_refs], axis=0)
     for head in range(HEADS):
         grad_o = grad_all[head * HD : (head + 1) * HD].astype(jnp.bfloat16)
-        rounded_t = attention_refs[head * PARTS // HEADS][head % (HEADS // PARTS)]
+        rounded_t = attention_of(saved_ref, head)
         wide = rounded_t.astype(jnp.float32)
-        spread_t = dot_nn(values_ref[head], grad_o)
+        spread_t = dot_tn(saved_ref[2, head], grad_o)
         delta = jnp.sum(wide * spread_t, axis=0, keepdims=True)
         dscore_t = (wide * (spread_t - delta)).astype(jnp.bfloat16)
         out_ref[0, head] = (dot_nn(saved_ref[1, head], dscore_t) * scale).astype(out_ref.dtype)
@@ -254,7 +248,7 @@
         out_ref[2, head] = dot_nt(grad_o, rounded_t).astype(out_ref.dtype)
 
 
-def spatial(attention_t, values, saved, stream, branch, weights):
+def spatial(saved, stream, branch, weights):
     tokens, depth = stream.shape
     width = HEADS * HD
     return pl.pallas_call(
@@ -267,10 +261,10 @@
         cost_estimate=pl.CostEstimate(
             flops=2 * tokens * depth * width + 10 * HEADS * tokens * tokens * 2 * LANES,
             bytes_accessed=2 * (3 * tokens * depth + depth * width + 6 * tokens * width),
-            transcendentals=0,
+            transcendentals=HEADS * tokens * tokens,
         ),
         name="spatial_backward",
-    )(values, saved, stream, branch, *attention_t, *weights)
+    )(saved, stream, branch, *weights)
 
 
 def moved(block, clips, devices, target):
@@ -394,14 +388,14 @@
         small, branch = tied(small, branch)
         small = gather.across(jnp.concatenate(small))
         small_pieces = [small, gather.swap(small)]
-    *parts, values, stream = prepare(
-        saved, stream_grad.reshape(tokens, depth), small_pieces, small_places, width
+    *parts, stream = prepare(
+        stream_grad.reshape(tokens, depth), small_pieces, small_places, width
     )
     branch = lax.all_to_all(
         branch.reshape(frames, patches, depth), "seq", split_axis=0, concat_axis=0, tiled=True
     )
     hidden_grad, spatial_grad = spatial(
-        parts[:PARTS], values, saved, stream, branch.reshape(tokens, depth), parts[PARTS:]
+        saved, stream, branch.reshape(tokens, depth), parts
     )
     spatial_grad = spatial_grad.reshape(3, 1, width, tokens).transpose(0, 1, 3, 2)
     return (hidden_grad.reshape(1, tokens, depth), spatial_grad)

time: 97.4 us -> 95.9 us (0.985)
  local copies, waits for them, and re-layouts: 7.19 us -> 3.49 us
  waiting for transfers between devices: 34.2 us -> 36.8 us
    unnamed x28 -> x20, local copies, waits for them, and re-layouts: 6.85 us -> 3.15 us
    all_to_all x1, waiting for transfers between devices: 7.13 us -> 9.68 us  [shards(): lax.all_to_all(branch.reshape(frames, patches, depth), 'seq', split_axis=...]
  transfers between devices with their start and end apart: 17 -> 17, of which waited for: 8 -> 8; matrix products, arithmetic and copies ran while one was open for 3% -> 3% of each run, Pallas kernels for 12% -> 11%
where the time goes in v5:
time: 95.9 us; the launch traced here: 95.5 us
  starting transfers between devices  37.4 us (39%)
  waiting for transfers between devices  36.8 us (38%)
  Pallas kernels  15.3 us (16%)
  local copies, waits for them, and re-layouts  3.49 us (4%)
  other arithmetic  1.58 us (2%)
    ppermute x15, waiting for transfers between devices, moved(): return lax.ppermute(block, ('clip', 'seq'), pairs)  27.1 us
    ppermute x15, starting transfers between devices, moved(): return lax.ppermute(block, ('clip', 'seq'), pairs)  22.3 us
    all_to_all x1, starting transfers between devices, shards(): lax.all_to_all(mixed, 'seq', split_axis=0, concat_axis=0, tiled=True)  11.2 us
    all_to_all x1, waiting for transfers between devices, shards(): lax.all_to_all(branch.reshape(frames, patches, depth), 'seq', split_axis=...  9.68 us
    pallas_call x1, Pallas kernels, temporal(): pl.pallas_call(functools.partial(temporal_kernel, patches, len(pieces)),...  9.33 us
    pallas_call x1, Pallas kernels, spatial(): pl.pallas_call(spatial_kernel, out_shape=(jax.ShapeDtypeStruct((tokens, d...  4.86 us
    all_to_all x1, starting transfers between devices, shards(): lax.all_to_all(branch.reshape(frames, patches, depth), 'seq', split_axis=...  3.91 us
    unnamed x20, local copies, waits for them, and re-layouts  3.15 us
  transfers between devices with their start and end apart: 17, of which 8 were waited for; matrix products, arithmetic and copies ran while one was open for 3% of the time, Pallas kernels for 11%

profile of v5, /device:TPU:0, one launch (start us, length us, event | category | flops | bytes accessed | tf_op | source)
XLA Modules:
  0.0 95.5 jit_solution(17661017118341447430)
XLA Ops:
  1.2 1.2 %copy.9 = bf16[1,256,576]{2,1,0:T(8,128)(2,1)S(1)} copy(bf16[1,256,576]{1,2,0:T(8,128)(2,1)} %param.9) | data formatting | bytes 589824 | tf_op args[2]
  2.3 1.0 %pad_maximum_fusion.1 = bf16[1,256,1728]{2,1,0:T(8,128)(2,1)} fusion(bf16[1,256,576]{2,1,0:T(8,128)(2,1)S(1)} %copy.9, bf16[1,256,1152]{2,1,0:T(8,128)(2,1)S(1)} %copy-done.4), kind=kLoop, calls=%fused_computation.1 | loop fusion | flops 1769472 | bytes 1769472 | tf_op jit(solution)/shard_map/concatenate | solution.py:360
  4.2 2.7 %collective-permute-start.2 = (bf16[1,144,896]{2,1,0:T(8,128)(2,1)S(1)}, bf16[1,144,896]{2,1,0:T(8,128)(2,1)S(1)}, u32[]{:S(2)}, u32[]{:S(2)}) collective-permute-start(bf16[1,144,896]{2,1,0:T(8,128)(2,1)S(1)} %bitcast.69), channel_id=1, source_target_pairs={{0,16},{1,3},{2,18},{3,1},{4,20},{5,7},{6,22},{7,5},{8,24},{9,11},... | collective-permute-start | bytes 774152 | tf_op jit(solution)/shard_map/ppermute | solution.py:276
  6.9 2.6 %collective-permute-start.3 = (bf16[144,896]{1,0:T(8,128)(2,1)S(1)}, bf16[144,896]{1,0:T(8,128)(2,1)S(1)}, u32[]{:S(2)}, u32[]{:S(2)}) collective-permute-start(bf16[144,896]{1,0:T(8,128)(2,1)S(1)} %fusion), channel_id=1, source_target_pairs={{0,8},{1,13},{2,10},{3,15},{4,12},{5,9},{6,14},{7,11},{8,0},{9,5},... | collective-permute-start | bytes 774152 | tf_op jit(solution)/shard_map/ppermute | solution.py:276
  9.7 1.5 %collective-permute-done.2 = bf16[1,144,896]{2,1,0:T(8,128)(2,1)S(1)} collective-permute-done((bf16[1,144,896]{2,1,0:T(8,128)(2,1)S(1)}, bf16[1,144,896]{2,1,0:T(8,128)(2,1)S(1)}, u32[]{:S(2)}, u32[]{:S(2)}) %collective-permute-start.2) | collective-permute-done | bytes 258080 | tf_op jit(solution)/shard_map/ppermute | solution.py:276
  11.3 4.7 %collective-permute-done.3 = bf16[144,896]{1,0:T(8,128)(2,1)S(1)} collective-permute-done((bf16[144,896]{1,0:T(8,128)(2,1)S(1)}, bf16[144,896]{1,0:T(8,128)(2,1)S(1)}, u32[]{:S(2)}, u32[]{:S(2)}) %collective-permute-start.3) | collective-permute-done | bytes 258080 | tf_op jit(solution)/shard_map/ppermute | solution.py:276
  16.0 11.2 %all-to-all-start = ((bf16[16,16,1728]{2,1,0:T(8,128)(2,1)}), bf16[16,16,1728]{2,1,0:T(8,128)(2,1)S(1)}, u32[]{:S(2)}, u32[]{:S(2)}) async-start(bf16[16,16,1728]{2,1,0:T(8,128)(2,1)} %bitcast.2), calls=%async_computation | async-start | bytes 1835008 | tf_op jit(solution)/shard_map/all_to_all | solution.py:374
  27.6 2.1 %collective-permute-start.4 = (bf16[1,144,896]{2,1,0:T(8,128)(2,1)S(1)}, bf16[1,144,896]{2,1,0:T(8,128)(2,1)S(1)}, u32[]{:S(2)}, u32[]{:S(2)}) collective-permute-start(bf16[1,144,896]{2,1,0:T(8,128)(2,1)S(1)} %bitcast.66), channel_id=1, source_target_pairs={{0,16},{1,3},{2,18},{3,1},{4,20},{5,7},{6,22},{7,5},{8,24},{9,11},... | collective-permute-start | bytes 774152 | tf_op jit(solution)/shard_map/ppermute | solution.py:276
  29.8 1.7 %collective-permute-start.10 = (bf16[2,144,896]{2,1,0:T(8,128)(2,1)S(1)}, bf16[2,144,896]{2,1,0:T(8,128)(2,1)S(1)}, u32[]{:S(2)}, u32[]{:S(2)}) collective-permute-start(bf16[2,144,896]{2,1,0:T(8,128)(2,1)S(1)} %pad_maximum_fusion.2), channel_id=1, source_target_pairs={{0,2},{1,17},{2,0},{3,19},{4,6},{5,21},{6,4},{7,23},{8,10},{9,25},... | collective-permute-start | bytes 1548296 | tf_op jit(solution)/shard_map/ppermute | solution.py:276
  31.5 4.3 %collective-permute-done.4 = bf16[1,144,896]{2,1,0:T(8,128)(2,1)S(1)} collective-permute-done((bf16[1,144,896]{2,1,0:T(8,128)(2,1)S(1)}, bf16[1,144,896]{2,1,0:T(8,128)(2,1)S(1)}, u32[]{:S(2)}, u32[]{:S(2)}) %collective-permute-start.4) | collective-permute-done | bytes 258080 | tf_op jit(solution)/shard_map/ppermute | solution.py:276
  35.8 2.8 %collective-permute-start.5 = (bf16[2,144,896]{2,1,0:T(8,128)(2,1)S(1)}, bf16[2,144,896]{2,1,0:T(8,128)(2,1)S(1)}, u32[]{:S(2)}, u32[]{:S(2)}) collective-permute-start(bf16[2,144,896]{2,1,0:T(8,128)(2,1)S(1)} %pad_maximum_fusion.3), channel_id=1, source_target_pairs={{0,2},{1,17},{2,0},{3,19},{4,6},{5,21},{6,4},{7,23},{8,10},{9,25},... | collective-permute-start | bytes 1548296 | tf_op jit(solution)/shard_map/ppermute | solution.py:276
  39.3 2.4 %collective-permute-start.8 = (bf16[72,640]{1,0:T(8,128)(2,1)S(1)}, bf16[72,640]{1,0:T(8,128)(2,1)S(1)}, u32[]{:S(2)}, u32[]{:S(2)}) collective-permute-start(bf16[72,640]{1,0:T(8,128)(2,1)S(1)} %fusion.1), channel_id=1, source_target_pairs={{0,8},{1,13},{2,10},{3,15},{4,12},{5,9},{6,14},{7,11},{8,0},{9,5},... | collective-permute-start | bytes 276488 | tf_op jit(solution)/shard_map/ppermute | solution.py:276
  41.8 12.4 %collective-permute-done.8 = bf16[72,640]{1,0:T(8,128)(2,1)S(1)} collective-permute-done((bf16[72,640]{1,0:T(8,128)(2,1)S(1)}, bf16[72,640]{1,0:T(8,128)(2,1)S(1)}, u32[]{:S(2)}, u32[]{:S(2)}) %collective-permute-start.8) | collective-permute-done | bytes 92192 | tf_op jit(solution)/shard_map/ppermute | solution.py:276
  55.1 2.8 %collective-permute-start.9 = (bf16[2,72,640]{2,1,0:T(8,128)(2,1)S(1)}, bf16[2,72,640]{2,1,0:T(8,128)(2,1)S(1)}, u32[]{:S(2)}, u32[]{:S(2)}) collective-permute-start(bf16[2,72,640]{2,1,0:T(8,128)(2,1)S(1)} %pad_maximum_fusion.5), channel_id=1, source_target_pairs={{0,16},{1,3},{2,18},{3,1},{4,20},{5,7},{6,22},{7,5},{8,24},{9,11},... | collective-permute-start | bytes 552968 | tf_op jit(solution)/shard_map/ppermute | solution.py:276
  58.5 9.3 %temporal_backward.1 = bf16[256,1152]{1,0:T(8,128)(2,1)} custom-call(s32[32]{0:T(128)S(1)} %stack.189.place_ref, bf16[256,1728]{1,0:T(8,128)(2,1)S(1)} %bitcast.62, f32[1,1152]{1,0:T(1,128)S(1)} %add.133.gain_ref, bf16[4,144,896]{2,1,0:T(8,128)(2,1)S(1)} %constant_dynamic-update-slice_fusion.refs_0_, bf16[4,144,896]{2,1,0:T(8,128)(2,1)} %collective-permute-done.11.refs_1_, ...), custom_call_target="tpu_custom_call" | custom-call | flops 3649044480 | bytes 5750784 | tf_op jit(solution)/shard_map/temporal_backward/pallas_call | solution.py:150
  67.9 2.2 %collective-permute-start.13 = (bf16[4,72,640]{2,1,0:T(8,128)(2,1)S(1)}, bf16[4,72,640]{2,1,0:T(8,128)(2,1)S(1)}, u32[]{:S(2)}, u32[]{:S(2)}) collective-permute-start(bf16[4,72,640]{2,1,0:T(8,128)(2,1)S(1)} %pad_maximum_fusion.4), channel_id=1, source_target_pairs={{0,2},{1,17},{2,0},{3,19},{4,6},{5,21},{6,4},{7,23},{8,10},{9,25},... | collective-permute-start | bytes 1105928 | tf_op jit(solution)/shard_map/ppermute | solution.py:276
  70.1 3.9 %all-to-all-start.1 = ((bf16[16,16,1152]{2,1,0:T(8,128)(2,1)}), bf16[16,16,1152]{2,1,0:T(8,128)(2,1)S(1)}, u32[]{:S(2)}, u32[]{:S(2)}) async-start(bf16[16,16,1152]{2,1,0:T(8,128)(2,1)} %bitcast.53), calls=%async_computation.1 | async-start | bytes 1179648 | tf_op jit(solution)/shard_map/all_to_all | solution.py:394
  74.1 1.5 %collective-permute-done.13 = bf16[4,72,640]{2,1,0:T(8,128)(2,1)S(1)} collective-permute-done((bf16[4,72,640]{2,1,0:T(8,128)(2,1)S(1)}, bf16[4,72,640]{2,1,0:T(8,128)(2,1)S(1)}, u32[]{:S(2)}, u32[]{:S(2)}) %collective-permute-start.13) | collective-permute-done | bytes 368672 | tf_op jit(solution)/shard_map/ppermute | solution.py:276
  75.8 2.1 %collective-permute-done.14.refs_1_ = bf16[8,72,640]{2,1,0:T(8,128)(2,1)S(1)} collective-permute-done((bf16[8,72,640]{2,1,0:T(8,128)(2,1)S(1)}, bf16[8,72,640]{2,1,0:T(8,128)(2,1)S(1)}, u32[]{:S(2)}, u32[]{:S(2)}) %collective-permute-start.14) | collective-permute-done | bytes 737312 | tf_op jit(solution)/shard_map/ppermute | solution.py:276
  77.9 1.1 %spatial_prepare.1 = (bf16[288,1152]{1,0:T(8,128)(2,1)S(1)}, bf16[288,1152]{1,0:T(8,128)(2,1)S(1)}, bf16[256,1152]{1,0:T(8,128)(2,1)S(1)}) custom-call(s32[32]{0:T(128)S(1)} %stack.212.place_ref, bf16[256,1152]{1,0:T(8,128)(2,1)S(1)} %bitcast.63, bf16[8,72,640]{2,1,0:T(8,128)(2,1)S(1)} %constant_dynamic-update-slice_fusion.2.refs_0_, ...), custom_call_target="tpu_custom_call" | custom-call | bytes 3833856 | tf_op jit(solution)/shard_map/spatial_prepare/pallas_call | solution.py:206
  79.0 0.8 copy-done.2
  79.8 9.7 %all-to-all-done.1 = bf16[16,16,1152]{2,1,0:T(8,128)(2,1)S(1)} async-done(((bf16[16,16,1152]{2,1,0:T(8,128)(2,1)}), bf16[16,16,1152]{2,1,0:T(8,128)(2,1)S(1)}, u32[]{:S(2)}, u32[]{:S(2)}) %all-to-all-start.1) | async-done | bytes 589856 | tf_op jit(solution)/shard_map/all_to_all | solution.py:394
  89.5 1.1 %copy-done.3 = bf16[256,1152]{1,0:T(8,128)(2,1)S(1)} copy-done((bf16[256,1152]{1,0:T(8,128)(2,1)S(1)}, bf16[256,1152]{1,0:T(8,128)(2,1)}, u32[]{:S(2)}) %copy-start.3) | copy-done | bytes 589848
  90.6 4.9 %spatial_backward.1 = (bf16[256,1152]{1,0:T(8,128)(2,1)}, bf16[3,8,72,256]{3,2,1,0:T(8,128)(2,1)}) custom-call(bf16[3,8,72,256]{3,2,1,0:T(8,128)(2,1)S(1)} %bitcast.65, bf16[256,1152]{1,0:T(8,128)(2,1)S(1)} %copy-done.3, bf16[256,1152]{1,0:T(8,128)(2,1)S(1)} %bitcast.64, bf16[288,1152]{1,0:T(8,128)(2,1)S(1)} %get-tuple-element.38.refs_0_, ...), custom_call_target="tpu_custom_call" | custom-call | flops 1681915904 | bytes 4866048 | tf_op jit(solution)/shard_map/spatial_backward/pallas_call | solution.py:254
  (49 shorter events, 4.8 us)
Async XLA Ops:
  0.6 1.7 %copy-start.4 = (bf16[1,256,1152]{2,1,0:T(8,128)(2,1)S(1)}, bf16[1,256,1152]{2,1,0:T(8,128)(2,1)}, u32[]{:S(2)}) copy-start(bf16[1,256,1152]{2,1,0:T(8,128)(2,1)} %param.8) | copy-start | bytes 1769476
  0.6 2.7 %collective-permute-start = (bf16[72,1728]{1,0:T(8,128)(2,1)}, bf16[72,1728]{1,0:T(8,128)(2,1)S(1)}, u32[]{:S(2)}, u32[]{:S(2)}) collective-permute-start(bf16[72,1728]{1,0:T(8,128)(2,1)} %param.12), channel_id=1, source_target_pairs={{0,1},{1,0},{2,3},{3,2},{4,5},{5,4},{6,7},{7,6},{8,9},{9,8},{10,11... | collective-permute-start | bytes 746504 | tf_op jit(solution)/shard_map/ppermute | solution.py:276
  2.3 1.0 %copy-start.5 = (bf16[72,1728]{1,0:T(8,128)(2,1)S(1)}, bf16[72,1728]{1,0:T(8,128)(2,1)}, u32[]{:S(2)}) copy-start(bf16[72,1728]{1,0:T(8,128)(2,1)} %param.12) | copy-start | bytes 746500
  3.4 6.1 %copy-start.7 = (f32[1152]{0:T(1024)S(1)}, f32[1152]{0:T(1024)}, u32[]{:S(2)}) copy-start(f32[1152]{0:T(1024)} %param.11) | copy-start | bytes 13828
  3.5 0.7 collective-permute-start.1
  4.2 7.0 %collective-permute-start.2 = (bf16[1,144,896]{2,1,0:T(8,128)(2,1)S(1)}, bf16[1,144,896]{2,1,0:T(8,128)(2,1)S(1)}, u32[]{:S(2)}, u32[]{:S(2)}) collective-permute-start(bf16[1,144,896]{2,1,0:T(8,128)(2,1)S(1)} %bitcast.69), channel_id=1, source_target_pairs={{0,16},{1,3},{2,18},{3,1},{4,20},{5,7},{6,22},{7,5},{8,24},{9,11},... | collective-permute-start | bytes 774152 | tf_op jit(solution)/shard_map/ppermute | solution.py:276
  6.9 9.1 %collective-permute-start.3 = (bf16[144,896]{1,0:T(8,128)(2,1)S(1)}, bf16[144,896]{1,0:T(8,128)(2,1)S(1)}, u32[]{:S(2)}, u32[]{:S(2)}) collective-permute-start(bf16[144,896]{1,0:T(8,128)(2,1)S(1)} %fusion), channel_id=1, source_target_pairs={{0,8},{1,13},{2,10},{3,15},{4,12},{5,9},{6,14},{7,11},{8,0},{9,5},... | collective-permute-start | bytes 774152 | tf_op jit(solution)/shard_map/ppermute | solution.py:276
  11.3 15.9 %copy-start.6 = (bf16[36,1152]{1,0:T(8,128)(2,1)S(1)}, bf16[36,1152]{1,0:T(8,128)(2,1)}, u32[]{:S(2)}) copy-start(bf16[36,1152]{1,0:T(8,128)(2,1)} %param.13) | copy-start | bytes 248836
  16.0 38.6 %all-to-all-start = ((bf16[16,16,1728]{2,1,0:T(8,128)(2,1)}), bf16[16,16,1728]{2,1,0:T(8,128)(2,1)S(1)}, u32[]{:S(2)}, u32[]{:S(2)}) async-start(bf16[16,16,1728]{2,1,0:T(8,128)(2,1)} %bitcast.2), calls=%async_computation | async-start | bytes 1835008 | tf_op jit(solution)/shard_map/all_to_all | solution.py:374
  27.2 4.3 %collective-permute-start.6 = (bf16[36,1152]{1,0:T(8,128)(2,1)S(1)}, bf16[36,1152]{1,0:T(8,128)(2,1)S(1)}, u32[]{:S(2)}, u32[]{:S(2)}) collective-permute-start(bf16[36,1152]{1,0:T(8,128)(2,1)S(1)} %copy-done.6), channel_id=1, source_target_pairs={{0,1},{1,0},{2,3},{3,2},{4,5},{5,4},{6,7},{7,6},{8,9},{9,8},{10,11... | collective-permute-start | bytes 248840 | tf_op jit(solution)/shard_map/ppermute | solution.py:276
  27.6 8.1 %collective-permute-start.4 = (bf16[1,144,896]{2,1,0:T(8,128)(2,1)S(1)}, bf16[1,144,896]{2,1,0:T(8,128)(2,1)S(1)}, u32[]{:S(2)}, u32[]{:S(2)}) collective-permute-start(bf16[1,144,896]{2,1,0:T(8,128)(2,1)S(1)} %bitcast.66), channel_id=1, source_target_pairs={{0,16},{1,3},{2,18},{3,1},{4,20},{5,7},{6,22},{7,5},{8,24},{9,11},... | collective-permute-start | bytes 774152 | tf_op jit(solution)/shard_map/ppermute | solution.py:276
  29.8 24.5 %collective-permute-start.10 = (bf16[2,144,896]{2,1,0:T(8,128)(2,1)S(1)}, bf16[2,144,896]{2,1,0:T(8,128)(2,1)S(1)}, u32[]{:S(2)}, u32[]{:S(2)}) collective-permute-start(bf16[2,144,896]{2,1,0:T(8,128)(2,1)S(1)} %pad_maximum_fusion.2), channel_id=1, source_target_pairs={{0,2},{1,17},{2,0},{3,19},{4,6},{5,21},{6,4},{7,23},{8,10},{9,25},... | collective-permute-start | bytes 1548296 | tf_op jit(solution)/shard_map/ppermute | solution.py:276
  35.8 18.6 %collective-permute-start.5 = (bf16[2,144,896]{2,1,0:T(8,128)(2,1)S(1)}, bf16[2,144,896]{2,1,0:T(8,128)(2,1)S(1)}, u32[]{:S(2)}, u32[]{:S(2)}) collective-permute-start(bf16[2,144,896]{2,1,0:T(8,128)(2,1)S(1)} %pad_maximum_fusion.3), channel_id=1, source_target_pairs={{0,2},{1,17},{2,0},{3,19},{4,6},{5,21},{6,4},{7,23},{8,10},{9,25},... | collective-permute-start | bytes 1548296 | tf_op jit(solution)/shard_map/ppermute | solution.py:276
  38.7 3.2 %collective-permute-start.7 = (bf16[72,640]{1,0:T(8,128)(2,1)S(1)}, bf16[72,640]{1,0:T(8,128)(2,1)S(1)}, u32[]{:S(2)}, u32[]{:S(2)}) collective-permute-start(bf16[72,640]{1,0:T(8,128)(2,1)S(1)} %fusion.1), channel_id=1, source_target_pairs={{0,0},{1,5},{2,2},{3,7},{4,4},{5,1},{6,6},{7,3},{8,8},{9,13},{10,1... | collective-permute-start | bytes 276488 | tf_op jit(solution)/shard_map/ppermute | solution.py:276
  39.3 14.9 %collective-permute-start.8 = (bf16[72,640]{1,0:T(8,128)(2,1)S(1)}, bf16[72,640]{1,0:T(8,128)(2,1)S(1)}, u32[]{:S(2)}, u32[]{:S(2)}) collective-permute-start(bf16[72,640]{1,0:T(8,128)(2,1)S(1)} %fusion.1), channel_id=1, source_target_pairs={{0,8},{1,13},{2,10},{3,15},{4,12},{5,9},{6,14},{7,11},{8,0},{9,5},... | collective-permute-start | bytes 276488 | tf_op jit(solution)/shard_map/ppermute | solution.py:276
  54.3 3.5 %collective-permute-start.11 = (bf16[4,144,896]{2,1,0:T(8,128)(2,1)S(1)}, bf16[4,144,896]{2,1,0:T(8,128)(2,1)}, u32[]{:S(2)}, u32[]{:S(2)}) collective-permute-start(bf16[4,144,896]{2,1,0:T(8,128)(2,1)S(1)} %constant_dynamic-update-slice_fusion.refs_0_), channel_id=1, source_target_pairs={{0,1},{1,0},{2,3},{3,2},{4,5},{5,4},{6,7},{7,6},{8,9},{9,8},{10,11... | collective-permute-start | bytes 3096584 | tf_op jit(solution)/shard_map/ppermute | solution.py:276
  54.6 3.9 %collective-permute-start.12 = (bf16[4,144,896]{2,1,0:T(8,128)(2,1)S(1)}, bf16[4,144,896]{2,1,0:T(8,128)(2,1)S(1)}, u32[]{:S(2)}, u32[]{:S(2)}) collective-permute-start(bf16[4,144,896]{2,1,0:T(8,128)(2,1)S(1)} %pad_maximum_fusion.refs_2_), channel_id=1, source_target_pairs={{0,1},{1,0},{2,3},{3,2},{4,5},{5,4},{6,7},{7,6},{8,9},{9,8},{10,11... | collective-permute-start | bytes 3096584 | tf_op jit(solution)/shard_map/ppermute | solution.py:276
  55.1 12.7 %collective-permute-start.9 = (bf16[2,72,640]{2,1,0:T(8,128)(2,1)S(1)}, bf16[2,72,640]{2,1,0:T(8,128)(2,1)S(1)}, u32[]{:S(2)}, u32[]{:S(2)}) collective-permute-start(bf16[2,72,640]{2,1,0:T(8,128)(2,1)S(1)} %pad_maximum_fusion.5), channel_id=1, source_target_pairs={{0,16},{1,3},{2,18},{3,1},{4,20},{5,7},{6,22},{7,5},{8,24},{9,11},... | collective-permute-start | bytes 552968 | tf_op jit(solution)/shard_map/ppermute | solution.py:276
  67.9 7.6 %collective-permute-start.13 = (bf16[4,72,640]{2,1,0:T(8,128)(2,1)S(1)}, bf16[4,72,640]{2,1,0:T(8,128)(2,1)S(1)}, u32[]{:S(2)}, u32[]{:S(2)}) collective-permute-start(bf16[4,72,640]{2,1,0:T(8,128)(2,1)S(1)} %pad_maximum_fusion.4), channel_id=1, source_target_pairs={{0,2},{1,17},{2,0},{3,19},{4,6},{5,21},{6,4},{7,23},{8,10},{9,25},... | collective-permute-start | bytes 1105928 | tf_op jit(solution)/shard_map/ppermute | solution.py:276
  70.1 19.5 %all-to-all-start.1 = ((bf16[16,16,1152]{2,1,0:T(8,128)(2,1)}), bf16[16,16,1152]{2,1,0:T(8,128)(2,1)S(1)}, u32[]{:S(2)}, u32[]{:S(2)}) async-start(bf16[16,16,1152]{2,1,0:T(8,128)(2,1)} %bitcast.53), calls=%async_computation.1 | async-start | bytes 1179648 | tf_op jit(solution)/shard_map/all_to_all | solution.py:394
  74.0 3.9 %copy-start = (bf16[1,256,1152]{2,1,0:T(8,128)(2,1)S(1)}, bf16[1,256,1152]{2,1,0:T(8,128)(2,1)}, u32[]{:S(2)}) copy-start(bf16[1,256,1152]{2,1,0:T(8,128)(2,1)} %param.10) | copy-start | bytes 1769476
  75.6 2.3 %collective-permute-start.14 = (bf16[8,72,640]{2,1,0:T(8,128)(2,1)S(1)}, bf16[8,72,640]{2,1,0:T(8,128)(2,1)S(1)}, u32[]{:S(2)}, u32[]{:S(2)}) collective-permute-start(bf16[8,72,640]{2,1,0:T(8,128)(2,1)S(1)} %constant_dynamic-update-slice_fusion.2.refs_0_), channel_id=1, source_target_pairs={{0,1},{1,0},{2,3},{3,2},{4,5},{5,4},{6,7},{7,6},{8,9},{9,8},{10,11... | collective-permute-start | bytes 2211848 | tf_op jit(solution)/shard_map/ppermute | solution.py:276
  77.9 11.6 %copy-start.1 = (bf16[3,1,256,576]{2,3,1,0:T(8,128)(2,1)S(1)}, bf16[3,1,256,576]{2,3,1,0:T(8,128)(2,1)}, u32[]{:S(2)}) copy-start(bf16[3,1,256,576]{2,3,1,0:T(8,128)(2,1)} %param.7) | copy-start | bytes 2654212
  89.5 1.1 %copy-start.3 = (bf16[256,1152]{1,0:T(8,128)(2,1)S(1)}, bf16[256,1152]{1,0:T(8,128)(2,1)}, u32[]{:S(2)}) copy-start(bf16[256,1152]{1,0:T(8,128)(2,1)} %copy-done.2) | copy-start | bytes 1769476
  (1 other events, 0.8 us)

commit v6 on v5

--- a/solution.py
+++ b/solution.py
@@ -11,7 +11,7 @@
 HEADS = 8
 HD = 72
 LANES = 128
-PARTS = 2
+PARTS = 3
 
 epsilon = 1e-06
 VMEM_LIMIT = 24 * 1024 * 1024

time: 95.9 us -> 95.1 us (level)
  local copies, waits for them, and re-layouts: 3.49 us -> 1.61 us
    unnamed x20 -> x16, local copies, waits for them, and re-layouts: 3.15 us -> 1.27 us
where the time goes in v6:
time: 95.1 us; the launch traced here: 94.7 us
  waiting for transfers between devices  37.6 us (40%)
  starting transfers between devices  37.4 us (39%)
  Pallas kernels  15.7 us (17%)
  local copies, waits for them, and re-layouts  1.61 us (2%)
  other arithmetic  1.57 us (2%)
    ppermute x15, waiting for transfers between devices, moved(): return lax.ppermute(block, ('clip', 'seq'), pairs)  27.1 us
    ppermute x15, starting transfers between devices, moved(): return lax.ppermute(block, ('clip', 'seq'), pairs)  22.3 us
    all_to_all x1, starting transfers between devices, shards(): lax.all_to_all(mixed, 'seq', split_axis=0, concat_axis=0, tiled=True)  11.2 us
    all_to_all x1, waiting for transfers between devices, shards(): lax.all_to_all(branch.reshape(frames, patches, depth), 'seq', split_axis=...  10.5 us
    pallas_call x1, Pallas kernels, temporal(): pl.pallas_call(functools.partial(temporal_kernel, patches, len(pieces)),...  9.33 us
    pallas_call x1, Pallas kernels, spatial(): pl.pallas_call(spatial_kernel, out_shape=(jax.ShapeDtypeStruct((tokens, d...  5.22 us
    all_to_all x1, starting transfers between devices, shards(): lax.all_to_all(branch.reshape(frames, patches, depth), 'seq', split_axis=...  3.91 us
  transfers between devices with their start and end apart: 17, of which 8 were waited for; matrix products, arithmetic and copies ran while one was open for 3% of the time, Pallas kernels for 11%

profile of v6, /device:TPU:0, one launch (start us, length us, event | category | flops | bytes accessed | tf_op | source)
XLA Modules:
  0.0 94.7 jit_solution(7834207546262382697)
XLA Ops:
  1.2 1.2 %copy.9 = bf16[1,256,576]{2,1,0:T(8,128)(2,1)S(1)} copy(bf16[1,256,576]{1,2,0:T(8,128)(2,1)} %param.9) | data formatting | bytes 589824 | tf_op args[2]
  2.3 1.0 %pad_maximum_fusion.1 = bf16[1,256,1728]{2,1,0:T(8,128)(2,1)} fusion(bf16[1,256,576]{2,1,0:T(8,128)(2,1)S(1)} %copy.9, bf16[1,256,1152]{2,1,0:T(8,128)(2,1)S(1)} %copy-done.2), kind=kLoop, calls=%fused_computation.1 | loop fusion | flops 1769472 | bytes 1769472 | tf_op jit(solution)/shard_map/concatenate | solution.py:360
  3.5 0.7 collective-permute-start.1
  4.2 2.7 %collective-permute-start.2 = (bf16[1,144,896]{2,1,0:T(8,128)(2,1)S(1)}, bf16[1,144,896]{2,1,0:T(8,128)(2,1)S(1)}, u32[]{:S(2)}, u32[]{:S(2)}) collective-permute-start(bf16[1,144,896]{2,1,0:T(8,128)(2,1)S(1)} %bitcast.69), channel_id=1, source_target_pairs={{0,16},{1,3},{2,18},{3,1},{4,20},{5,7},{6,22},{7,5},{8,24},{9,11},... | collective-permute-start | bytes 774152 | tf_op jit(solution)/shard_map/ppermute | solution.py:276
  6.9 2.6 %collective-permute-start.3 = (bf16[144,896]{1,0:T(8,128)(2,1)S(1)}, bf16[144,896]{1,0:T(8,128)(2,1)S(1)}, u32[]{:S(2)}, u32[]{:S(2)}) collective-permute-start(bf16[144,896]{1,0:T(8,128)(2,1)S(1)} %fusion), channel_id=1, source_target_pairs={{0,8},{1,13},{2,10},{3,15},{4,12},{5,9},{6,14},{7,11},{8,0},{9,5},... | collective-permute-start | bytes 774152 | tf_op jit(solution)/shard_map/ppermute | solution.py:276
  9.7 1.5 %collective-permute-done.2 = bf16[1,144,896]{2,1,0:T(8,128)(2,1)S(1)} collective-permute-done((bf16[1,144,896]{2,1,0:T(8,128)(2,1)S(1)}, bf16[1,144,896]{2,1,0:T(8,128)(2,1)S(1)}, u32[]{:S(2)}, u32[]{:S(2)}) %collective-permute-start.2) | collective-permute-done | bytes 258080 | tf_op jit(solution)/shard_map/ppermute | solution.py:276
  11.3 4.7 %collective-permute-done.3 = bf16[144,896]{1,0:T(8,128)(2,1)S(1)} collective-permute-done((bf16[144,896]{1,0:T(8,128)(2,1)S(1)}, bf16[144,896]{1,0:T(8,128)(2,1)S(1)}, u32[]{:S(2)}, u32[]{:S(2)}) %collective-permute-start.3) | collective-permute-done | bytes 258080 | tf_op jit(solution)/shard_map/ppermute | solution.py:276
  16.0 11.2 %all-to-all-start = ((bf16[16,16,1728]{2,1,0:T(8,128)(2,1)}), bf16[16,16,1728]{2,1,0:T(8,128)(2,1)S(1)}, u32[]{:S(2)}, u32[]{:S(2)}) async-start(bf16[16,16,1728]{2,1,0:T(8,128)(2,1)} %bitcast.2), calls=%async_computation | async-start | bytes 1835008 | tf_op jit(solution)/shard_map/all_to_all | solution.py:374
  27.6 2.1 %collective-permute-start.4 = (bf16[1,144,896]{2,1,0:T(8,128)(2,1)S(1)}, bf16[1,144,896]{2,1,0:T(8,128)(2,1)S(1)}, u32[]{:S(2)}, u32[]{:S(2)}) collective-permute-start(bf16[1,144,896]{2,1,0:T(8,128)(2,1)S(1)} %bitcast.66), channel_id=1, source_target_pairs={{0,16},{1,3},{2,18},{3,1},{4,20},{5,7},{6,22},{7,5},{8,24},{9,11},... | collective-permute-start | bytes 774152 | tf_op jit(solution)/shard_map/ppermute | solution.py:276
  29.8 1.7 %collective-permute-start.10 = (bf16[2,144,896]{2,1,0:T(8,128)(2,1)S(1)}, bf16[2,144,896]{2,1,0:T(8,128)(2,1)S(1)}, u32[]{:S(2)}, u32[]{:S(2)}) collective-permute-start(bf16[2,144,896]{2,1,0:T(8,128)(2,1)S(1)} %pad_maximum_fusion.2), channel_id=1, source_target_pairs={{0,2},{1,17},{2,0},{3,19},{4,6},{5,21},{6,4},{7,23},{8,10},{9,25},... | collective-permute-start | bytes 1548296 | tf_op jit(solution)/shard_map/ppermute | solution.py:276
  31.5 4.3 %collective-permute-done.4 = bf16[1,144,896]{2,1,0:T(8,128)(2,1)S(1)} collective-permute-done((bf16[1,144,896]{2,1,0:T(8,128)(2,1)S(1)}, bf16[1,144,896]{2,1,0:T(8,128)(2,1)S(1)}, u32[]{:S(2)}, u32[]{:S(2)}) %collective-permute-start.4) | collective-permute-done | bytes 258080 | tf_op jit(solution)/shard_map/ppermute | solution.py:276
  35.8 2.8 %collective-permute-start.5 = (bf16[2,144,896]{2,1,0:T(8,128)(2,1)S(1)}, bf16[2,144,896]{2,1,0:T(8,128)(2,1)S(1)}, u32[]{:S(2)}, u32[]{:S(2)}) collective-permute-start(bf16[2,144,896]{2,1,0:T(8,128)(2,1)S(1)} %pad_maximum_fusion.3), channel_id=1, source_target_pairs={{0,2},{1,17},{2,0},{3,19},{4,6},{5,21},{6,4},{7,23},{8,10},{9,25},... | collective-permute-start | bytes 1548296 | tf_op jit(solution)/shard_map/ppermute | solution.py:276
  38.6 0.7 collective-permute-start.7
  39.3 2.4 %collective-permute-start.8 = (bf16[72,640]{1,0:T(8,128)(2,1)S(1)}, bf16[72,640]{1,0:T(8,128)(2,1)S(1)}, u32[]{:S(2)}, u32[]{:S(2)}) collective-permute-start(bf16[72,640]{1,0:T(8,128)(2,1)S(1)} %fusion.1), channel_id=1, source_target_pairs={{0,8},{1,13},{2,10},{3,15},{4,12},{5,9},{6,14},{7,11},{8,0},{9,5},... | collective-permute-start | bytes 276488 | tf_op jit(solution)/shard_map/ppermute | solution.py:276
  41.8 12.4 %collective-permute-done.8 = bf16[72,640]{1,0:T(8,128)(2,1)S(1)} collective-permute-done((bf16[72,640]{1,0:T(8,128)(2,1)S(1)}, bf16[72,640]{1,0:T(8,128)(2,1)S(1)}, u32[]{:S(2)}, u32[]{:S(2)}) %collective-permute-start.8) | collective-permute-done | bytes 92192 | tf_op jit(solution)/shard_map/ppermute | solution.py:276
  55.1 2.8 %collective-permute-start.9 = (bf16[2,72,640]{2,1,0:T(8,128)(2,1)S(1)}, bf16[2,72,640]{2,1,0:T(8,128)(2,1)S(1)}, u32[]{:S(2)}, u32[]{:S(2)}) collective-permute-start(bf16[2,72,640]{2,1,0:T(8,128)(2,1)S(1)} %pad_maximum_fusion.5), channel_id=1, source_target_pairs={{0,16},{1,3},{2,18},{3,1},{4,20},{5,7},{6,22},{7,5},{8,24},{9,11},... | collective-permute-start | bytes 552968 | tf_op jit(solution)/shard_map/ppermute | solution.py:276
  58.5 9.3 %temporal_backward.1 = bf16[256,1152]{1,0:T(8,128)(2,1)} custom-call(s32[32]{0:T(128)S(1)} %stack.189.place_ref, bf16[256,1728]{1,0:T(8,128)(2,1)S(1)} %bitcast.62, f32[1,1152]{1,0:T(1,128)S(1)} %add.133.gain_ref, bf16[4,144,896]{2,1,0:T(8,128)(2,1)S(1)} %constant_dynamic-update-slice_fusion.refs_0_, bf16[4,144,896]{2,1,0:T(8,128)(2,1)} %collective-permute-done.11.refs_1_, ...), custom_call_target="tpu_custom_call" | custom-call | flops 3649044480 | bytes 5750784 | tf_op jit(solution)/shard_map/temporal_backward/pallas_call | solution.py:150
  67.9 2.2 %collective-permute-start.13 = (bf16[4,72,640]{2,1,0:T(8,128)(2,1)S(1)}, bf16[4,72,640]{2,1,0:T(8,128)(2,1)S(1)}, u32[]{:S(2)}, u32[]{:S(2)}) collective-permute-start(bf16[4,72,640]{2,1,0:T(8,128)(2,1)S(1)} %pad_maximum_fusion.4), channel_id=1, source_target_pairs={{0,2},{1,17},{2,0},{3,19},{4,6},{5,21},{6,4},{7,23},{8,10},{9,25},... | collective-permute-start | bytes 1105928 | tf_op jit(solution)/shard_map/ppermute | solution.py:276
  70.1 3.9 %all-to-all-start.1 = ((bf16[16,16,1152]{2,1,0:T(8,128)(2,1)}), bf16[16,16,1152]{2,1,0:T(8,128)(2,1)S(1)}, u32[]{:S(2)}, u32[]{:S(2)}) async-start(bf16[16,16,1152]{2,1,0:T(8,128)(2,1)} %bitcast.53), calls=%async_computation.1 | async-start | bytes 1179648 | tf_op jit(solution)/shard_map/all_to_all | solution.py:394
  74.0 1.5 %collective-permute-done.13 = bf16[4,72,640]{2,1,0:T(8,128)(2,1)S(1)} collective-permute-done((bf16[4,72,640]{2,1,0:T(8,128)(2,1)S(1)}, bf16[4,72,640]{2,1,0:T(8,128)(2,1)S(1)}, u32[]{:S(2)}, u32[]{:S(2)}) %collective-permute-start.13) | collective-permute-done | bytes 368672 | tf_op jit(solution)/shard_map/ppermute | solution.py:276
  75.8 2.1 %collective-permute-done.14.refs_1_ = bf16[8,72,640]{2,1,0:T(8,128)(2,1)S(1)} collective-permute-done((bf16[8,72,640]{2,1,0:T(8,128)(2,1)S(1)}, bf16[8,72,640]{2,1,0:T(8,128)(2,1)S(1)}, u32[]{:S(2)}, u32[]{:S(2)}) %collective-permute-start.14) | collective-permute-done | bytes 737312 | tf_op jit(solution)/shard_map/ppermute | solution.py:276
  77.9 1.1 %spatial_prepare.1 = (bf16[192,1152]{1,0:T(8,128)(2,1)S(1)}, bf16[192,1152]{1,0:T(8,128)(2,1)S(1)}, bf16[192,1152]{1,0:T(8,128)(2,1)S(1)}, bf16[256,1152]{1,0:T(8,128)(2,1)S(1)}) custom-call(s32[32]{0:T(128)S(1)} %stack.212.place_ref, bf16[256,1152]{1,0:T(8,128)(2,1)S(1)} %bitcast.63, bf16[8,72,640]{2,1,0:T(8,128)(2,1)S(1)} %constant_dynamic-update-slice_fusion.2.refs_0_, ...), custom_call_target="tpu_custom_call" | custom-call | bytes 3833856 | tf_op jit(solution)/shard_map/spatial_prepare/pallas_call | solution.py:206
  79.0 10.5 %all-to-all-done.1 = bf16[16,16,1152]{2,1,0:T(8,128)(2,1)S(1)} async-done(((bf16[16,16,1152]{2,1,0:T(8,128)(2,1)}), bf16[16,16,1152]{2,1,0:T(8,128)(2,1)S(1)}, u32[]{:S(2)}, u32[]{:S(2)}) %all-to-all-start.1) | async-done | bytes 589856 | tf_op jit(solution)/shard_map/all_to_all | solution.py:394
  89.5 5.2 %spatial_backward.1 = (bf16[256,1152]{1,0:T(8,128)(2,1)}, bf16[3,8,72,256]{3,2,1,0:T(8,128)(2,1)}) custom-call(bf16[3,8,72,256]{3,2,1,0:T(8,128)(2,1)S(1)} %bitcast.65, bf16[256,1152]{1,0:T(8,128)(2,1)S(1)} %get-tuple-element.37.stream_ref, bf16[256,1152]{1,0:T(8,128)(2,1)S(1)} %bitcast.64, bf16[192,1152]{1,0:T(8,128)(2,1)S(1)} %get-tuple-element.39.refs_0_, ...), custom_call_target="tpu_custom_call" | custom-call | flops 1681915904 | bytes 4866048 | tf_op jit(solution)/shard_map/spatial_backward/pallas_call | solution.py:254
  (45 shorter events, 3.5 us)
Async XLA Ops:
  0.6 1.7 %copy-start.2 = (bf16[1,256,1152]{2,1,0:T(8,128)(2,1)S(1)}, bf16[1,256,1152]{2,1,0:T(8,128)(2,1)}, u32[]{:S(2)}) copy-start(bf16[1,256,1152]{2,1,0:T(8,128)(2,1)} %param.8) | copy-start | bytes 1769476
  0.6 2.7 %collective-permute-start = (bf16[72,1728]{1,0:T(8,128)(2,1)}, bf16[72,1728]{1,0:T(8,128)(2,1)S(1)}, u32[]{:S(2)}, u32[]{:S(2)}) collective-permute-start(bf16[72,1728]{1,0:T(8,128)(2,1)} %param.12), channel_id=1, source_target_pairs={{0,1},{1,0},{2,3},{3,2},{4,5},{5,4},{6,7},{7,6},{8,9},{9,8},{10,11... | collective-permute-start | bytes 746504 | tf_op jit(solution)/shard_map/ppermute | solution.py:276
  2.3 1.0 %copy-start.3 = (bf16[72,1728]{1,0:T(8,128)(2,1)S(1)}, bf16[72,1728]{1,0:T(8,128)(2,1)}, u32[]{:S(2)}) copy-start(bf16[72,1728]{1,0:T(8,128)(2,1)} %param.12) | copy-start | bytes 746500
  3.4 6.1 %copy-start.5 = (f32[1152]{0:T(1024)S(1)}, f32[1152]{0:T(1024)}, u32[]{:S(2)}) copy-start(f32[1152]{0:T(1024)} %param.11) | copy-start | bytes 13828
  3.5 0.7 collective-permute-start.1
  4.2 7.0 %collective-permute-start.2 = (bf16[1,144,896]{2,1,0:T(8,128)(2,1)S(1)}, bf16[1,144,896]{2,1,0:T(8,128)(2,1)S(1)}, u32[]{:S(2)}, u32[]{:S(2)}) collective-permute-start(bf16[1,144,896]{2,1,0:T(8,128)(2,1)S(1)} %bitcast.69), channel_id=1, source_target_pairs={{0,16},{1,3},{2,18},{3,1},{4,20},{5,7},{6,22},{7,5},{8,24},{9,11},... | collective-permute-start | bytes 774152 | tf_op jit(solution)/shard_map/ppermute | solution.py:276
  6.9 9.1 %collective-permute-start.3 = (bf16[144,896]{1,0:T(8,128)(2,1)S(1)}, bf16[144,896]{1,0:T(8,128)(2,1)S(1)}, u32[]{:S(2)}, u32[]{:S(2)}) collective-permute-start(bf16[144,896]{1,0:T(8,128)(2,1)S(1)} %fusion), channel_id=1, source_target_pairs={{0,8},{1,13},{2,10},{3,15},{4,12},{5,9},{6,14},{7,11},{8,0},{9,5},... | collective-permute-start | bytes 774152 | tf_op jit(solution)/shard_map/ppermute | solution.py:276
  11.3 15.9 %copy-start.4 = (bf16[36,1152]{1,0:T(8,128)(2,1)S(1)}, bf16[36,1152]{1,0:T(8,128)(2,1)}, u32[]{:S(2)}) copy-start(bf16[36,1152]{1,0:T(8,128)(2,1)} %param.13) | copy-start | bytes 248836
  16.0 38.6 %all-to-all-start = ((bf16[16,16,1728]{2,1,0:T(8,128)(2,1)}), bf16[16,16,1728]{2,1,0:T(8,128)(2,1)S(1)}, u32[]{:S(2)}, u32[]{:S(2)}) async-start(bf16[16,16,1728]{2,1,0:T(8,128)(2,1)} %bitcast.2), calls=%async_computation | async-start | bytes 1835008 | tf_op jit(solution)/shard_map/all_to_all | solution.py:374
  27.2 4.3 %collective-permute-start.6 = (bf16[36,1152]{1,0:T(8,128)(2,1)S(1)}, bf16[36,1152]{1,0:T(8,128)(2,1)S(1)}, u32[]{:S(2)}, u32[]{:S(2)}) collective-permute-start(bf16[36,1152]{1,0:T(8,128)(2,1)S(1)} %copy-done.4), channel_id=1, source_target_pairs={{0,1},{1,0},{2,3},{3,2},{4,5},{5,4},{6,7},{7,6},{8,9},{9,8},{10,11... | collective-permute-start | bytes 248840 | tf_op jit(solution)/shard_map/ppermute | solution.py:276
  27.6 8.1 %collective-permute-start.4 = (bf16[1,144,896]{2,1,0:T(8,128)(2,1)S(1)}, bf16[1,144,896]{2,1,0:T(8,128)(2,1)S(1)}, u32[]{:S(2)}, u32[]{:S(2)}) collective-permute-start(bf16[1,144,896]{2,1,0:T(8,128)(2,1)S(1)} %bitcast.66), channel_id=1, source_target_pairs={{0,16},{1,3},{2,18},{3,1},{4,20},{5,7},{6,22},{7,5},{8,24},{9,11},... | collective-permute-start | bytes 774152 | tf_op jit(solution)/shard_map/ppermute | solution.py:276
  29.8 24.5 %collective-permute-start.10 = (bf16[2,144,896]{2,1,0:T(8,128)(2,1)S(1)}, bf16[2,144,896]{2,1,0:T(8,128)(2,1)S(1)}, u32[]{:S(2)}, u32[]{:S(2)}) collective-permute-start(bf16[2,144,896]{2,1,0:T(8,128)(2,1)S(1)} %pad_maximum_fusion.2), channel_id=1, source_target_pairs={{0,2},{1,17},{2,0},{3,19},{4,6},{5,21},{6,4},{7,23},{8,10},{9,25},... | collective-permute-start | bytes 1548296 | tf_op jit(solution)/shard_map/ppermute | solution.py:276
  35.8 18.6 %collective-permute-start.5 = (bf16[2,144,896]{2,1,0:T(8,128)(2,1)S(1)}, bf16[2,144,896]{2,1,0:T(8,128)(2,1)S(1)}, u32[]{:S(2)}, u32[]{:S(2)}) collective-permute-start(bf16[2,144,896]{2,1,0:T(8,128)(2,1)S(1)} %pad_maximum_fusion.3), channel_id=1, source_target_pairs={{0,2},{1,17},{2,0},{3,19},{4,6},{5,21},{6,4},{7,23},{8,10},{9,25},... | collective-permute-start | bytes 1548296 | tf_op jit(solution)/shard_map/ppermute | solution.py:276
  38.6 3.2 %collective-permute-start.7 = (bf16[72,640]{1,0:T(8,128)(2,1)S(1)}, bf16[72,640]{1,0:T(8,128)(2,1)S(1)}, u32[]{:S(2)}, u32[]{:S(2)}) collective-permute-start(bf16[72,640]{1,0:T(8,128)(2,1)S(1)} %fusion.1), channel_id=1, source_target_pairs={{0,0},{1,5},{2,2},{3,7},{4,4},{5,1},{6,6},{7,3},{8,8},{9,13},{10,1... | collective-permute-start | bytes 276488 | tf_op jit(solution)/shard_map/ppermute | solution.py:276
  39.3 14.9 %collective-permute-start.8 = (bf16[72,640]{1,0:T(8,128)(2,1)S(1)}, bf16[72,640]{1,0:T(8,128)(2,1)S(1)}, u32[]{:S(2)}, u32[]{:S(2)}) collective-permute-start(bf16[72,640]{1,0:T(8,128)(2,1)S(1)} %fusion.1), channel_id=1, source_target_pairs={{0,8},{1,13},{2,10},{3,15},{4,12},{5,9},{6,14},{7,11},{8,0},{9,5},... | collective-permute-start | bytes 276488 | tf_op jit(solution)/shard_map/ppermute | solution.py:276
  54.3 3.5 %collective-permute-start.11 = (bf16[4,144,896]{2,1,0:T(8,128)(2,1)S(1)}, bf16[4,144,896]{2,1,0:T(8,128)(2,1)}, u32[]{:S(2)}, u32[]{:S(2)}) collective-permute-start(bf16[4,144,896]{2,1,0:T(8,128)(2,1)S(1)} %constant_dynamic-update-slice_fusion.refs_0_), channel_id=1, source_target_pairs={{0,1},{1,0},{2,3},{3,2},{4,5},{5,4},{6,7},{7,6},{8,9},{9,8},{10,11... | collective-permute-start | bytes 3096584 | tf_op jit(solution)/shard_map/ppermute | solution.py:276
  54.6 3.9 %collective-permute-start.12 = (bf16[4,144,896]{2,1,0:T(8,128)(2,1)S(1)}, bf16[4,144,896]{2,1,0:T(8,128)(2,1)S(1)}, u32[]{:S(2)}, u32[]{:S(2)}) collective-permute-start(bf16[4,144,896]{2,1,0:T(8,128)(2,1)S(1)} %pad_maximum_fusion.refs_2_), channel_id=1, source_target_pairs={{0,1},{1,0},{2,3},{3,2},{4,5},{5,4},{6,7},{7,6},{8,9},{9,8},{10,11... | collective-permute-start | bytes 3096584 | tf_op jit(solution)/shard_map/ppermute | solution.py:276
  55.1 12.7 %collective-permute-start.9 = (bf16[2,72,640]{2,1,0:T(8,128)(2,1)S(1)}, bf16[2,72,640]{2,1,0:T(8,128)(2,1)S(1)}, u32[]{:S(2)}, u32[]{:S(2)}) collective-permute-start(bf16[2,72,640]{2,1,0:T(8,128)(2,1)S(1)} %pad_maximum_fusion.5), channel_id=1, source_target_pairs={{0,16},{1,3},{2,18},{3,1},{4,20},{5,7},{6,22},{7,5},{8,24},{9,11},... | collective-permute-start | bytes 552968 | tf_op jit(solution)/shard_map/ppermute | solution.py:276
  67.9 7.6 %collective-permute-start.13 = (bf16[4,72,640]{2,1,0:T(8,128)(2,1)S(1)}, bf16[4,72,640]{2,1,0:T(8,128)(2,1)S(1)}, u32[]{:S(2)}, u32[]{:S(2)}) collective-permute-start(bf16[4,72,640]{2,1,0:T(8,128)(2,1)S(1)} %pad_maximum_fusion.4), channel_id=1, source_target_pairs={{0,2},{1,17},{2,0},{3,19},{4,6},{5,21},{6,4},{7,23},{8,10},{9,25},... | collective-permute-start | bytes 1105928 | tf_op jit(solution)/shard_map/ppermute | solution.py:276
  70.1 19.5 %all-to-all-start.1 = ((bf16[16,16,1152]{2,1,0:T(8,128)(2,1)}), bf16[16,16,1152]{2,1,0:T(8,128)(2,1)S(1)}, u32[]{:S(2)}, u32[]{:S(2)}) async-start(bf16[16,16,1152]{2,1,0:T(8,128)(2,1)} %bitcast.53), calls=%async_computation.1 | async-start | bytes 1179648 | tf_op jit(solution)/shard_map/all_to_all | solution.py:394
  74.0 3.9 %copy-start = (bf16[1,256,1152]{2,1,0:T(8,128)(2,1)S(1)}, bf16[1,256,1152]{2,1,0:T(8,128)(2,1)}, u32[]{:S(2)}) copy-start(bf16[1,256,1152]{2,1,0:T(8,128)(2,1)} %param.10) | copy-start | bytes 1769476
  75.6 2.3 %collective-permute-start.14 = (bf16[8,72,640]{2,1,0:T(8,128)(2,1)S(1)}, bf16[8,72,640]{2,1,0:T(8,128)(2,1)S(1)}, u32[]{:S(2)}, u32[]{:S(2)}) collective-permute-start(bf16[8,72,640]{2,1,0:T(8,128)(2,1)S(1)} %constant_dynamic-update-slice_fusion.2.refs_0_), channel_id=1, source_target_pairs={{0,1},{1,0},{2,3},{3,2},{4,5},{5,4},{6,7},{7,6},{8,9},{9,8},{10,11... | collective-permute-start | bytes 2211848 | tf_op jit(solution)/shard_map/ppermute | solution.py:276
  77.9 11.6 %copy-start.1 = (bf16[3,1,256,576]{2,3,1,0:T(8,128)(2,1)S(1)}, bf16[3,1,256,576]{2,3,1,0:T(8,128)(2,1)}, u32[]{:S(2)}) copy-start(bf16[3,1,256,576]{2,3,1,0:T(8,128)(2,1)} %param.7) | copy-start | bytes 2654212

commit v7 on v6

--- a/solution.py
+++ b/solution.py
@@ -70,7 +70,7 @@
     spread_t = dot_nt(keep(values, start, low, high), grad_o)
     wide = rounded_t.astype(jnp.float32)
     delta = jnp.sum(wide * spread_t, axis=0, keepdims=True)
-    dscore_t = (attention_t.astype(jnp.float32) * (spread_t - delta)).astype(jnp.bfloat16)
+    dscore_t = (wide * (spread_t - delta)).astype(jnp.bfloat16)
     return (
         dot_tn(dscore_t, keep(keys, start, low, high)),
         dot_nn(dscore_t, keep(query, start, low, high)),
@@ -108,7 +108,8 @@
     bias_ref[...] = jnp.where(lax.rem(row, patches) == lax.rem(column, patches), 0.0, -1e30)
     gain = gain_ref[...]
     widened = x_ref[:, :depth].astype(jnp.float32)
-    centered = widened - jnp.mean(widened, axis=-1, keepdims=True)
+    mean = jnp.mean(widened, axis=-1, keepdims=True)
+    centered = widened - mean
     inverse = lax.rsqrt(jnp.mean(centered * centered, axis=-1, keepdims=True) + epsilon)
     normed = (centered * inverse * gain).astype(jnp.bfloat16)
     for copy in copies:
@@ -133,7 +134,7 @@
     grad_ref[:, width : 2 * width] = gk_ref[...]
     scaled = dot_nt(grad_ref[...], held_ref[:, : 3 * width]) * gain
     widened = x_ref[:, :depth].astype(jnp.float32)
-    centered = widened - jnp.mean(widened, axis=-1, keepdims=True)
+    centered = widened - mean
     normal_form = centered * inverse
     branch = inverse * (
         scaled

time: 95.1 us -> 95.1 us (level)
  no operation moved by 1% of the time
where the time goes in v7:
time: 95.1 us; the launch traced here: 94.7 us
  waiting for transfers between devices  37.6 us (40%)
  starting transfers between devices  37.4 us (39%)
  Pallas kernels  15.7 us (17%)
  local copies, waits for them, and re-layouts  1.61 us (2%)
  other arithmetic  1.57 us (2%)
    ppermute x15, waiting for transfers between devices, moved(): return lax.ppermute(block, ('clip', 'seq'), pairs)  27.1 us
    ppermute x15, starting transfers between devices, moved(): return lax.ppermute(block, ('clip', 'seq'), pairs)  22.3 us
    all_to_all x1, starting transfers between devices, shards(): lax.all_to_all(mixed, 'seq', split_axis=0, concat_axis=0, tiled=True)  11.2 us
    all_to_all x1, waiting for transfers between devices, shards(): lax.all_to_all(branch.reshape(frames, patches, depth), 'seq', split_axis=...  10.5 us
    pallas_call x1, Pallas kernels, temporal(): pl.pallas_call(functools.partial(temporal_kernel, patches, len(pieces)),...  9.31 us
    pallas_call x1, Pallas kernels, spatial(): pl.pallas_call(spatial_kernel, out_shape=(jax.ShapeDtypeStruct((tokens, d...  5.22 us
    all_to_all x1, starting transfers between devices, shards(): lax.all_to_all(branch.reshape(frames, patches, depth), 'seq', split_axis=...  3.91 us
  transfers between devices with their start and end apart: 17, of which 8 were waited for; matrix products, arithmetic and copies ran while one was open for 3% of the time, Pallas kernels for 11%

profile of v7, /device:TPU:0, one launch (start us, length us, event | category | flops | bytes accessed | tf_op | source)
XLA Modules:
  0.0 94.7 jit_solution(17903451499564194066)
XLA Ops:
  1.2 1.2 %copy.9 = bf16[1,256,576]{2,1,0:T(8,128)(2,1)S(1)} copy(bf16[1,256,576]{1,2,0:T(8,128)(2,1)} %param.9) | data formatting | bytes 589824 | tf_op args[2]
  2.3 1.0 %pad_maximum_fusion.1 = bf16[1,256,1728]{2,1,0:T(8,128)(2,1)} fusion(bf16[1,256,576]{2,1,0:T(8,128)(2,1)S(1)} %copy.9, bf16[1,256,1152]{2,1,0:T(8,128)(2,1)S(1)} %copy-done.2), kind=kLoop, calls=%fused_computation.1 | loop fusion | flops 1769472 | bytes 1769472 | tf_op jit(solution)/shard_map/concatenate | solution.py:361
  3.5 0.7 collective-permute-start.1
  4.2 2.7 %collective-permute-start.2 = (bf16[1,144,896]{2,1,0:T(8,128)(2,1)S(1)}, bf16[1,144,896]{2,1,0:T(8,128)(2,1)S(1)}, u32[]{:S(2)}, u32[]{:S(2)}) collective-permute-start(bf16[1,144,896]{2,1,0:T(8,128)(2,1)S(1)} %bitcast.69), channel_id=1, source_target_pairs={{0,16},{1,3},{2,18},{3,1},{4,20},{5,7},{6,22},{7,5},{8,24},{9,11},... | collective-permute-start | bytes 774152 | tf_op jit(solution)/shard_map/ppermute | solution.py:277
  6.9 2.6 %collective-permute-start.3 = (bf16[144,896]{1,0:T(8,128)(2,1)S(1)}, bf16[144,896]{1,0:T(8,128)(2,1)S(1)}, u32[]{:S(2)}, u32[]{:S(2)}) collective-permute-start(bf16[144,896]{1,0:T(8,128)(2,1)S(1)} %fusion), channel_id=1, source_target_pairs={{0,8},{1,13},{2,10},{3,15},{4,12},{5,9},{6,14},{7,11},{8,0},{9,5},... | collective-permute-start | bytes 774152 | tf_op jit(solution)/shard_map/ppermute | solution.py:277
  9.7 1.5 %collective-permute-done.2 = bf16[1,144,896]{2,1,0:T(8,128)(2,1)S(1)} collective-permute-done((bf16[1,144,896]{2,1,0:T(8,128)(2,1)S(1)}, bf16[1,144,896]{2,1,0:T(8,128)(2,1)S(1)}, u32[]{:S(2)}, u32[]{:S(2)}) %collective-permute-start.2) | collective-permute-done | bytes 258080 | tf_op jit(solution)/shard_map/ppermute | solution.py:277
  11.3 4.7 %collective-permute-done.3 = bf16[144,896]{1,0:T(8,128)(2,1)S(1)} collective-permute-done((bf16[144,896]{1,0:T(8,128)(2,1)S(1)}, bf16[144,896]{1,0:T(8,128)(2,1)S(1)}, u32[]{:S(2)}, u32[]{:S(2)}) %collective-permute-start.3) | collective-permute-done | bytes 258080 | tf_op jit(solution)/shard_map/ppermute | solution.py:277
  16.0 11.2 %all-to-all-start = ((bf16[16,16,1728]{2,1,0:T(8,128)(2,1)}), bf16[16,16,1728]{2,1,0:T(8,128)(2,1)S(1)}, u32[]{:S(2)}, u32[]{:S(2)}) async-start(bf16[16,16,1728]{2,1,0:T(8,128)(2,1)} %bitcast.2), calls=%async_computation | async-start | bytes 1835008 | tf_op jit(solution)/shard_map/all_to_all | solution.py:375
  27.6 2.1 %collective-permute-start.4 = (bf16[1,144,896]{2,1,0:T(8,128)(2,1)S(1)}, bf16[1,144,896]{2,1,0:T(8,128)(2,1)S(1)}, u32[]{:S(2)}, u32[]{:S(2)}) collective-permute-start(bf16[1,144,896]{2,1,0:T(8,128)(2,1)S(1)} %bitcast.66), channel_id=1, source_target_pairs={{0,16},{1,3},{2,18},{3,1},{4,20},{5,7},{6,22},{7,5},{8,24},{9,11},... | collective-permute-start | bytes 774152 | tf_op jit(solution)/shard_map/ppermute | solution.py:277
  29.8 1.7 %collective-permute-start.10 = (bf16[2,144,896]{2,1,0:T(8,128)(2,1)S(1)}, bf16[2,144,896]{2,1,0:T(8,128)(2,1)S(1)}, u32[]{:S(2)}, u32[]{:S(2)}) collective-permute-start(bf16[2,144,896]{2,1,0:T(8,128)(2,1)S(1)} %pad_maximum_fusion.2), channel_id=1, source_target_pairs={{0,2},{1,17},{2,0},{3,19},{4,6},{5,21},{6,4},{7,23},{8,10},{9,25},... | collective-permute-start | bytes 1548296 | tf_op jit(solution)/shard_map/ppermute | solution.py:277
  31.5 4.3 %collective-permute-done.4 = bf16[1,144,896]{2,1,0:T(8,128)(2,1)S(1)} collective-permute-done((bf16[1,144,896]{2,1,0:T(8,128)(2,1)S(1)}, bf16[1,144,896]{2,1,0:T(8,128)(2,1)S(1)}, u32[]{:S(2)}, u32[]{:S(2)}) %collective-permute-start.4) | collective-permute-done | bytes 258080 | tf_op jit(solution)/shard_map/ppermute | solution.py:277
  35.8 2.8 %collective-permute-start.5 = (bf16[2,144,896]{2,1,0:T(8,128)(2,1)S(1)}, bf16[2,144,896]{2,1,0:T(8,128)(2,1)S(1)}, u32[]{:S(2)}, u32[]{:S(2)}) collective-permute-start(bf16[2,144,896]{2,1,0:T(8,128)(2,1)S(1)} %pad_maximum_fusion.3), channel_id=1, source_target_pairs={{0,2},{1,17},{2,0},{3,19},{4,6},{5,21},{6,4},{7,23},{8,10},{9,25},... | collective-permute-start | bytes 1548296 | tf_op jit(solution)/shard_map/ppermute | solution.py:277
  38.6 0.7 collective-permute-start.7
  39.3 2.4 %collective-permute-start.8 = (bf16[72,640]{1,0:T(8,128)(2,1)S(1)}, bf16[72,640]{1,0:T(8,128)(2,1)S(1)}, u32[]{:S(2)}, u32[]{:S(2)}) collective-permute-start(bf16[72,640]{1,0:T(8,128)(2,1)S(1)} %fusion.1), channel_id=1, source_target_pairs={{0,8},{1,13},{2,10},{3,15},{4,12},{5,9},{6,14},{7,11},{8,0},{9,5},... | collective-permute-start | bytes 276488 | tf_op jit(solution)/shard_map/ppermute | solution.py:277
  41.8 12.4 %collective-permute-done.8 = bf16[72,640]{1,0:T(8,128)(2,1)S(1)} collective-permute-done((bf16[72,640]{1,0:T(8,128)(2,1)S(1)}, bf16[72,640]{1,0:T(8,128)(2,1)S(1)}, u32[]{:S(2)}, u32[]{:S(2)}) %collective-permute-start.8) | collective-permute-done | bytes 92192 | tf_op jit(solution)/shard_map/ppermute | solution.py:277
  55.1 2.8 %collective-permute-start.9 = (bf16[2,72,640]{2,1,0:T(8,128)(2,1)S(1)}, bf16[2,72,640]{2,1,0:T(8,128)(2,1)S(1)}, u32[]{:S(2)}, u32[]{:S(2)}) collective-permute-start(bf16[2,72,640]{2,1,0:T(8,128)(2,1)S(1)} %pad_maximum_fusion.5), channel_id=1, source_target_pairs={{0,16},{1,3},{2,18},{3,1},{4,20},{5,7},{6,22},{7,5},{8,24},{9,11},... | collective-permute-start | bytes 552968 | tf_op jit(solution)/shard_map/ppermute | solution.py:277
  58.5 9.3 %temporal_backward.1 = bf16[256,1152]{1,0:T(8,128)(2,1)} custom-call(s32[32]{0:T(128)S(1)} %stack.189.place_ref, bf16[256,1728]{1,0:T(8,128)(2,1)S(1)} %bitcast.62, f32[1,1152]{1,0:T(1,128)S(1)} %add.133.gain_ref, bf16[4,144,896]{2,1,0:T(8,128)(2,1)S(1)} %constant_dynamic-update-slice_fusion.refs_0_, bf16[4,144,896]{2,1,0:T(8,128)(2,1)} %collective-permute-done.11.refs_1_, ...), custom_call_target="tpu_custom_call" | custom-call | flops 3649044480 | bytes 5750784 | tf_op jit(solution)/shard_map/temporal_backward/pallas_call | solution.py:151
  67.9 2.2 %collective-permute-start.13 = (bf16[4,72,640]{2,1,0:T(8,128)(2,1)S(1)}, bf16[4,72,640]{2,1,0:T(8,128)(2,1)S(1)}, u32[]{:S(2)}, u32[]{:S(2)}) collective-permute-start(bf16[4,72,640]{2,1,0:T(8,128)(2,1)S(1)} %pad_maximum_fusion.4), channel_id=1, source_target_pairs={{0,2},{1,17},{2,0},{3,19},{4,6},{5,21},{6,4},{7,23},{8,10},{9,25},... | collective-permute-start | bytes 1105928 | tf_op jit(solution)/shard_map/ppermute | solution.py:277
  70.0 3.9 %all-to-all-start.1 = ((bf16[16,16,1152]{2,1,0:T(8,128)(2,1)}), bf16[16,16,1152]{2,1,0:T(8,128)(2,1)S(1)}, u32[]{:S(2)}, u32[]{:S(2)}) async-start(bf16[16,16,1152]{2,1,0:T(8,128)(2,1)} %bitcast.53), calls=%async_computation.1 | async-start | bytes 1179648 | tf_op jit(solution)/shard_map/all_to_all | solution.py:395
  74.0 1.5 %collective-permute-done.13 = bf16[4,72,640]{2,1,0:T(8,128)(2,1)S(1)} collective-permute-done((bf16[4,72,640]{2,1,0:T(8,128)(2,1)S(1)}, bf16[4,72,640]{2,1,0:T(8,128)(2,1)S(1)}, u32[]{:S(2)}, u32[]{:S(2)}) %collective-permute-start.13) | collective-permute-done | bytes 368672 | tf_op jit(solution)/shard_map/ppermute | solution.py:277
  75.8 2.1 %collective-permute-done.14.refs_1_ = bf16[8,72,640]{2,1,0:T(8,128)(2,1)S(1)} collective-permute-done((bf16[8,72,640]{2,1,0:T(8,128)(2,1)S(1)}, bf16[8,72,640]{2,1,0:T(8,128)(2,1)S(1)}, u32[]{:S(2)}, u32[]{:S(2)}) %collective-permute-start.14) | collective-permute-done | bytes 737312 | tf_op jit(solution)/shard_map/ppermute | solution.py:277
  77.9 1.1 %spatial_prepare.1 = (bf16[192,1152]{1,0:T(8,128)(2,1)S(1)}, bf16[192,1152]{1,0:T(8,128)(2,1)S(1)}, bf16[192,1152]{1,0:T(8,128)(2,1)S(1)}, bf16[256,1152]{1,0:T(8,128)(2,1)S(1)}) custom-call(s32[32]{0:T(128)S(1)} %stack.212.place_ref, bf16[256,1152]{1,0:T(8,128)(2,1)S(1)} %bitcast.63, bf16[8,72,640]{2,1,0:T(8,128)(2,1)S(1)} %constant_dynamic-update-slice_fusion.2.refs_0_, ...), custom_call_target="tpu_custom_call" | custom-call | bytes 3833856 | tf_op jit(solution)/shard_map/spatial_prepare/pallas_call | solution.py:207
  79.0 10.5 %all-to-all-done.1 = bf16[16,16,1152]{2,1,0:T(8,128)(2,1)S(1)} async-done(((bf16[16,16,1152]{2,1,0:T(8,128)(2,1)}), bf16[16,16,1152]{2,1,0:T(8,128)(2,1)S(1)}, u32[]{:S(2)}, u32[]{:S(2)}) %all-to-all-start.1) | async-done | bytes 589856 | tf_op jit(solution)/shard_map/all_to_all | solution.py:395
  89.5 5.2 %spatial_backward.1 = (bf16[256,1152]{1,0:T(8,128)(2,1)}, bf16[3,8,72,256]{3,2,1,0:T(8,128)(2,1)}) custom-call(bf16[3,8,72,256]{3,2,1,0:T(8,128)(2,1)S(1)} %bitcast.65, bf16[256,1152]{1,0:T(8,128)(2,1)S(1)} %get-tuple-element.37.stream_ref, bf16[256,1152]{1,0:T(8,128)(2,1)S(1)} %bitcast.64, bf16[192,1152]{1,0:T(8,128)(2,1)S(1)} %get-tuple-element.39.refs_0_, ...), custom_call_target="tpu_custom_call" | custom-call | flops 1681915904 | bytes 4866048 | tf_op jit(solution)/shard_map/spatial_backward/pallas_call | solution.py:255
  (45 shorter events, 3.5 us)
Async XLA Ops:
  0.6 1.7 %copy-start.2 = (bf16[1,256,1152]{2,1,0:T(8,128)(2,1)S(1)}, bf16[1,256,1152]{2,1,0:T(8,128)(2,1)}, u32[]{:S(2)}) copy-start(bf16[1,256,1152]{2,1,0:T(8,128)(2,1)} %param.8) | copy-start | bytes 1769476
  0.6 2.7 %collective-permute-start = (bf16[72,1728]{1,0:T(8,128)(2,1)}, bf16[72,1728]{1,0:T(8,128)(2,1)S(1)}, u32[]{:S(2)}, u32[]{:S(2)}) collective-permute-start(bf16[72,1728]{1,0:T(8,128)(2,1)} %param.12), channel_id=1, source_target_pairs={{0,1},{1,0},{2,3},{3,2},{4,5},{5,4},{6,7},{7,6},{8,9},{9,8},{10,11... | collective-permute-start | bytes 746504 | tf_op jit(solution)/shard_map/ppermute | solution.py:277
  2.3 1.0 %copy-start.3 = (bf16[72,1728]{1,0:T(8,128)(2,1)S(1)}, bf16[72,1728]{1,0:T(8,128)(2,1)}, u32[]{:S(2)}) copy-start(bf16[72,1728]{1,0:T(8,128)(2,1)} %param.12) | copy-start | bytes 746500
  3.4 6.1 %copy-start.5 = (f32[1152]{0:T(1024)S(1)}, f32[1152]{0:T(1024)}, u32[]{:S(2)}) copy-start(f32[1152]{0:T(1024)} %param.11) | copy-start | bytes 13828
  3.5 0.7 collective-permute-start.1
  4.2 7.0 %collective-permute-start.2 = (bf16[1,144,896]{2,1,0:T(8,128)(2,1)S(1)}, bf16[1,144,896]{2,1,0:T(8,128)(2,1)S(1)}, u32[]{:S(2)}, u32[]{:S(2)}) collective-permute-start(bf16[1,144,896]{2,1,0:T(8,128)(2,1)S(1)} %bitcast.69), channel_id=1, source_target_pairs={{0,16},{1,3},{2,18},{3,1},{4,20},{5,7},{6,22},{7,5},{8,24},{9,11},... | collective-permute-start | bytes 774152 | tf_op jit(solution)/shard_map/ppermute | solution.py:277
  6.9 9.1 %collective-permute-start.3 = (bf16[144,896]{1,0:T(8,128)(2,1)S(1)}, bf16[144,896]{1,0:T(8,128)(2,1)S(1)}, u32[]{:S(2)}, u32[]{:S(2)}) collective-permute-start(bf16[144,896]{1,0:T(8,128)(2,1)S(1)} %fusion), channel_id=1, source_target_pairs={{0,8},{1,13},{2,10},{3,15},{4,12},{5,9},{6,14},{7,11},{8,0},{9,5},... | collective-permute-start | bytes 774152 | tf_op jit(solution)/shard_map/ppermute | solution.py:277
  11.3 15.9 %copy-start.4 = (bf16[36,1152]{1,0:T(8,128)(2,1)S(1)}, bf16[36,1152]{1,0:T(8,128)(2,1)}, u32[]{:S(2)}) copy-start(bf16[36,1152]{1,0:T(8,128)(2,1)} %param.13) | copy-start | bytes 248836
  16.0 38.6 %all-to-all-start = ((bf16[16,16,1728]{2,1,0:T(8,128)(2,1)}), bf16[16,16,1728]{2,1,0:T(8,128)(2,1)S(1)}, u32[]{:S(2)}, u32[]{:S(2)}) async-start(bf16[16,16,1728]{2,1,0:T(8,128)(2,1)} %bitcast.2), calls=%async_computation | async-start | bytes 1835008 | tf_op jit(solution)/shard_map/all_to_all | solution.py:375
  27.2 4.3 %collective-permute-start.6 = (bf16[36,1152]{1,0:T(8,128)(2,1)S(1)}, bf16[36,1152]{1,0:T(8,128)(2,1)S(1)}, u32[]{:S(2)}, u32[]{:S(2)}) collective-permute-start(bf16[36,1152]{1,0:T(8,128)(2,1)S(1)} %copy-done.4), channel_id=1, source_target_pairs={{0,1},{1,0},{2,3},{3,2},{4,5},{5,4},{6,7},{7,6},{8,9},{9,8},{10,11... | collective-permute-start | bytes 248840 | tf_op jit(solution)/shard_map/ppermute | solution.py:277
  27.6 8.1 %collective-permute-start.4 = (bf16[1,144,896]{2,1,0:T(8,128)(2,1)S(1)}, bf16[1,144,896]{2,1,0:T(8,128)(2,1)S(1)}, u32[]{:S(2)}, u32[]{:S(2)}) collective-permute-start(bf16[1,144,896]{2,1,0:T(8,128)(2,1)S(1)} %bitcast.66), channel_id=1, source_target_pairs={{0,16},{1,3},{2,18},{3,1},{4,20},{5,7},{6,22},{7,5},{8,24},{9,11},... | collective-permute-start | bytes 774152 | tf_op jit(solution)/shard_map/ppermute | solution.py:277
  29.8 24.5 %collective-permute-start.10 = (bf16[2,144,896]{2,1,0:T(8,128)(2,1)S(1)}, bf16[2,144,896]{2,1,0:T(8,128)(2,1)S(1)}, u32[]{:S(2)}, u32[]{:S(2)}) collective-permute-start(bf16[2,144,896]{2,1,0:T(8,128)(2,1)S(1)} %pad_maximum_fusion.2), channel_id=1, source_target_pairs={{0,2},{1,17},{2,0},{3,19},{4,6},{5,21},{6,4},{7,23},{8,10},{9,25},... | collective-permute-start | bytes 1548296 | tf_op jit(solution)/shard_map/ppermute | solution.py:277
  35.8 18.6 %collective-permute-start.5 = (bf16[2,144,896]{2,1,0:T(8,128)(2,1)S(1)}, bf16[2,144,896]{2,1,0:T(8,128)(2,1)S(1)}, u32[]{:S(2)}, u32[]{:S(2)}) collective-permute-start(bf16[2,144,896]{2,1,0:T(8,128)(2,1)S(1)} %pad_maximum_fusion.3), channel_id=1, source_target_pairs={{0,2},{1,17},{2,0},{3,19},{4,6},{5,21},{6,4},{7,23},{8,10},{9,25},... | collective-permute-start | bytes 1548296 | tf_op jit(solution)/shard_map/ppermute | solution.py:277
  38.6 3.2 %collective-permute-start.7 = (bf16[72,640]{1,0:T(8,128)(2,1)S(1)}, bf16[72,640]{1,0:T(8,128)(2,1)S(1)}, u32[]{:S(2)}, u32[]{:S(2)}) collective-permute-start(bf16[72,640]{1,0:T(8,128)(2,1)S(1)} %fusion.1), channel_id=1, source_target_pairs={{0,0},{1,5},{2,2},{3,7},{4,4},{5,1},{6,6},{7,3},{8,8},{9,13},{10,1... | collective-permute-start | bytes 276488 | tf_op jit(solution)/shard_map/ppermute | solution.py:277
  39.3 14.9 %collective-permute-start.8 = (bf16[72,640]{1,0:T(8,128)(2,1)S(1)}, bf16[72,640]{1,0:T(8,128)(2,1)S(1)}, u32[]{:S(2)}, u32[]{:S(2)}) collective-permute-start(bf16[72,640]{1,0:T(8,128)(2,1)S(1)} %fusion.1), channel_id=1, source_target_pairs={{0,8},{1,13},{2,10},{3,15},{4,12},{5,9},{6,14},{7,11},{8,0},{9,5},... | collective-permute-start | bytes 276488 | tf_op jit(solution)/shard_map/ppermute | solution.py:277
  54.3 3.5 %collective-permute-start.11 = (bf16[4,144,896]{2,1,0:T(8,128)(2,1)S(1)}, bf16[4,144,896]{2,1,0:T(8,128)(2,1)}, u32[]{:S(2)}, u32[]{:S(2)}) collective-permute-start(bf16[4,144,896]{2,1,0:T(8,128)(2,1)S(1)} %constant_dynamic-update-slice_fusion.refs_0_), channel_id=1, source_target_pairs={{0,1},{1,0},{2,3},{3,2},{4,5},{5,4},{6,7},{7,6},{8,9},{9,8},{10,11... | collective-permute-start | bytes 3096584 | tf_op jit(solution)/shard_map/ppermute | solution.py:277
  54.6 3.9 %collective-permute-start.12 = (bf16[4,144,896]{2,1,0:T(8,128)(2,1)S(1)}, bf16[4,144,896]{2,1,0:T(8,128)(2,1)S(1)}, u32[]{:S(2)}, u32[]{:S(2)}) collective-permute-start(bf16[4,144,896]{2,1,0:T(8,128)(2,1)S(1)} %pad_maximum_fusion.refs_2_), channel_id=1, source_target_pairs={{0,1},{1,0},{2,3},{3,2},{4,5},{5,4},{6,7},{7,6},{8,9},{9,8},{10,11... | collective-permute-start | bytes 3096584 | tf_op jit(solution)/shard_map/ppermute | solution.py:277
  55.1 12.7 %collective-permute-start.9 = (bf16[2,72,640]{2,1,0:T(8,128)(2,1)S(1)}, bf16[2,72,640]{2,1,0:T(8,128)(2,1)S(1)}, u32[]{:S(2)}, u32[]{:S(2)}) collective-permute-start(bf16[2,72,640]{2,1,0:T(8,128)(2,1)S(1)} %pad_maximum_fusion.5), channel_id=1, source_target_pairs={{0,16},{1,3},{2,18},{3,1},{4,20},{5,7},{6,22},{7,5},{8,24},{9,11},... | collective-permute-start | bytes 552968 | tf_op jit(solution)/shard_map/ppermute | solution.py:277
  67.9 7.6 %collective-permute-start.13 = (bf16[4,72,640]{2,1,0:T(8,128)(2,1)S(1)}, bf16[4,72,640]{2,1,0:T(8,128)(2,1)S(1)}, u32[]{:S(2)}, u32[]{:S(2)}) collective-permute-start(bf16[4,72,640]{2,1,0:T(8,128)(2,1)S(1)} %pad_maximum_fusion.4), channel_id=1, source_target_pairs={{0,2},{1,17},{2,0},{3,19},{4,6},{5,21},{6,4},{7,23},{8,10},{9,25},... | collective-permute-start | bytes 1105928 | tf_op jit(solution)/shard_map/ppermute | solution.py:277
  70.0 19.5 %all-to-all-start.1 = ((bf16[16,16,1152]{2,1,0:T(8,128)(2,1)}), bf16[16,16,1152]{2,1,0:T(8,128)(2,1)S(1)}, u32[]{:S(2)}, u32[]{:S(2)}) async-start(bf16[16,16,1152]{2,1,0:T(8,128)(2,1)} %bitcast.53), calls=%async_computation.1 | async-start | bytes 1179648 | tf_op jit(solution)/shard_map/all_to_all | solution.py:395
  74.0 3.9 %copy-start = (bf16[1,256,1152]{2,1,0:T(8,128)(2,1)S(1)}, bf16[1,256,1152]{2,1,0:T(8,128)(2,1)}, u32[]{:S(2)}) copy-start(bf16[1,256,1152]{2,1,0:T(8,128)(2,1)} %param.10) | copy-start | bytes 1769476
  75.6 2.3 %collective-permute-start.14 = (bf16[8,72,640]{2,1,0:T(8,128)(2,1)S(1)}, bf16[8,72,640]{2,1,0:T(8,128)(2,1)S(1)}, u32[]{:S(2)}, u32[]{:S(2)}) collective-permute-start(bf16[8,72,640]{2,1,0:T(8,128)(2,1)S(1)} %constant_dynamic-update-slice_fusion.2.refs_0_), channel_id=1, source_target_pairs={{0,1},{1,0},{2,3},{3,2},{4,5},{5,4},{6,7},{7,6},{8,9},{9,8},{10,11... | collective-permute-start | bytes 2211848 | tf_op jit(solution)/shard_map/ppermute | solution.py:277
  77.9 11.6 %copy-start.1 = (bf16[3,1,256,576]{2,3,1,0:T(8,128)(2,1)S(1)}, bf16[3,1,256,576]{2,3,1,0:T(8,128)(2,1)}, u32[]{:S(2)}) copy-start(bf16[3,1,256,576]{2,3,1,0:T(8,128)(2,1)} %param.7) | copy-start | bytes 2654212
